TPU v7x, 32 devices: a whole 2x2x4 slice. The times are simulated.
32 devices in a mesh: beh: 4 (over y, x), node: 8 (over z, core).
Axes of the slice: x: 2, y: 2, z: 4, core: 2. Of those that a mesh axis runs over, the one named last changes fastest.
Arguments:
- embeddings: bfloat16 [16384, 128], P('node'), may hold values from -16 to 16, as said below
- adjacency: bfloat16 [4, 896, 128, 128], P('beh', 'node'), may hold values from -0.1875 to 0.1875
- tile_rows: int32 [4, 896], P('beh', 'node'), may hold values from 0 to 15
- tile_cols: int32 [4, 896], P('beh', 'node'), may hold values from 0 to 3
- tile_count: int32 [4, 8], P('beh', 'node'), may hold values from 28 to 112, as said below
- need_ids: int32 [4, 32], P('beh', 'node'), may hold values from 0 to 127, as said below
- w_query: bfloat16 [128, 128], replicated, may hold values from -0.5 to 0.5
- w_key: bfloat16 [128, 128], replicated, may hold values from -0.5 to 0.5
- w_value: bfloat16 [128, 128], replicated, may hold values from -0.5 to 0.5
- w_out: bfloat16 [128, 128], replicated, may hold values from -0.5 to 0.5
- mlp_gain: float32 [128], replicated, may hold values from 0.1 to 1.9
- w_up: bfloat16 [128, 512], replicated, may hold values from -0.5 to 0.5
- w_down: bfloat16 [512, 128], replicated, may hold values from -0.25 to 0.25
Outputs:
- merged: bfloat16 [4, 16384, 128], P('beh', 'node')
Inputs may be any that keep to these rules, and one draw needn't show every extreme that they name: `tile_count`: live slots of one behavior and shard; every behavior has a shard with all 112 slots live. `need_ids`: for each behavior b and shard n, entry n * 4 + m (m < 4) names a block owned by shard 2 m or shard 2 m + 1, block g being owned by shard g // 16. `embeddings`: entries keep within the stated bound.
All inputs are finite; a program needn't handle non-finite values.
Results may differ from a plain program's by a relative error of at most 0.0077.
Values may be sent and summed in bfloat16 or wider, within the bound.
No kernel may reach another device: no remote copies, remote signals or barrier semaphores. Data moves between devices by JAX's collectives and lax.ppermute only.
A program may use at most 64 MiB of HBM per device.

v0:
```python
import math

import jax
import jax.numpy as jnp
from jax import lax
from jax.sharding import PartitionSpec as P

TB = 128
HEADS = 4
HEAD = 32


def partner(value, axis, stride):
    mask = 2**stride
    pairs = [(source, source ^ mask) for source in range(lax.axis_size(axis))]
    return lax.ppermute(value, axis, pairs)


def merge_behaviors(behaviors, queries, w_query, w_key, w_value, w_out, mlp_gain, w_up, w_down):
    count_k, row_count, feature = behaviors.shape
    count_q = queries.shape[0]
    flat_keys = behaviors.reshape(count_k * row_count, feature)
    key_rows = jnp.dot(flat_keys, w_key, preferred_element_type=jnp.float32).reshape(
        count_k, row_count, HEADS, HEAD
    )
    value_rows = jnp.dot(flat_keys, w_value, preferred_element_type=jnp.float32).reshape(
        count_k, row_count, HEADS, HEAD
    )
    flat_queries = queries.reshape(count_q * row_count, feature)
    query_rows = jnp.dot(flat_queries, w_query, preferred_element_type=jnp.float32).reshape(
        count_q, row_count, HEADS, HEAD
    )
    scores = jnp.einsum(
        "qrhe,krhe->qrhk", query_rows, key_rows, precision=lax.Precision.HIGHEST
    ) / math.sqrt(HEAD)
    highest = jnp.max(scores, axis=-1, keepdims=True)
    weights = jnp.exp(scores - highest)
    weights = weights / jnp.sum(weights, axis=-1, keepdims=True)
    mixture = jnp.einsum("qrhk,krhe->qrhe", weights, value_rows, precision=lax.Precision.HIGHEST)
    mixture = mixture.reshape(count_q * row_count, feature).astype(jnp.bfloat16)
    residual = flat_queries.astype(jnp.float32) + jnp.dot(
        mixture, w_out, preferred_element_type=jnp.float32
    )
    meansq = jnp.mean(residual * residual, axis=-1, keepdims=True)
    normed = (residual * lax.rsqrt(meansq + 1e-06) * mlp_gain).astype(jnp.bfloat16)
    hidden = jax.nn.silu(jnp.dot(normed, w_up, preferred_element_type=jnp.float32)).astype(
        jnp.bfloat16
    )
    result = residual + jnp.dot(hidden, w_down, preferred_element_type=jnp.float32)
    return result.astype(jnp.bfloat16).reshape(count_q, row_count, feature)


def shards(
    embeddings,
    adjacency,
    tile_rows,
    tile_cols,
    tile_count,
    need_ids,
    w_query,
    w_key,
    w_value,
    w_out,
    mlp_gain,
    w_up,
    w_down,
):
    peer_count = lax.axis_size("node")
    node_rows, feature = embeddings.shape
    block_count = node_rows // TB
    needed = need_ids[0]
    owners = needed // block_count
    within = needed % block_count
    matches = owners[:, None] == jnp.arange(peer_count, dtype=jnp.int32)[None, :]
    request = jnp.sum(jnp.where(matches, within[:, None] + 1, 0), axis=0)
    peer_ids = jnp.arange(peer_count, dtype=jnp.int32)
    partner_ids = peer_ids + 1 - 2 * (peer_ids % 2)
    request_pair = jnp.stack([request, request[partner_ids]], axis=1)
    incoming = lax.all_to_all(request_pair, "node", split_axis=0, concat_axis=0, tiled=True)
    own_blocks = embeddings.reshape(block_count, TB, feature)
    parity = lax.axis_index("node") % 2
    partner_rows = partner(embeddings, "node", 0)
    other_blocks = partner_rows.reshape(block_count, TB, feature)
    own_code = jnp.where(incoming[:, 0] > 0, parity * block_count + incoming[:, 0], 0)
    other_code = jnp.where(incoming[:, 1] > 0, (1 - parity) * block_count + incoming[:, 1], 0)
    codes = own_code + other_code
    pair_stack = jnp.where(
        parity == 0,
        jnp.concatenate([own_blocks, other_blocks], axis=0),
        jnp.concatenate([other_blocks, own_blocks], axis=0),
    )
    half_rows = TB // 2
    halves = lax.dynamic_slice_in_dim(pair_stack, parity * half_rows, half_rows, 1)
    chooser = (codes[:, None] - 1 == jnp.arange(2 * block_count, dtype=jnp.int32)[None, :]).astype(
        jnp.bfloat16
    )
    outgoing = jnp.einsum(
        "pk,kid->pid", chooser, halves, preferred_element_type=jnp.float32
    ).astype(jnp.bfloat16)
    arrived = lax.all_to_all(outgoing, "node", split_axis=0, concat_axis=0, tiled=True)
    pairs = arrived.reshape(peer_count // 2, TB, feature)
    sources = pairs[owners[tile_cols[0]] // 2]
    product = jnp.einsum("tij,tjd->tid", adjacency[0], sources, preferred_element_type=jnp.float32)
    active = jnp.arange(adjacency.shape[1], dtype=jnp.int32) < tile_count[0, 0]
    select = (
        (tile_rows[0][:, None] == jnp.arange(block_count, dtype=jnp.int32)[None, :])
        & active[:, None]
    ).astype(jnp.float32)
    summed = jnp.einsum("tb,tid->bid", select, product, precision=lax.Precision.HIGHEST).reshape(
        node_rows, feature
    )
    spread = (summed + embeddings.astype(jnp.float32)).astype(jnp.bfloat16)
    everyone = lax.all_gather(spread[None], "beh", axis=0, tiled=True)
    index_now = lax.axis_index("beh")
    mine = lax.dynamic_slice_in_dim(everyone, index_now, 1, 0)
    return merge_behaviors(everyone, mine, w_query, w_key, w_value, w_out, mlp_gain, w_up, w_down)


def solution(mesh):
    in_specs = (
        P("node", None),
        P("beh", "node", None, None),
        P("beh", "node"),
        P("beh", "node"),
        P("beh", "node"),
        P("beh", "node"),
        P(),
        P(),
        P(),
        P(),
        P(),
        P(),
        P(),
    )
    out_specs = P("beh", "node", None)
    return jax.shard_map(shards, mesh=mesh, in_specs=in_specs, out_specs=out_specs, check_vma=False)
```

profile of v0, /device:TPU:0, one launch (start us, length us, event | category | flops | bytes accessed | tf_op | source)
XLA Modules:
  0.0 108.0 jit_solution(4433912679245027338)
XLA Ops:
  6.5 0.5 collective-permute-start
  7.0 0.7 and_select_fusion.3
  7.8 0.6 gather_fusion
  8.4 0.7 copy.43
  9.1 6.0 %all-to-all-start = ((s32[8,1,2]{2,1,0:T(1,128)}), s32[8,1,2]{2,1,0:T(1,128)S(1)}, u32[]{:S(2)}, u32[]{:S(2)}) async-start(s32[8,1,2]{2,1,0:T(1,128)} %copy.43), calls=%async_computation | async-start | bytes 8192 | tf_op jit(solution)/shard_map/all_to_all | solution.py:79
  15.1 0.7 fusion.46
  15.7 1.4 %copy.45 = bf16[16,128,128]{2,0,1:T(8,128)(2,1)S(1)} copy(bf16[16,128,128]{2,1,0:T(8,128)(2,1)} %bitcast.104) | data formatting | bytes 1048576 | tf_op jit(solution)/shard_map/reshape | solution.py:80
  17.1 3.4 %all-to-all-done = s32[8,1,2]{2,1,0:T(1,128)S(1)} async-done(((s32[8,1,2]{2,1,0:T(1,128)}), s32[8,1,2]{2,1,0:T(1,128)S(1)}, u32[]{:S(2)}, u32[]{:S(2)}) %all-to-all-start) | async-done | bytes 96 | tf_op jit(solution)/shard_map/all_to_all | solution.py:79
  20.7 0.3 copy.46
  21.3 0.7 copy.49
  22.0 3.4 %all-to-all-start.1 = ((bf16[8,64,128]{2,1,0:T(8,128)(2,1)}), bf16[8,64,128]{2,1,0:T(8,128)(2,1)S(1)}, u32[]{:S(2)}, u32[]{:S(2)}) async-start(bf16[8,64,128]{2,1,0:T(8,128)(2,1)} %copy.49), calls=%async_computation.1 | async-start | bytes 262144 | tf_op jit(solution)/shard_map/all_to_all | solution.py:100
  25.4 2.5 %fusion.42 = s32[112]{0:T(128)S(1)} fusion(s32[1,112]{1,0:T(1,128)S(1)} %copy-done.8, s32[]{:T(128)} %bitcast.17, s32[]{:T(128)} %bitcast.18, s32[]{:T(128)} %bitcast.20, s32[]{:T(128)} %bitcast.19), kind=kLoop, calls=%fused_computation.79 | loop fusion | flops 3024 | bytes 912 | tf_op jit(solution)/shard_map/select_n | solution.py:102
  28.6 3.5 %all-to-all-done.1 = bf16[8,64,128]{2,1,0:T(8,128)(2,1)S(1)} async-done(((bf16[8,64,128]{2,1,0:T(8,128)(2,1)}), bf16[8,64,128]{2,1,0:T(8,128)(2,1)S(1)}, u32[]{:S(2)}, u32[]{:S(2)}) %all-to-all-start.1) | async-done | bytes 131104 | tf_op jit(solution)/shard_map/all_to_all | solution.py:100
  32.0 3.0 %gather_fusion.1 = bf16[112,128,128]{2,1,0:T(8,128)(2,1)} fusion(bf16[4,128,128]{2,1,0:T(8,128)(2,1)S(1)} %bitcast.99, s32[1024]{0:T(1024)S(1)} %pad_clamp_fusion), kind=kCustom, calls=%fused_computation.1 | custom fusion | bytes 7340480 | tf_op jit(solution)/shard_map/gather | solution.py:102
  35.0 8.8 %fusion.3 = f32[112,128,128]{1,2,0:T(8,128)} fusion(bf16[112,128,128]{2,1,0:T(8,128)(2,1)} %gather_fusion.1, bf16[1,112,128,128]{3,2,1,0:T(8,128)(2,1)} %param.14), kind=kOutput, calls=%fused_computation.8 | convolution fusion | flops 469762048 | bytes 14680064 | tf_op jit(solution)/shard_map/tij,tjd->tid/dot_general | solution.py:103
  43.8 8.5 %copy.51 = f32[112,128,128]{2,0,1:T(8,128)} copy(f32[112,128,128]{1,2,0:T(8,128)} %fusion.3) | data formatting | bytes 14680064 | tf_op jit(solution)/shard_map/tij,tjd->tid/dot_general | solution.py:103
  52.3 4.7 %fusion.28 = f32[16,128,128]{2,0,1:T(8,128)S(1)} fusion(f32[112,128,128]{2,0,1:T(8,128)} %copy.51, s32[112]{0:T(128)S(1)} %bitcast.112, pred[112]{0:T(512)(128)(4,1)S(1)} %iota_compare_fusion.3), kind=kOutput, calls=%fused_computation.41 | convolution fusion | flops 352325120 | bytes 8389168 | tf_op jit(solution)/shard_map/tb,tid->bid/dot_general | solution.py:109
  57.4 0.9 fusion.10
  58.7 34.1 %all-gather.3.cloned.1.call-done = bf16[8192,128]{1,0:T(8,128)(2,1)} async-done(((bf16[2048,128]{1,0:T(8,128)(2,1)}), bf16[8192,128]{1,0:T(8,128)(2,1)}) %all-gather.3.cloned.1.call-update) | async-done | bytes 2097168 | tf_op jit(solution)/shard_map/all_gather | solution.py:113
  92.8 1.3 %fusion.16 = f32[2048,4,32]{0,2,1:T(8,128)S(1)} fusion(bf16[4,32,128]{2,1,0:T(8,128)(2,1)S(1)} %bitcast.108, bf16[4,2048,128]{2,1,0:T(8,128)(2,1)} %bitcast.100, s32[]{:T(128)S(6)} %select_n.122), kind=kOutput, calls=%fused_computation.27 | convolution fusion | flops 67108864 | bytes 1605636 | tf_op jit(solution)/shard_map/dot_general | solution.py:30
  94.2 2.6 %multiply_reduce_fusion.1 = f32[2048,4,4]{0,1,2:T(4,128)S(1)} fusion(bf16[4,2048,128,1]{2,1,3,0:T(8,128)(2,1)} %bitcast.101, bf16[4,32,128,1]{2,1,0,3:T(8,128)(2,1)S(1)} %bitcast.107, f32[2048,4,32]{0,2,1:T(8,128)S(1)} %fusion.16), kind=kOutput, calls=%fused_computation.4 | convolution fusion | flops 270499840 | bytes 3309568 | tf_op jit(solution)/shard_map/dot_general | solution.py:23
  97.2 0.7 multiply_reduce_fusion
  97.9 0.6 multiply_reduce_fusion.2
  98.6 2.6 %fusion.7 = bf16[1,2048,128]{2,1,0:T(8,128)(2,1)} fusion(f32[2048,128]{1,0:T(8,128)S(1)} %get-tuple-element.14, bf16[512,128]{1,0:T(8,128)(2,1)S(1)} %copy-done, bf16[128,512]{1,0:T(8,128)(2,1)S(1)} %copy-done.9, f32[128]{0:T(128)S(1)} %copy-done.10, f32[2048]{0:T(1024)S(1)} %add_rsqrt_fusion), kind=kOutput, calls=%fused_computation.12 | convolution fusion | flops 543424512 | bytes 1843712 | tf_op jit(solution)/shard_map/dot_general | solution.py:49
  (42 shorter events, 1.6 us)
Async XLA Ops:
  6.5 92.0 %copy-start = (bf16[512,128]{1,0:T(8,128)(2,1)S(1)}, bf16[512,128]{1,0:T(8,128)(2,1)}, u32[]{:S(2)}) copy-start(bf16[512,128]{1,0:T(8,128)(2,1)} %param.25) | copy-start | bytes 393220
  6.5 18.8 %copy-start.8 = (s32[1,112]{1,0:T(1,128)S(1)}, s32[1,112]{1,0:T(1,128)}, u32[]{:S(2)}) copy-start(s32[1,112]{1,0:T(1,128)} %param.16) | copy-start | bytes 1348
  6.5 14.1 %collective-permute-start = (bf16[2048,128]{1,0:T(8,128)(2,1)}, bf16[2048,128]{1,0:T(8,128)(2,1)S(1)}, u32[]{:S(2)}, u32[]{:S(2)}) collective-permute-start(bf16[2048,128]{1,0:T(8,128)(2,1)} %param.13), channel_id=1, source_target_pairs={{0,1},{1,0},{2,3},{3,2},{4,5},{5,4},{6,7},{7,6},{8,9},{9,8},{10,11... | collective-permute-start | bytes 1572872 | tf_op jit(solution)/shard_map/ppermute | solution.py:16
  9.1 11.5 %all-to-all-start = ((s32[8,1,2]{2,1,0:T(1,128)}), s32[8,1,2]{2,1,0:T(1,128)S(1)}, u32[]{:S(2)}, u32[]{:S(2)}) async-start(s32[8,1,2]{2,1,0:T(1,128)} %copy.43), calls=%async_computation | async-start | bytes 8192 | tf_op jit(solution)/shard_map/all_to_all | solution.py:79
  22.0 10.1 %all-to-all-start.1 = ((bf16[8,64,128]{2,1,0:T(8,128)(2,1)}), bf16[8,64,128]{2,1,0:T(8,128)(2,1)S(1)}, u32[]{:S(2)}, u32[]{:S(2)}) async-start(bf16[8,64,128]{2,1,0:T(8,128)(2,1)} %copy.49), calls=%async_computation.1 | async-start | bytes 262144 | tf_op jit(solution)/shard_map/all_to_all | solution.py:100
  25.3 67.5 %all-gather.3.cloned.1.call-start = ((), (), s32[]{:S(2)}) async-start(), calls=%async_computation.2 | async-start | bytes 2621440 | tf_op jit(solution)/shard_map/all_gather | solution.py:113
  43.8 8.5 %copy-start.7 = (s32[1,112]{1,0:T(1,128)S(1)}, s32[1,112]{1,0:T(1,128)}, u32[]{:S(2)}) copy-start(s32[1,112]{1,0:T(1,128)} %param.15) | copy-start | bytes 1348
  52.3 5.1 %copy-start.2 = (bf16[2048,128]{1,0:T(8,128)(2,1)S(1)}, bf16[2048,128]{1,0:T(8,128)(2,1)}, u32[]{:S(2)}) copy-start(bf16[2048,128]{1,0:T(8,128)(2,1)} %param.13) | copy-start | bytes 1572868
  57.0 1.4 %copy-start.4 = (bf16[128,128]{1,0:T(8,128)(2,1)S(1)}, bf16[128,128]{1,0:T(8,128)(2,1)}, u32[]{:S(2)}) copy-start(bf16[128,128]{1,0:T(8,128)(2,1)} %param.19) | copy-start | bytes 98308
  57.0 1.5 %copy-start.5 = (bf16[128,128]{1,0:T(8,128)(2,1)S(1)}, bf16[128,128]{1,0:T(8,128)(2,1)}, u32[]{:S(2)}) copy-start(bf16[128,128]{1,0:T(8,128)(2,1)} %param.20) | copy-start | bytes 98308
  57.0 1.6 %copy-start.6 = (bf16[128,128]{1,0:T(8,128)(2,1)S(1)}, bf16[128,128]{1,0:T(8,128)(2,1)}, u32[]{:S(2)}) copy-start(bf16[128,128]{1,0:T(8,128)(2,1)} %param.21) | copy-start | bytes 98308
  94.2 3.0 %copy-start.1 = (bf16[8192,128]{1,0:T(8,128)(2,1)S(1)}, bf16[8192,128]{1,0:T(8,128)(2,1)}, u32[]{:S(2)}) copy-start(bf16[8192,128]{1,0:T(8,128)(2,1)} %all-gather.3.cloned.1.call-done) | copy-start | bytes 6291460
  96.8 1.2 %copy-start.3 = (bf16[128,128]{1,0:T(8,128)(2,1)S(1)}, bf16[128,128]{1,0:T(8,128)(2,1)}, u32[]{:S(2)}) copy-start(bf16[128,128]{1,0:T(8,128)(2,1)} %param.22) | copy-start | bytes 98308
  97.1 1.4 %copy-start.9 = (bf16[128,512]{1,0:T(8,128)(2,1)S(1)}, bf16[128,512]{1,0:T(8,128)(2,1)}, u32[]{:S(2)}) copy-start(bf16[128,512]{1,0:T(8,128)(2,1)} %param.24) | copy-start | bytes 393220
  97.2 1.4 %copy-start.10 = (f32[128]{0:T(128)S(1)}, f32[128]{0:T(128)}, u32[]{:S(2)}) copy-start(f32[128]{0:T(128)} %param.23) | copy-start | bytes 1540
Sparse Core Ops, SparseCore 0:
  58.5 34.3 all-gather.2
where the time goes:
time: 108 us
  waiting for transfers between devices  41 us (38%)
  matrix products  21.5 us (20%)
  local copies, waits for them, and re-layouts  16.8 us (16%)
  between operations  14.3 us (13%)
  starting transfers between devices  9.85 us (9%)
  other arithmetic  4.5 us (4%)
    all_gather x1, waiting for transfers between devices, shards(): everyone = lax.all_gather(spread[None], 'beh', axis=0, tiled=True)  34.1 us
    dot_general x1, matrix products, shards(): jnp.einsum('tij,tjd->tid', adjacency[0], sources, preferred_element_type=...  8.8 us
    dot_general x1, local copies, waits for them, and re-layouts, shards(): jnp.einsum('tij,tjd->tid', adjacency[0], sources, preferred_element_type=...  8.48 us
    all_to_all x1, starting transfers between devices, shards(): lax.all_to_all(request_pair, 'node', split_axis=0, concat_axis=0, tiled=T...  5.99 us
    dot_general x1, matrix products, shards(): jnp.einsum('tb,tid->bid', select, product, precision=lax.Precision.HIGHEST)  4.67 us
    gather x2, local copies, waits for them, and re-layouts, shards(): sources = pairs[owners[tile_cols[0]] // 2]  3.63 us
    all_to_all x1, waiting for transfers between devices, shards(): lax.all_to_all(outgoing, 'node', split_axis=0, concat_axis=0, tiled=True)  3.48 us
    all_to_all x1, waiting for transfers between devices, shards(): lax.all_to_all(request_pair, 'node', split_axis=0, concat_axis=0, tiled=T...  3.44 us
  transfers between devices with their start and end apart: 4, of which 3 were waited for; matrix products, arithmetic and copies ran while one was open for 7% of the time, Pallas kernels for 0%

commit v1 on v0

v1 whole, which is shorter than its diff:
```python
import functools
import math

import jax
import jax.numpy as jnp
from jax import lax
from jax.experimental import pallas as pl
from jax.experimental.pallas import tpu as pltpu
from jax.sharding import PartitionSpec as P

TB = 128
HEADS = 4
HEAD = 32
F32 = jnp.float32
BF16 = jnp.bfloat16
SMEM = pl.BlockSpec(memory_space=pltpu.SMEM)
VMEM = pl.BlockSpec(memory_space=pltpu.VMEM)
ANY = pl.BlockSpec(memory_space=pl.ANY)
VMEM_LIMIT = 48 * 2**20


def exchange(value, axis, mask):
    pairs = [(source, source ^ mask) for source in range(lax.axis_size(axis))]
    return lax.ppermute(value, axis, pairs)


def params(**more):
    return pltpu.CompilerParams(vmem_limit_bytes=VMEM_LIMIT, **more)


def cost(flops, moved):
    return pl.CostEstimate(flops=flops, bytes_accessed=moved, transcendentals=0)


def cells_kernel(chunk, pairs, cell_count, place, rows, cols, count, tiles, out, total):
    step = pl.program_id(0)

    @pl.when(step == 0)
    def _():
        total[...] = jnp.zeros_like(total)

    for i in range(chunk):
        slot = step * chunk + i
        cell = rows[0, slot] * pairs + (cols[0, slot] ^ place[0])
        cell = jnp.where(slot < count[0, 0], cell, cell_count)
        total[cell] += tiles[i].astype(F32)

    @pl.when(step == pl.num_programs(0) - 1)
    def _():
        out[...] = total[:cell_count].astype(BF16)


def sum_cells(place, rows, cols, count, tiles, pairs, block_count):
    slots = tiles.shape[0]
    chunk = math.gcd(slots, 16)
    cell_count = pairs * block_count
    return pl.pallas_call(
        functools.partial(cells_kernel, chunk, pairs, cell_count),
        grid=(slots // chunk,),
        in_specs=[SMEM] * 4 + [pl.BlockSpec((chunk, TB, TB), lambda s: (s, 0, 0))],
        out_specs=pl.BlockSpec((cell_count, TB, TB), lambda s: (0, 0, 0)),
        out_shape=jax.ShapeDtypeStruct((cell_count, TB, TB), BF16),
        scratch_shapes=[pltpu.VMEM((cell_count + 1, TB, TB), F32)],
        compiler_params=params(),
        cost_estimate=cost(0, tiles.size * 2),
        name="cells",
    )(place, rows, cols, count, tiles)


def serve_kernel(block_count, pairs, place, *refs):
    asks, (own, other), outs, sems = refs[:pairs], refs[pairs : pairs + 2], refs[pairs + 2 : -1], refs[-1]
    here, core = place[0], place[1]
    for phase in (0, 1):
        for k in range(pairs):
            block = asks[k][0, here] - 2 * here * block_count
            upper = (block >= block_count).astype(jnp.int32)
            start = pl.multiple_of((block - upper * block_count) * TB, TB)
            for source, match in ((own, upper == core), (other, upper != core)):

                @pl.when(match)
                def _():
                    copy = pltpu.make_async_copy(source.at[pl.ds(start, TB), :], outs[k], sems.at[k])
                    if phase == 0:
                        copy.start()
                    else:
                        copy.wait()


def serve(place, asks, own, other, block_count):
    pairs = len(asks)
    return pl.pallas_call(
        functools.partial(serve_kernel, block_count, pairs),
        in_specs=[SMEM] * (1 + pairs) + [ANY] * 2,
        out_specs=[ANY] * pairs,
        out_shape=[jax.ShapeDtypeStruct((TB, own.shape[1]), own.dtype)] * pairs,
        scratch_shapes=[pltpu.SemaphoreType.DMA((pairs,))],
        name="serve",
    )(place, *asks, own, other)


def spread_kernel(pairs, order, cells, *refs):
    sources, own, outs = refs[:pairs], refs[pairs], refs[pairs + 1 :]
    feature = own.shape[1]
    stack = jnp.concatenate([s[...] for s in sources], axis=0)
    size = outs[0].shape[0]
    for k, out in enumerate(outs):
        start = pl.multiple_of(order[k] * size, size)
        block = order[k] * (size // TB)
        for r in range(size // TB):
            lhs = jnp.concatenate([cells[(block + r) * pairs + m] for m in range(pairs)], axis=1)
            part = jnp.dot(lhs, stack, preferred_element_type=F32)
            rows = own[pl.ds(start + r * TB, TB), :].astype(F32)
            out[r * TB : (r + 1) * TB, :] = (part + rows).astype(BF16)


def spread_cells(order, cells, sources, own, parts):
    size = own.shape[0] // parts
    return pl.pallas_call(
        functools.partial(spread_kernel, len(sources)),
        in_specs=[SMEM] + [VMEM] * (len(sources) + 2),
        out_specs=[VMEM] * parts,
        out_shape=[jax.ShapeDtypeStruct((size, own.shape[1]), BF16)] * parts,
        compiler_params=params(),
        name="spread",
    )(order, cells, *sources, own)


def merge_kernel(count, tile, *refs):
    xs = refs[:count]
    w_qkv, w_out, gain, w_up, w_down = refs[count : count + 5]
    outs = refs[count + 5 :]
    feature = w_out.shape[0]
    scale = math.log2(math.e) / math.sqrt(HEAD)

    def body(step, carry):
        start = pl.multiple_of(step * tile, tile)
        rows = pl.ds(start, tile)
        queries, keys, values = [], [], []
        for x in xs:
            full = lax.dot_general(
                w_qkv[...], x[rows, :], (((1,), (1,)), ((), ())), preferred_element_type=F32
            )
            queries.append(full[:feature].reshape(HEADS, HEAD, tile) * scale)
            keys.append(full[feature : 2 * feature].reshape(HEADS, HEAD, tile))
            values.append(full[2 * feature :].reshape(HEADS, HEAD, tile))
        for x, query, out in zip(xs, queries, outs):
            scores = [jnp.sum(query * key, axis=1, keepdims=True) for key in keys]
            top = functools.reduce(jnp.maximum, scores)
            weights = [jnp.exp2(s - top) for s in scores]
            inverse = 1.0 / functools.reduce(jnp.add, weights)
            mixture = functools.reduce(
                jnp.add, [(w * inverse) * value for w, value in zip(weights, values)]
            )
            mixture = mixture.reshape(feature, tile).astype(BF16)
            residual = x[rows, :].astype(F32) + lax.dot_general(
                mixture, w_out[...], (((0,), (0,)), ((), ())), preferred_element_type=F32
            )
            meansq = jnp.mean(residual * residual, axis=-1, keepdims=True)
            normed = (residual * lax.rsqrt(meansq + 1e-06) * gain[...]).astype(BF16)
            half = 0.5 * jnp.dot(normed, w_up[...], preferred_element_type=F32)
            hidden = (half + half * jnp.tanh(half)).astype(BF16)
            result = residual + jnp.dot(hidden, w_down[...], preferred_element_type=F32)
            out[rows, :] = result.astype(BF16)
        return carry

    lax.fori_loop(0, xs[0].shape[0] // tile, body, 0)


def merge(xs, w_qkv, w_out, gain, w_up, w_down):
    size, feature = xs[0].shape
    tile = math.gcd(size, 256)
    return pl.pallas_call(
        functools.partial(merge_kernel, len(xs), tile),
        in_specs=[VMEM] * (len(xs) + 5),
        out_specs=[VMEM] * len(xs),
        out_shape=[jax.ShapeDtypeStruct((size, feature), BF16)] * len(xs),
        compiler_params=params(),
        name="merge",
    )(*xs, w_qkv, w_out, gain, w_up, w_down)


def place_kernel(order, *refs):
    parts, out, sems = refs[:-2], refs[-2], refs[-1]
    size = parts[0].shape[0]
    copies = []
    for k, part in enumerate(parts):
        start = pl.multiple_of(order[k] * size, size)
        copies.append(pltpu.make_async_copy(part, out.at[pl.ds(start, size), :], sems.at[k]))
        copies[-1].start()
    for copy in copies:
        copy.wait()


def place_parts(order, parts):
    size, feature = parts[0].shape
    return pl.pallas_call(
        place_kernel,
        in_specs=[SMEM] + [ANY] * len(parts),
        out_specs=ANY,
        out_shape=jax.ShapeDtypeStruct((size * len(parts), feature), BF16),
        scratch_shapes=[pltpu.SemaphoreType.DMA((len(parts),))],
        name="place",
    )(order, *parts)


def tiles_kernel(chunk, rows, cols, count, tiles, sources, own, out, total):
    step = pl.program_id(0)

    @pl.when(step == 0)
    def _():
        total[...] = own[...].astype(F32)

    for i in range(chunk):
        slot = step * chunk + i

        @pl.when(slot < count[0, 0])
        def _():
            start = pl.multiple_of(rows[0, slot] * TB, TB)
            total[pl.ds(start, TB), :] += jnp.dot(
                tiles[i], sources[cols[0, slot]], preferred_element_type=F32
            )

    @pl.when(step == pl.num_programs(0) - 1)
    def _():
        out[...] = total[...].astype(BF16)


def spread_tiles(rows, cols, count, tiles, sources, own):
    slots = tiles.shape[0]
    chunk = math.gcd(slots, 16)
    return pl.pallas_call(
        functools.partial(tiles_kernel, chunk),
        grid=(slots // chunk,),
        in_specs=[SMEM] * 3
        + [
            pl.BlockSpec((chunk, TB, TB), lambda s: (s, 0, 0)),
            pl.BlockSpec(sources.shape, lambda s: (0, 0, 0)),
            pl.BlockSpec(own.shape, lambda s: (0, 0)),
        ],
        out_specs=pl.BlockSpec(own.shape, lambda s: (0, 0)),
        out_shape=jax.ShapeDtypeStruct(own.shape, BF16),
        scratch_shapes=[pltpu.VMEM(own.shape, F32)],
        compiler_params=params(),
        name="tiles",
    )(rows, cols, count, tiles, sources, own)


def fetch_many(embeddings, need_ids, block_count):
    peer_count = lax.axis_size("node")
    feature = embeddings.shape[1]
    needed = need_ids[0]
    owners = needed // block_count
    within = needed % block_count
    peer_ids = jnp.arange(peer_count, dtype=jnp.int32)
    matches = owners[:, None] == peer_ids[None, :]
    request = jnp.sum(jnp.where(matches, within[:, None] + 1, 0), axis=0)
    swapped = request.reshape(-1, 2)[:, ::-1].reshape(-1)
    request_pair = jnp.stack([request, swapped], axis=1)
    incoming = lax.all_to_all(request_pair, "node", split_axis=0, concat_axis=0, tiled=True)
    parity = lax.axis_index("node") % 2
    own = embeddings.reshape(block_count, TB, feature)
    other = exchange(embeddings, "node", 1).reshape(block_count, TB, feature)
    stack = jnp.concatenate([own, other], axis=0)
    codes = jnp.where(incoming[:, 0] > 0, incoming[:, 0], block_count + incoming[:, 1])
    half = TB // 2
    halves = lax.dynamic_slice_in_dim(stack, parity * half, half, 1)
    chooser = (codes[:, None] - 1 == jnp.arange(2 * block_count, dtype=jnp.int32)[None, :]).astype(BF16)
    outgoing = jnp.einsum("pk,kid->pid", chooser, halves, preferred_element_type=F32).astype(BF16)
    arrived = lax.all_to_all(outgoing, "node", split_axis=0, concat_axis=0, tiled=True)
    return arrived.reshape(peer_count // 2, TB, feature)


def shards(
    embeddings,
    adjacency,
    tile_rows,
    tile_cols,
    tile_count,
    need_ids,
    w_query,
    w_key,
    w_value,
    w_out,
    mlp_gain,
    w_up,
    w_down,
):
    parts = lax.axis_size("beh")
    pairs = lax.axis_size("node") // 2
    block_count = embeddings.shape[0] // TB
    tiles = adjacency[0]
    me = lax.axis_index("beh")
    here = lax.axis_index("node")
    order = jnp.stack([me ^ k for k in range(parts)]).astype(jnp.int32)
    if pairs * block_count <= tiles.shape[0]:
        place = jnp.stack([here // 2, here % 2]).astype(jnp.int32)
        asks = [need_ids] + [exchange(need_ids, "node", 2 * k) for k in range(1, pairs)]
        other = exchange(embeddings, "node", 1)
        cells = sum_cells(place, tile_rows, tile_cols, tile_count, tiles, pairs, block_count)
        served = serve(place, asks, embeddings, other, block_count)
        sources = [served[0]] + [exchange(served[k], "node", 2 * k) for k in range(1, pairs)]
        quarters = spread_cells(order, cells, sources, embeddings, parts)
    else:
        sources = fetch_many(embeddings, need_ids, block_count)
        spread = spread_tiles(tile_rows, tile_cols, tile_count, tiles, sources, embeddings)
        size = spread.shape[0] // parts
        quarters = [lax.dynamic_slice_in_dim(spread, order[k] * size, size, 0) for k in range(parts)]
    xs = [quarters[0]] + [exchange(quarters[k], "beh", k) for k in range(1, parts)]
    w_qkv = jnp.concatenate([w_query, w_key, w_value], axis=1).T
    merged = merge(xs, w_qkv, w_out, mlp_gain[None], w_up, w_down)
    back = [merged[0]] + [exchange(merged[k], "beh", k) for k in range(1, parts)]
    return place_parts(order, back)[None]


def solution(mesh):
    in_specs = (
        P("node", None),
        P("beh", "node", None, None),
        P("beh", "node"),
        P("beh", "node"),
        P("beh", "node"),
        P("beh", "node"),
        P(),
        P(),
        P(),
        P(),
        P(),
        P(),
        P(),
    )
    out_specs = P("beh", "node", None)
    return jax.shard_map(shards, mesh=mesh, in_specs=in_specs, out_specs=out_specs, check_vma=False)
```

time: 108 us -> 71.3 us (0.66)
  Pallas kernels: 0 us -> 32.1 us
  waiting for transfers between devices: 41 us -> 13.3 us
  matrix products: 21.5 us -> 0 us
  between operations: 14.3 us -> 0.88 us
  local copies, waits for them, and re-layouts: 16.8 us -> 6.99 us
  starting transfers between devices: 9.85 us -> 17.2 us
  other arithmetic: 4.5 us -> 0.69 us
    all_gather x1 -> x0, waiting for transfers between devices: 34.1 us -> none  [shards(): everyone = lax.all_gather(spread[None], 'beh', axis=0, tiled=True)]
    pallas_call x0 -> x5, Pallas kernels: none -> 32.1 us  [the longest x1 17.7 us: place_parts(): pl.pallas_call(place_kernel, in_specs=[SMEM] + [ANY] * len(parts), out_sp...]
    dot_general x8 -> x0, matrix products: 21.5 us -> none  [the longest x1 8.8 us: shards(): jnp.einsum('tij,tjd->tid', adjacency[0], sources, preferred_element_type=...]
    ppermute x1 -> x13, starting transfers between devices: 0.45 us -> 17.2 us  [exchange(): return lax.ppermute(value, axis, pairs)]
    ppermute x1 -> x13, waiting for transfers between devices: 0.01 us -> 13.3 us  [exchange(): return lax.ppermute(value, axis, pairs)]
    all_to_all x2 -> x0, starting transfers between devices: 9.36 us -> none  [the longest x1 5.99 us: shards(): lax.all_to_all(request_pair, 'node', split_axis=0, concat_axis=0, tiled=T...]
    dot_general x2 -> x0, local copies, waits for them, and re-layouts: 8.82 us -> none  [the longest x1 8.48 us: shards(): jnp.einsum('tij,tjd->tid', adjacency[0], sources, preferred_element_type=...]
    all_to_all x2 -> x0, waiting for transfers between devices: 6.91 us -> none  [the longest x1 3.48 us: shards(): lax.all_to_all(outgoing, 'node', split_axis=0, concat_axis=0, tiled=True)]
  transfers between devices with their start and end apart: 4 -> 13, of which waited for: 3 -> 8; matrix products, arithmetic and copies ran while one was open for 7% -> 1% of each run, Pallas kernels for 0% -> 3%
where the time goes in v1:
time: 71.3 us; the launch traced here: 71.1 us
  Pallas kernels  32.1 us (45%)
  starting transfers between devices  17.2 us (24%)
  waiting for transfers between devices  13.3 us (19%)
  local copies, waits for them, and re-layouts  6.99 us (10%)
  between operations  0.88 us (1%)
    pallas_call x1, Pallas kernels, place_parts(): pl.pallas_call(place_kernel, in_specs=[SMEM] + [ANY] * len(parts), out_sp...  17.7 us
    ppermute x13, starting transfers between devices, exchange(): return lax.ppermute(value, axis, pairs)  17.2 us
    ppermute x13, waiting for transfers between devices, exchange(): return lax.ppermute(value, axis, pairs)  13.3 us
    unnamed x47, local copies, waits for them, and re-layouts  6.99 us
    pallas_call x1, Pallas kernels, serve(): pl.pallas_call(functools.partial(serve_kernel, block_count, pairs), in_sp...  5.81 us
    pallas_call x1, Pallas kernels, merge(): pl.pallas_call(functools.partial(merge_kernel, len(xs), tile), in_specs=[...  5.2 us
    pallas_call x1, Pallas kernels, sum_cells(): pl.pallas_call(functools.partial(cells_kernel, chunk, pairs, cell_count),...  2.16 us
  transfers between devices with their start and end apart: 13, of which 8 were waited for; matrix products, arithmetic and copies ran while one was open for 1% of the time, Pallas kernels for 3%

profile of v1, /device:TPU:0, one launch (start us, length us, event | category | flops | bytes accessed | tf_op | source)
XLA Modules:
  0.0 71.1 jit_solution(17695790362418938380)
XLA Ops:
  0.5 2.6 %collective-permute-start = (s32[1,4]{1,0:T(1,128)}, s32[1,4]{1,0:T(1,128)S(1)}, u32[]{:S(2)}, u32[]{:S(2)}) collective-permute-start(s32[1,4]{1,0:T(1,128)} %refs_0_.1), channel_id=1, source_target_pairs={{0,2},{1,3},{2,0},{3,1},{4,6},{5,7},{6,4},{7,5},{8,10},{9,11},{10,... | collective-permute-start | bytes 56 | tf_op jit(solution)/shard_map/ppermute | solution.py:24
  3.1 2.6 %collective-permute-start.1 = (s32[1,4]{1,0:T(1,128)}, s32[1,4]{1,0:T(1,128)S(1)}, u32[]{:S(2)}, u32[]{:S(2)}) collective-permute-start(s32[1,4]{1,0:T(1,128)} %refs_0_.1), channel_id=1, source_target_pairs={{0,4},{1,5},{2,6},{3,7},{4,0},{5,1},{6,2},{7,3},{8,12},{9,13},{10,... | collective-permute-start | bytes 56 | tf_op jit(solution)/shard_map/ppermute | solution.py:24
  6.3 1.4 %collective-permute-done.1.refs_2_ = s32[1,4]{1,0:T(1,128)S(1)} collective-permute-done((s32[1,4]{1,0:T(1,128)}, s32[1,4]{1,0:T(1,128)S(1)}, u32[]{:S(2)}, u32[]{:S(2)}) %collective-permute-start.1) | collective-permute-done | bytes 48 | tf_op jit(solution)/shard_map/ppermute | solution.py:24
  7.7 3.5 %collective-permute-done.2.refs_3_ = s32[1,4]{1,0:T(1,128)S(1)} collective-permute-done((s32[1,4]{1,0:T(1,128)}, s32[1,4]{1,0:T(1,128)S(1)}, u32[]{:S(2)}, u32[]{:S(2)}) %collective-permute-start.2) | collective-permute-done | bytes 48 | tf_op jit(solution)/shard_map/ppermute | solution.py:24
  11.7 0.8 %copy-done.12 = bf16[2048,128]{1,0:T(8,128)(2,1)} copy-done((bf16[2048,128]{1,0:T(8,128)(2,1)}, bf16[2048,128]{1,0:T(8,128)(2,1)S(1)}, u32[]{:S(2)}) %copy-start.12) | copy-done | bytes 524312
  12.5 5.8 %serve.1 = (bf16[128,128]{1,0:T(8,128)(2,1)}, bf16[128,128]{1,0:T(8,128)(2,1)}, bf16[128,128]{1,0:T(8,128)(2,1)}, bf16[128,128]{1,0:T(8,128)(2,1)}) custom-call(s32[2]{0:T(128)} %pad_add_fusion.1.place, s32[1,4]{1,0:T(1,128)} %refs_0_.1, s32[1,4]{1,0:T(1,128)} %copy-done.19, s32[1,4]{1,0:T(1,128)} %copy-done.20, s32[1,4]{1,0:T(1,128)} %copy-done.21, ...), custom_call_target="tpu_custom_call" | custom-call | tf_op jit(solution)/shard_map/serve/pallas_call | solution.py:91
  19.0 3.8 %collective-permute-start.6 = (bf16[128,128]{1,0:T(8,128)(2,1)}, bf16[128,128]{1,0:T(8,128)(2,1)S(1)}, u32[]{:S(2)}, u32[]{:S(2)}) collective-permute-start(bf16[128,128]{1,0:T(8,128)(2,1)} %get-tuple-element.20), channel_id=1, source_target_pairs={{0,6},{1,7},{2,4},{3,5},{4,2},{5,3},{6,0},{7,1},{8,14},{9,15},{10,... | collective-permute-start | bytes 98312 | tf_op jit(solution)/shard_map/ppermute | solution.py:24
  23.5 2.0 %copy-done = bf16[1,112,128,128]{3,2,1,0:T(8,128)(2,1)S(1)} copy-done((bf16[1,112,128,128]{3,2,1,0:T(8,128)(2,1)S(1)}, bf16[1,112,128,128]{3,2,1,0:T(8,128)(2,1)}, u32[]{:S(2)}) %copy-start) | copy-done | bytes 3670040
  26.2 0.7 copy-done.10
  26.8 0.7 copy-done.11
  27.6 2.2 %cells.1 = bf16[64,128,128]{2,1,0:T(8,128)(2,1)S(1)} custom-call(s32[2]{0:T(128)S(1)} %copy-done.8, s32[1,112]{1,0:T(1,128)S(1)} %copy-done.10, s32[1,112]{1,0:T(1,128)S(1)} %copy-done.11, s32[1,1]{1,0:T(1,128)S(6)} %copy.17.count, bf16[112,128,128]{2,1,0:T(8,128)(2,1)S(1)} %bitcast.11), custom_call_target="tpu_custom_call" | custom-call | bytes 3670016 | tf_op jit(solution)/shard_map/cells/pallas_call | solution.py:57
  29.8 1.2 %spread.1 = (bf16[512,128]{1,0:T(8,128)(2,1)S(1)}, bf16[512,128]{1,0:T(8,128)(2,1)S(1)}, bf16[512,128]{1,0:T(8,128)(2,1)S(1)}, bf16[512,128]{1,0:T(8,128)(2,1)S(1)}) custom-call(s32[4]{0:T(128)S(1)} %pad_add_fusion.order, bf16[64,128,128]{2,1,0:T(8,128)(2,1)S(1)} %cells.1, bf16[128,128]{1,0:T(8,128)(2,1)S(1)} %copy-done.5, ...), custom_call_target="tpu_custom_call" | custom-call | tf_op jit(solution)/shard_map/spread/pallas_call | solution.py:118
  31.0 1.6 %collective-permute-start.7 = (bf16[512,128]{1,0:T(8,128)(2,1)S(1)}, bf16[512,128]{1,0:T(8,128)(2,1)S(1)}, u32[]{:S(2)}, u32[]{:S(2)}) collective-permute-start(bf16[512,128]{1,0:T(8,128)(2,1)S(1)} %get-tuple-element.22), channel_id=1, source_target_pairs={{0,8},{8,0},{16,24},{24,16},{1,9},{9,1},{17,25},{25,17},{2,10},{10... | collective-permute-start | bytes 393224 | tf_op jit(solution)/shard_map/ppermute | solution.py:24
  32.6 1.5 %collective-permute-start.8 = (bf16[512,128]{1,0:T(8,128)(2,1)S(1)}, bf16[512,128]{1,0:T(8,128)(2,1)S(1)}, u32[]{:S(2)}, u32[]{:S(2)}) collective-permute-start(bf16[512,128]{1,0:T(8,128)(2,1)S(1)} %get-tuple-element.23), channel_id=1, source_target_pairs={{0,16},{8,24},{16,0},{24,8},{1,17},{9,25},{17,1},{25,9},{2,18},{10... | collective-permute-start | bytes 393224 | tf_op jit(solution)/shard_map/ppermute | solution.py:24
  35.0 1.8 %collective-permute-done.7.refs_1_ = bf16[512,128]{1,0:T(8,128)(2,1)S(1)} collective-permute-done((bf16[512,128]{1,0:T(8,128)(2,1)S(1)}, bf16[512,128]{1,0:T(8,128)(2,1)S(1)}, u32[]{:S(2)}, u32[]{:S(2)}) %collective-permute-start.7) | collective-permute-done | bytes 131104 | tf_op jit(solution)/shard_map/ppermute | solution.py:24
  36.8 1.3 %collective-permute-done.8.refs_2_ = bf16[512,128]{1,0:T(8,128)(2,1)S(1)} collective-permute-done((bf16[512,128]{1,0:T(8,128)(2,1)S(1)}, bf16[512,128]{1,0:T(8,128)(2,1)S(1)}, u32[]{:S(2)}, u32[]{:S(2)}) %collective-permute-start.8) | collective-permute-done | bytes 131104 | tf_op jit(solution)/shard_map/ppermute | solution.py:24
  38.1 1.9 %collective-permute-done.9.refs_3_ = bf16[512,128]{1,0:T(8,128)(2,1)S(1)} collective-permute-done((bf16[512,128]{1,0:T(8,128)(2,1)S(1)}, bf16[512,128]{1,0:T(8,128)(2,1)S(1)}, u32[]{:S(2)}, u32[]{:S(2)}) %collective-permute-start.9) | collective-permute-done | bytes 131104 | tf_op jit(solution)/shard_map/ppermute | solution.py:24
  40.0 5.2 %merge.1 = (bf16[512,128]{1,0:T(8,128)(2,1)S(1)}, bf16[512,128]{1,0:T(8,128)(2,1)S(1)}, bf16[512,128]{1,0:T(8,128)(2,1)S(1)}, bf16[512,128]{1,0:T(8,128)(2,1)S(1)}) custom-call(bf16[512,128]{1,0:T(8,128)(2,1)S(1)} %get-tuple-element.21.refs_0_, bf16[512,128]{1,0:T(8,128)(2,1)S(1)} %collective-permute-done.7.refs_1_, ...), custom_call_target="tpu_custom_call" | custom-call | tf_op jit(solution)/shard_map/merge/pallas_call | solution.py:172
  45.2 0.6 copy-done.4
  46.9 2.4 %collective-permute-start.12 = (bf16[512,128]{1,0:T(8,128)(2,1)S(1)}, bf16[512,128]{1,0:T(8,128)(2,1)S(1)}, u32[]{:S(2)}, u32[]{:S(2)}) collective-permute-start(bf16[512,128]{1,0:T(8,128)(2,1)S(1)} %get-tuple-element.28), channel_id=1, source_target_pairs={{0,24},{8,16},{16,8},{24,0},{1,25},{9,17},{17,9},{25,1},{2,26},{10... | collective-permute-start | bytes 393224 | tf_op jit(solution)/shard_map/ppermute | solution.py:24
  49.4 1.5 %collective-permute-done.10.refs_1_ = bf16[512,128]{1,0:T(8,128)(2,1)S(1)} collective-permute-done((bf16[512,128]{1,0:T(8,128)(2,1)S(1)}, bf16[512,128]{1,0:T(8,128)(2,1)S(1)}, u32[]{:S(2)}, u32[]{:S(2)}) %collective-permute-start.10) | collective-permute-done | bytes 131104 | tf_op jit(solution)/shard_map/ppermute | solution.py:24
  51.4 1.4 %collective-permute-done.12.refs_3_ = bf16[512,128]{1,0:T(8,128)(2,1)S(1)} collective-permute-done((bf16[512,128]{1,0:T(8,128)(2,1)S(1)}, bf16[512,128]{1,0:T(8,128)(2,1)S(1)}, u32[]{:S(2)}, u32[]{:S(2)}) %collective-permute-start.12) | collective-permute-done | bytes 131104 | tf_op jit(solution)/shard_map/ppermute | solution.py:24
  52.8 0.7 copy-done.15
  53.5 17.7 %place.1 = bf16[2048,128]{1,0:T(8,128)(2,1)} custom-call(s32[4]{0:T(128)} %copy-done.7, bf16[512,128]{1,0:T(8,128)(2,1)} %copy-done.4, bf16[512,128]{1,0:T(8,128)(2,1)} %copy-done.13, bf16[512,128]{1,0:T(8,128)(2,1)} %copy-done.14, bf16[512,128]{1,0:T(8,128)(2,1)} %copy-done.15), custom_call_target="tpu_custom_call" | custom-call | tf_op jit(solution)/shard_map/place/pallas_call | solution.py:196
  (57 shorter events, 5.5 us)
Async XLA Ops:
  0.0 29.8 %copy-start.1 = (bf16[2048,128]{1,0:T(8,128)(2,1)S(1)}, bf16[2048,128]{1,0:T(8,128)(2,1)}, u32[]{:S(2)}) copy-start(bf16[2048,128]{1,0:T(8,128)(2,1)} %refs_4_.3) | copy-start | bytes 1572868
  0.0 11.2 %collective-permute-start.3 = (bf16[2048,128]{1,0:T(8,128)(2,1)}, bf16[2048,128]{1,0:T(8,128)(2,1)S(1)}, u32[]{:S(2)}, u32[]{:S(2)}) collective-permute-start(bf16[2048,128]{1,0:T(8,128)(2,1)} %refs_4_.3), channel_id=1, source_target_pairs={{0,1},{1,0},{2,3},{3,2},{4,5},{5,4},{6,7},{7,6},{8,9},{9,8},{10,11... | collective-permute-start | bytes 1572872 | tf_op jit(solution)/shard_map/ppermute | solution.py:24
  0.5 5.8 %collective-permute-start = (s32[1,4]{1,0:T(1,128)}, s32[1,4]{1,0:T(1,128)S(1)}, u32[]{:S(2)}, u32[]{:S(2)}) collective-permute-start(s32[1,4]{1,0:T(1,128)} %refs_0_.1), channel_id=1, source_target_pairs={{0,2},{1,3},{2,0},{3,1},{4,6},{5,7},{6,4},{7,5},{8,10},{9,11},{10,... | collective-permute-start | bytes 56 | tf_op jit(solution)/shard_map/ppermute | solution.py:24
  3.1 4.6 %collective-permute-start.1 = (s32[1,4]{1,0:T(1,128)}, s32[1,4]{1,0:T(1,128)S(1)}, u32[]{:S(2)}, u32[]{:S(2)}) collective-permute-start(s32[1,4]{1,0:T(1,128)} %refs_0_.1), channel_id=1, source_target_pairs={{0,4},{1,5},{2,6},{3,7},{4,0},{5,1},{6,2},{7,3},{8,12},{9,13},{10,... | collective-permute-start | bytes 56 | tf_op jit(solution)/shard_map/ppermute | solution.py:24
  5.7 5.5 %collective-permute-start.2 = (s32[1,4]{1,0:T(1,128)}, s32[1,4]{1,0:T(1,128)S(1)}, u32[]{:S(2)}, u32[]{:S(2)}) collective-permute-start(s32[1,4]{1,0:T(1,128)} %refs_0_.1), channel_id=1, source_target_pairs={{0,6},{1,7},{2,4},{3,5},{4,2},{5,3},{6,0},{7,1},{8,14},{9,15},{10,... | collective-permute-start | bytes 56 | tf_op jit(solution)/shard_map/ppermute | solution.py:24
  6.3 4.9 %copy-start.19 = (s32[1,4]{1,0:T(1,128)}, s32[1,4]{1,0:T(1,128)S(1)}, u32[]{:S(2)}) copy-start(s32[1,4]{1,0:T(1,128)S(1)} %collective-permute-done.refs_1_) | copy-start | bytes 52
  7.7 3.5 %copy-start.20 = (s32[1,4]{1,0:T(1,128)}, s32[1,4]{1,0:T(1,128)S(1)}, u32[]{:S(2)}) copy-start(s32[1,4]{1,0:T(1,128)S(1)} %collective-permute-done.1.refs_2_) | copy-start | bytes 52
  18.3 11.4 %collective-permute-start.4 = (bf16[128,128]{1,0:T(8,128)(2,1)}, bf16[128,128]{1,0:T(8,128)(2,1)S(1)}, u32[]{:S(2)}, u32[]{:S(2)}) collective-permute-start(bf16[128,128]{1,0:T(8,128)(2,1)} %get-tuple-element.18), channel_id=1, source_target_pairs={{0,2},{1,3},{2,0},{3,1},{4,6},{5,7},{6,4},{7,5},{8,10},{9,11},{10,... | collective-permute-start | bytes 98312 | tf_op jit(solution)/shard_map/ppermute | solution.py:24
  18.4 11.3 %collective-permute-start.5 = (bf16[128,128]{1,0:T(8,128)(2,1)}, bf16[128,128]{1,0:T(8,128)(2,1)S(1)}, u32[]{:S(2)}, u32[]{:S(2)}) collective-permute-start(bf16[128,128]{1,0:T(8,128)(2,1)} %get-tuple-element.19), channel_id=1, source_target_pairs={{0,4},{1,5},{2,6},{3,7},{4,0},{5,1},{6,2},{7,3},{8,12},{9,13},{10,... | collective-permute-start | bytes 98312 | tf_op jit(solution)/shard_map/ppermute | solution.py:24
  19.0 10.7 %collective-permute-start.6 = (bf16[128,128]{1,0:T(8,128)(2,1)}, bf16[128,128]{1,0:T(8,128)(2,1)S(1)}, u32[]{:S(2)}, u32[]{:S(2)}) collective-permute-start(bf16[128,128]{1,0:T(8,128)(2,1)} %get-tuple-element.20), channel_id=1, source_target_pairs={{0,6},{1,7},{2,4},{3,5},{4,2},{5,3},{6,0},{7,1},{8,14},{9,15},{10,... | collective-permute-start | bytes 98312 | tf_op jit(solution)/shard_map/ppermute | solution.py:24
  22.9 8.2 %copy-start.7 = (s32[4]{0:T(128)}, s32[4]{0:T(128)S(1)}, u32[]{:S(2)}) copy-start(s32[4]{0:T(128)S(1)} %pad_add_fusion.order) | copy-start | bytes 52
  27.5 7.1 %copy-start.16 = (bf16[128,128]{1,0:T(8,128)(2,1)S(1)}, bf16[128,128]{1,0:T(8,128)(2,1)}, u32[]{:S(2)}) copy-start(bf16[128,128]{1,0:T(8,128)(2,1)} %param.19) | copy-start | bytes 98308
  27.5 7.2 %copy-start.17 = (bf16[128,128]{1,0:T(8,128)(2,1)S(1)}, bf16[128,128]{1,0:T(8,128)(2,1)}, u32[]{:S(2)}) copy-start(bf16[128,128]{1,0:T(8,128)(2,1)} %param.20) | copy-start | bytes 98308
  27.5 7.3 %copy-start.18 = (bf16[128,128]{1,0:T(8,128)(2,1)S(1)}, bf16[128,128]{1,0:T(8,128)(2,1)}, u32[]{:S(2)}) copy-start(bf16[128,128]{1,0:T(8,128)(2,1)} %param.21) | copy-start | bytes 98308
  27.5 12.5 %copy-start.2 = (bf16[128,512]{1,0:T(8,128)(2,1)S(1)}, bf16[128,512]{1,0:T(8,128)(2,1)}, u32[]{:S(2)}) copy-start(bf16[128,512]{1,0:T(8,128)(2,1)} %refs_7_.1) | copy-start | bytes 393220
  27.5 12.5 %copy-start.3 = (bf16[512,128]{1,0:T(8,128)(2,1)S(1)}, bf16[512,128]{1,0:T(8,128)(2,1)}, u32[]{:S(2)}) copy-start(bf16[512,128]{1,0:T(8,128)(2,1)} %refs_8_.1) | copy-start | bytes 393220
  27.5 12.5 %copy-start.6 = (bf16[128,128]{1,0:T(8,128)(2,1)S(1)}, bf16[128,128]{1,0:T(8,128)(2,1)}, u32[]{:S(2)}) copy-start(bf16[128,128]{1,0:T(8,128)(2,1)} %refs_5_.1) | copy-start | bytes 98308
  27.5 12.5 %copy-start.9 = (f32[128]{0:T(128)S(1)}, f32[128]{0:T(128)}, u32[]{:S(2)}) copy-start(f32[128]{0:T(128)} %param.23) | copy-start | bytes 1540
  31.0 5.8 %collective-permute-start.7 = (bf16[512,128]{1,0:T(8,128)(2,1)S(1)}, bf16[512,128]{1,0:T(8,128)(2,1)S(1)}, u32[]{:S(2)}, u32[]{:S(2)}) collective-permute-start(bf16[512,128]{1,0:T(8,128)(2,1)S(1)} %get-tuple-element.22), channel_id=1, source_target_pairs={{0,8},{8,0},{16,24},{24,16},{1,9},{9,1},{17,25},{25,17},{2,10},{10... | collective-permute-start | bytes 393224 | tf_op jit(solution)/shard_map/ppermute | solution.py:24
  32.6 5.5 %collective-permute-start.8 = (bf16[512,128]{1,0:T(8,128)(2,1)S(1)}, bf16[512,128]{1,0:T(8,128)(2,1)S(1)}, u32[]{:S(2)}, u32[]{:S(2)}) collective-permute-start(bf16[512,128]{1,0:T(8,128)(2,1)S(1)} %get-tuple-element.23), channel_id=1, source_target_pairs={{0,16},{8,24},{16,0},{24,8},{1,17},{9,25},{17,1},{25,9},{2,18},{10... | collective-permute-start | bytes 393224 | tf_op jit(solution)/shard_map/ppermute | solution.py:24
  34.1 5.9 %collective-permute-start.9 = (bf16[512,128]{1,0:T(8,128)(2,1)S(1)}, bf16[512,128]{1,0:T(8,128)(2,1)S(1)}, u32[]{:S(2)}, u32[]{:S(2)}) collective-permute-start(bf16[512,128]{1,0:T(8,128)(2,1)S(1)} %get-tuple-element.24), channel_id=1, source_target_pairs={{0,24},{8,16},{16,8},{24,0},{1,25},{9,17},{17,9},{25,1},{2,26},{10... | collective-permute-start | bytes 393224 | tf_op jit(solution)/shard_map/ppermute | solution.py:24
  45.9 5.0 %collective-permute-start.10 = (bf16[512,128]{1,0:T(8,128)(2,1)S(1)}, bf16[512,128]{1,0:T(8,128)(2,1)S(1)}, u32[]{:S(2)}, u32[]{:S(2)}) collective-permute-start(bf16[512,128]{1,0:T(8,128)(2,1)S(1)} %get-tuple-element.26), channel_id=1, source_target_pairs={{0,8},{8,0},{16,24},{24,16},{1,9},{9,1},{17,25},{25,17},{2,10},{10... | collective-permute-start | bytes 393224 | tf_op jit(solution)/shard_map/ppermute | solution.py:24
  46.4 5.0 %collective-permute-start.11 = (bf16[512,128]{1,0:T(8,128)(2,1)S(1)}, bf16[512,128]{1,0:T(8,128)(2,1)S(1)}, u32[]{:S(2)}, u32[]{:S(2)}) collective-permute-start(bf16[512,128]{1,0:T(8,128)(2,1)S(1)} %get-tuple-element.27), channel_id=1, source_target_pairs={{0,16},{8,24},{16,0},{24,8},{1,17},{9,25},{17,1},{25,9},{2,18},{10... | collective-permute-start | bytes 393224 | tf_op jit(solution)/shard_map/ppermute | solution.py:24
  46.9 5.9 %collective-permute-start.12 = (bf16[512,128]{1,0:T(8,128)(2,1)S(1)}, bf16[512,128]{1,0:T(8,128)(2,1)S(1)}, u32[]{:S(2)}, u32[]{:S(2)}) collective-permute-start(bf16[512,128]{1,0:T(8,128)(2,1)S(1)} %get-tuple-element.28), channel_id=1, source_target_pairs={{0,24},{8,16},{16,8},{24,0},{1,25},{9,17},{17,9},{25,1},{2,26},{10... | collective-permute-start | bytes 393224 | tf_op jit(solution)/shard_map/ppermute | solution.py:24
  (11 other events, 12.3 us)

commit v2 on v1

--- a/solution.py
+++ b/solution.py
@@ -16,7 +16,16 @@
 SMEM = pl.BlockSpec(memory_space=pltpu.SMEM)
 VMEM = pl.BlockSpec(memory_space=pltpu.VMEM)
 ANY = pl.BlockSpec(memory_space=pl.ANY)
+HBM = pl.BlockSpec(memory_space=pltpu.HBM)
 VMEM_LIMIT = 48 * 2**20
+
+
+def hbm(*values):
+    return [pltpu.with_memory_space_constraint(v, pltpu.HBM) for v in values]
+
+
+def vmem(*values):
+    return [pltpu.with_memory_space_constraint(v, pltpu.VMEM) for v in values]
 
 
 def exchange(value, axis, mask):
@@ -32,80 +41,101 @@
     return pl.CostEstimate(flops=flops, bytes_accessed=moved, transcendentals=0)
 
 
-def cells_kernel(chunk, pairs, cell_count, place, rows, cols, count, tiles, out, total):
-    step = pl.program_id(0)
-
-    @pl.when(step == 0)
-    def _():
-        total[...] = jnp.zeros_like(total)
-
-    for i in range(chunk):
-        slot = step * chunk + i
-        cell = rows[0, slot] * pairs + (cols[0, slot] ^ place[0])
-        cell = jnp.where(slot < count[0, 0], cell, cell_count)
-        total[cell] += tiles[i].astype(F32)
-
-    @pl.when(step == pl.num_programs(0) - 1)
-    def _():
-        out[...] = total[:cell_count].astype(BF16)
-
-
-def sum_cells(place, rows, cols, count, tiles, pairs, block_count):
+def cells_kernel(chunk, pairs, cell_count, *refs):
+    rows, cols, count, tiles, out, total, held, row_list, col_list, sems = refs
+    steps = tiles.shape[0] // chunk
+    here = lax.axis_index("node") // 2
+    lists = [
+        pltpu.make_async_copy(source, target, sems.at[steps + k])
+        for k, (source, target) in enumerate(((rows, row_list), (cols, col_list)))
+    ]
+    loads = [
+        pltpu.make_async_copy(tiles.at[pl.ds(s * chunk, chunk)], held.at[s], sems.at[s]) for s in range(steps)
+    ]
+    for copy in lists + loads:
+        copy.start()
+    total[...] = jnp.zeros_like(total)
+    for copy in lists:
+        copy.wait()
+    for step, load in enumerate(loads):
+        load.wait()
+        for i in range(chunk):
+            slot = step * chunk + i
+            cell = row_list[0, slot] * pairs + (col_list[0, slot] ^ here)
+            cell = jnp.where(slot < count[0, 0], cell, cell_count)
+            total[cell] += held[step, i].astype(F32)
+    out[...] = total[:cell_count].astype(BF16)
+
+
+def sum_cells(rows, cols, count, tiles, pairs, block_count):
     slots = tiles.shape[0]
     chunk = math.gcd(slots, 16)
     cell_count = pairs * block_count
     return pl.pallas_call(
         functools.partial(cells_kernel, chunk, pairs, cell_count),
-        grid=(slots // chunk,),
-        in_specs=[SMEM] * 4 + [pl.BlockSpec((chunk, TB, TB), lambda s: (s, 0, 0))],
-        out_specs=pl.BlockSpec((cell_count, TB, TB), lambda s: (0, 0, 0)),
+        in_specs=[HBM, HBM, SMEM, HBM],
+        out_specs=VMEM,
         out_shape=jax.ShapeDtypeStruct((cell_count, TB, TB), BF16),
-        scratch_shapes=[pltpu.VMEM((cell_count + 1, TB, TB), F32)],
+        scratch_shapes=[
+            pltpu.VMEM((cell_count + 1, TB, TB), F32),
+            pltpu.VMEM((slots // chunk, chunk, TB, TB), BF16),
+            pltpu.SMEM(rows.shape, jnp.int32),
+            pltpu.SMEM(cols.shape, jnp.int32),
+            pltpu.SemaphoreType.DMA((slots // chunk + 2,)),
+        ],
         compiler_params=params(),
         cost_estimate=cost(0, tiles.size * 2),
         name="cells",
-    )(place, rows, cols, count, tiles)
-
-
-def serve_kernel(block_count, pairs, place, *refs):
-    asks, (own, other), outs, sems = refs[:pairs], refs[pairs : pairs + 2], refs[pairs + 2 : -1], refs[-1]
-    here, core = place[0], place[1]
-    for phase in (0, 1):
-        for k in range(pairs):
-            block = asks[k][0, here] - 2 * here * block_count
-            upper = (block >= block_count).astype(jnp.int32)
-            start = pl.multiple_of((block - upper * block_count) * TB, TB)
-            for source, match in ((own, upper == core), (other, upper != core)):
-
-                @pl.when(match)
-                def _():
-                    copy = pltpu.make_async_copy(source.at[pl.ds(start, TB), :], outs[k], sems.at[k])
-                    if phase == 0:
-                        copy.start()
-                    else:
-                        copy.wait()
-
-
-def serve(place, asks, own, other, block_count):
+    )(*hbm(rows, cols), count, *hbm(tiles))
+
+
+def serve_kernel(block_count, pairs, *refs):
+    asks, (own, other), outs = refs[:pairs], refs[pairs : pairs + 2], refs[pairs + 2 : 2 * pairs + 2]
+    lists, sems = refs[2 * pairs + 2 : -1], refs[-1]
+    here = lax.axis_index("node") // 2
+    core = lax.axis_index("node") % 2
+    copies = [
+        pltpu.make_async_copy(ask, target, sems.at[k]) for k, (ask, target) in enumerate(zip(asks, lists))
+    ]
+    for copy in copies:
+        copy.start()
+    for copy in copies:
+        copy.wait()
+    for k, out in enumerate(outs):
+        block = lists[k][0, here] - 2 * here * block_count
+        upper = (block >= block_count).astype(jnp.int32)
+        start = pl.multiple_of((block - upper * block_count) * TB, TB)
+
+        @pl.when(upper == core)
+        def _():
+            out[...] = own[pl.ds(start, TB), :]
+
+        @pl.when(upper != core)
+        def _():
+            out[...] = other[pl.ds(start, TB), :]
+
+
+def serve(asks, own, other, block_count):
     pairs = len(asks)
     return pl.pallas_call(
         functools.partial(serve_kernel, block_count, pairs),
-        in_specs=[SMEM] * (1 + pairs) + [ANY] * 2,
-        out_specs=[ANY] * pairs,
+        in_specs=[ANY] * pairs + [VMEM] * 2,
+        out_specs=[VMEM] * pairs,
         out_shape=[jax.ShapeDtypeStruct((TB, own.shape[1]), own.dtype)] * pairs,
-        scratch_shapes=[pltpu.SemaphoreType.DMA((pairs,))],
+        scratch_shapes=[pltpu.SMEM(asks[0].shape, jnp.int32)] * pairs + [pltpu.SemaphoreType.DMA((pairs,))],
+        compiler_params=params(),
         name="serve",
-    )(place, *asks, own, other)
-
-
-def spread_kernel(pairs, order, cells, *refs):
+    )(*asks, own, other)
+
+
+def spread_kernel(pairs, cells, *refs):
     sources, own, outs = refs[:pairs], refs[pairs], refs[pairs + 1 :]
-    feature = own.shape[1]
+    me = lax.axis_index("beh")
     stack = jnp.concatenate([s[...] for s in sources], axis=0)
     size = outs[0].shape[0]
     for k, out in enumerate(outs):
-        start = pl.multiple_of(order[k] * size, size)
-        block = order[k] * (size // TB)
+        start = pl.multiple_of((me ^ k) * size, size)
+        block = (me ^ k) * (size // TB)
         for r in range(size // TB):
             lhs = jnp.concatenate([cells[(block + r) * pairs + m] for m in range(pairs)], axis=1)
             part = jnp.dot(lhs, stack, preferred_element_type=F32)
@@ -113,16 +143,16 @@
             out[r * TB : (r + 1) * TB, :] = (part + rows).astype(BF16)
 
 
-def spread_cells(order, cells, sources, own, parts):
+def spread_cells(cells, sources, own, parts):
     size = own.shape[0] // parts
     return pl.pallas_call(
         functools.partial(spread_kernel, len(sources)),
-        in_specs=[SMEM] + [VMEM] * (len(sources) + 2),
+        in_specs=[VMEM] * (len(sources) + 2),
         out_specs=[VMEM] * parts,
         out_shape=[jax.ShapeDtypeStruct((size, own.shape[1]), BF16)] * parts,
         compiler_params=params(),
         name="spread",
-    )(order, cells, *sources, own)
+    )(cells, *sources, own)
 
 
 def merge_kernel(count, tile, *refs):
@@ -179,28 +209,29 @@
     )(*xs, w_qkv, w_out, gain, w_up, w_down)
 
 
-def place_kernel(order, *refs):
+def place_kernel(*refs):
+    me = lax.axis_index("beh")
     parts, out, sems = refs[:-2], refs[-2], refs[-1]
     size = parts[0].shape[0]
     copies = []
     for k, part in enumerate(parts):
-        start = pl.multiple_of(order[k] * size, size)
+        start = pl.multiple_of((me ^ k) * size, size)
         copies.append(pltpu.make_async_copy(part, out.at[pl.ds(start, size), :], sems.at[k]))
         copies[-1].start()
     for copy in copies:
         copy.wait()
 
 
-def place_parts(order, parts):
+def place_parts(parts):
     size, feature = parts[0].shape
     return pl.pallas_call(
         place_kernel,
-        in_specs=[SMEM] + [ANY] * len(parts),
-        out_specs=ANY,
+        in_specs=[VMEM] * len(parts),
+        out_specs=HBM,
         out_shape=jax.ShapeDtypeStruct((size * len(parts), feature), BF16),
         scratch_shapes=[pltpu.SemaphoreType.DMA((len(parts),))],
         name="place",
-    )(order, *parts)
+    )(*vmem(*parts))
 
 
 def tiles_kernel(chunk, rows, cols, count, tiles, sources, own, out, total):
@@ -290,26 +321,23 @@
     block_count = embeddings.shape[0] // TB
     tiles = adjacency[0]
     me = lax.axis_index("beh")
-    here = lax.axis_index("node")
-    order = jnp.stack([me ^ k for k in range(parts)]).astype(jnp.int32)
     if pairs * block_count <= tiles.shape[0]:
-        place = jnp.stack([here // 2, here % 2]).astype(jnp.int32)
         asks = [need_ids] + [exchange(need_ids, "node", 2 * k) for k in range(1, pairs)]
         other = exchange(embeddings, "node", 1)
-        cells = sum_cells(place, tile_rows, tile_cols, tile_count, tiles, pairs, block_count)
-        served = serve(place, asks, embeddings, other, block_count)
+        cells = sum_cells(tile_rows, tile_cols, tile_count, tiles, pairs, block_count)
+        served = serve(asks, embeddings, other, block_count)
         sources = [served[0]] + [exchange(served[k], "node", 2 * k) for k in range(1, pairs)]
-        quarters = spread_cells(order, cells, sources, embeddings, parts)
+        quarters = spread_cells(cells, sources, embeddings, parts)
     else:
         sources = fetch_many(embeddings, need_ids, block_count)
         spread = spread_tiles(tile_rows, tile_cols, tile_count, tiles, sources, embeddings)
         size = spread.shape[0] // parts
-        quarters = [lax.dynamic_slice_in_dim(spread, order[k] * size, size, 0) for k in range(parts)]
+        quarters = [lax.dynamic_slice_in_dim(spread, (me ^ k) * size, size, 0) for k in range(parts)]
     xs = [quarters[0]] + [exchange(quarters[k], "beh", k) for k in range(1, parts)]
     w_qkv = jnp.concatenate([w_query, w_key, w_value], axis=1).T
     merged = merge(xs, w_qkv, w_out, mlp_gain[None], w_up, w_down)
     back = [merged[0]] + [exchange(merged[k], "beh", k) for k in range(1, parts)]
-    return place_parts(order, back)[None]
+    return place_parts(back)[None]
 
 
 def solution(mesh):

time: 71.3 us -> 44.1 us (0.62)
  Pallas kernels: 32.1 us -> 9.89 us
  local copies, waits for them, and re-layouts: 6.99 us -> 2.08 us
    pallas_call x1, Pallas kernels: 17.7 us -> 0.82 us  [place_parts(): pl.pallas_call(place_kernel, in_specs=[VMEM] * len(parts), out_specs=HBM,...]
    pallas_call x1, Pallas kernels: 5.81 us -> 0.66 us  [serve(): pl.pallas_call(functools.partial(serve_kernel, block_count, pairs), in_sp...]
    unnamed x47 -> x23, local copies, waits for them, and re-layouts: 6.99 us -> 2.08 us
  transfers between devices with their start and end apart: 13 -> 13, of which waited for: 8 -> 8; matrix products, arithmetic and copies ran while one was open for 1% -> 1% of each run, Pallas kernels for 3% -> 6%
where the time goes in v2:
time: 44.1 us; the launch traced here: 43.9 us
  starting transfers between devices  17.2 us (39%)
  waiting for transfers between devices  13.9 us (32%)
  Pallas kernels  9.89 us (22%)
  local copies, waits for them, and re-layouts  2.08 us (5%)
  between operations  0.84 us (2%)
    ppermute x13, starting transfers between devices, exchange(): return lax.ppermute(value, axis, pairs)  17.2 us
    ppermute x13, waiting for transfers between devices, exchange(): return lax.ppermute(value, axis, pairs)  13.9 us
    pallas_call x1, Pallas kernels, merge(): pl.pallas_call(functools.partial(merge_kernel, len(xs), tile), in_specs=[...  5.2 us
    pallas_call x1, Pallas kernels, sum_cells(): pl.pallas_call(functools.partial(cells_kernel, chunk, pairs, cell_count),...  2.51 us
    unnamed x23, local copies, waits for them, and re-layouts  2.08 us
  transfers between devices with their start and end apart: 13, of which 8 were waited for; matrix products, arithmetic and copies ran while one was open for 1% of the time, Pallas kernels for 6%

profile of v2, /device:TPU:0, one launch (start us, length us, event | category | flops | bytes accessed | tf_op | source)
XLA Modules:
  0.0 43.9 jit_solution(7549927008943257494)
XLA Ops:
  0.5 2.6 %collective-permute-start = (s32[1,4]{1,0:T(1,128)}, s32[1,4]{1,0:T(1,128)S(1)}, u32[]{:S(2)}, u32[]{:S(2)}) collective-permute-start(s32[1,4]{1,0:T(1,128)} %refs_0_.3), channel_id=1, source_target_pairs={{0,2},{1,3},{2,0},{3,1},{4,6},{5,7},{6,4},{7,5},{8,10},{9,11},{10,... | collective-permute-start | bytes 56 | tf_op jit(solution)/shard_map/ppermute | solution.py:33
  3.0 2.6 %collective-permute-start.1 = (s32[1,4]{1,0:T(1,128)}, s32[1,4]{1,0:T(1,128)S(1)}, u32[]{:S(2)}, u32[]{:S(2)}) collective-permute-start(s32[1,4]{1,0:T(1,128)} %refs_0_.3), channel_id=1, source_target_pairs={{0,4},{1,5},{2,6},{3,7},{4,0},{5,1},{6,2},{7,3},{8,12},{9,13},{10,... | collective-permute-start | bytes 56 | tf_op jit(solution)/shard_map/ppermute | solution.py:33
  5.6 2.0 %collective-permute-done.1.refs_2_ = s32[1,4]{1,0:T(1,128)S(1)} collective-permute-done((s32[1,4]{1,0:T(1,128)}, s32[1,4]{1,0:T(1,128)S(1)}, u32[]{:S(2)}, u32[]{:S(2)}) %collective-permute-start.1) | collective-permute-done | bytes 48 | tf_op jit(solution)/shard_map/ppermute | solution.py:33
  7.6 3.5 %collective-permute-done.2.refs_3_ = s32[1,4]{1,0:T(1,128)S(1)} collective-permute-done((s32[1,4]{1,0:T(1,128)}, s32[1,4]{1,0:T(1,128)S(1)}, u32[]{:S(2)}, u32[]{:S(2)}) %collective-permute-start.2) | collective-permute-done | bytes 48 | tf_op jit(solution)/shard_map/ppermute | solution.py:33
  11.1 1.0 %copy-done = bf16[2048,128]{1,0:T(8,128)(2,1)S(1)} copy-done((bf16[2048,128]{1,0:T(8,128)(2,1)S(1)}, bf16[2048,128]{1,0:T(8,128)(2,1)}, u32[]{:S(2)}) %copy-start) | copy-done | bytes 524312
  12.1 0.7 %copy-done.5 = s32[1,4]{1,0:T(1,128)S(1)} copy-done((s32[1,4]{1,0:T(1,128)S(1)}, s32[1,4]{1,0:T(1,128)}, u32[]{:S(2)}) %copy-start.5) | copy-done | bytes 40
  12.8 0.7 %serve.1 = (bf16[128,128]{1,0:T(8,128)(2,1)S(1)}, bf16[128,128]{1,0:T(8,128)(2,1)S(1)}, bf16[128,128]{1,0:T(8,128)(2,1)S(1)}, bf16[128,128]{1,0:T(8,128)(2,1)S(1)}) custom-call(s32[1,4]{1,0:T(1,128)S(1)} %copy-done.5, s32[1,4]{1,0:T(1,128)S(1)} %collective-permute-done.refs_1_, s32[1,4]{1,0:T(1,128)S(1)} %collective-permute-done.1.refs_2_, ...), custom_call_target="tpu_custom_call" | custom-call | tf_op jit(solution)/shard_map/serve/pallas_call | solution.py:120
  13.5 0.6 %collective-permute-start.5 = (bf16[128,128]{1,0:T(8,128)(2,1)S(1)}, bf16[128,128]{1,0:T(8,128)(2,1)S(1)}, u32[]{:S(2)}, u32[]{:S(2)}) collective-permute-start(bf16[128,128]{1,0:T(8,128)(2,1)S(1)} %get-tuple-element.19), channel_id=1, source_target_pairs={{0,4},{1,5},{2,6},{3,7},{4,0},{5,1},{6,2},{7,3},{8,12},{9,13},{10,... | collective-permute-start | bytes 98312 | tf_op jit(solution)/shard_map/ppermute | solution.py:33
  14.1 3.8 %collective-permute-start.6 = (bf16[128,128]{1,0:T(8,128)(2,1)S(1)}, bf16[128,128]{1,0:T(8,128)(2,1)S(1)}, u32[]{:S(2)}, u32[]{:S(2)}) collective-permute-start(bf16[128,128]{1,0:T(8,128)(2,1)S(1)} %get-tuple-element.20), channel_id=1, source_target_pairs={{0,6},{1,7},{2,4},{3,5},{4,2},{5,3},{6,0},{7,1},{8,14},{9,15},{10,... | collective-permute-start | bytes 98312 | tf_op jit(solution)/shard_map/ppermute | solution.py:33
  18.7 2.5 %cells.1 = bf16[64,128,128]{2,1,0:T(8,128)(2,1)S(1)} custom-call(s32[1,112]{1,0:T(1,128)} %refs_0_.2, s32[1,112]{1,0:T(1,128)} %refs_1_.1, s32[1,1]{1,0:T(1,128)S(6)} %copy.17.refs_2_, bf16[112,128,128]{2,1,0:T(8,128)(2,1)} %bitcast.6), custom_call_target="tpu_custom_call" | custom-call | bytes 3670016 | tf_op jit(solution)/shard_map/cells/pallas_call | solution.py:74
  21.2 0.7 %spread.1 = (bf16[512,128]{1,0:T(8,128)(2,1)S(1)}, bf16[512,128]{1,0:T(8,128)(2,1)S(1)}, bf16[512,128]{1,0:T(8,128)(2,1)S(1)}, bf16[512,128]{1,0:T(8,128)(2,1)S(1)}) custom-call(bf16[64,128,128]{2,1,0:T(8,128)(2,1)S(1)} %cells.1, bf16[128,128]{1,0:T(8,128)(2,1)S(1)} %get-tuple-element.17.refs_0_, bf16[128,128]{1,0:T(8,128)(2,1)S(1)} %collective-permute-done.4.refs_1_, ...), custom_call_target="tpu_custom_call" | custom-call | tf_op jit(solution)/shard_map/spread/pallas_call | solution.py:148
  21.9 1.6 %collective-permute-start.7 = (bf16[512,128]{1,0:T(8,128)(2,1)S(1)}, bf16[512,128]{1,0:T(8,128)(2,1)S(1)}, u32[]{:S(2)}, u32[]{:S(2)}) collective-permute-start(bf16[512,128]{1,0:T(8,128)(2,1)S(1)} %get-tuple-element.22), channel_id=1, source_target_pairs={{0,8},{8,0},{16,24},{24,16},{1,9},{9,1},{17,25},{25,17},{2,10},{10... | collective-permute-start | bytes 393224 | tf_op jit(solution)/shard_map/ppermute | solution.py:33
  23.5 1.5 %collective-permute-start.8 = (bf16[512,128]{1,0:T(8,128)(2,1)S(1)}, bf16[512,128]{1,0:T(8,128)(2,1)S(1)}, u32[]{:S(2)}, u32[]{:S(2)}) collective-permute-start(bf16[512,128]{1,0:T(8,128)(2,1)S(1)} %get-tuple-element.23), channel_id=1, source_target_pairs={{0,16},{8,24},{16,0},{24,8},{1,17},{9,25},{17,1},{25,9},{2,18},{10... | collective-permute-start | bytes 393224 | tf_op jit(solution)/shard_map/ppermute | solution.py:33
  25.9 1.9 %collective-permute-done.7.refs_1_ = bf16[512,128]{1,0:T(8,128)(2,1)S(1)} collective-permute-done((bf16[512,128]{1,0:T(8,128)(2,1)S(1)}, bf16[512,128]{1,0:T(8,128)(2,1)S(1)}, u32[]{:S(2)}, u32[]{:S(2)}) %collective-permute-start.7) | collective-permute-done | bytes 131104 | tf_op jit(solution)/shard_map/ppermute | solution.py:33
  27.7 1.3 %collective-permute-done.8.refs_2_ = bf16[512,128]{1,0:T(8,128)(2,1)S(1)} collective-permute-done((bf16[512,128]{1,0:T(8,128)(2,1)S(1)}, bf16[512,128]{1,0:T(8,128)(2,1)S(1)}, u32[]{:S(2)}, u32[]{:S(2)}) %collective-permute-start.8) | collective-permute-done | bytes 131104 | tf_op jit(solution)/shard_map/ppermute | solution.py:33
  29.0 1.9 %collective-permute-done.9.refs_3_ = bf16[512,128]{1,0:T(8,128)(2,1)S(1)} collective-permute-done((bf16[512,128]{1,0:T(8,128)(2,1)S(1)}, bf16[512,128]{1,0:T(8,128)(2,1)S(1)}, u32[]{:S(2)}, u32[]{:S(2)}) %collective-permute-start.9) | collective-permute-done | bytes 131104 | tf_op jit(solution)/shard_map/ppermute | solution.py:33
  30.9 5.2 %merge.1 = (bf16[512,128]{1,0:T(8,128)(2,1)S(1)}, bf16[512,128]{1,0:T(8,128)(2,1)S(1)}, bf16[512,128]{1,0:T(8,128)(2,1)S(1)}, bf16[512,128]{1,0:T(8,128)(2,1)S(1)}) custom-call(bf16[512,128]{1,0:T(8,128)(2,1)S(1)} %get-tuple-element.21.refs_0_, bf16[512,128]{1,0:T(8,128)(2,1)S(1)} %collective-permute-done.7.refs_1_, ...), custom_call_target="tpu_custom_call" | custom-call | tf_op jit(solution)/shard_map/merge/pallas_call | solution.py:202
  36.1 0.6 %collective-permute-start.10 = (bf16[512,128]{1,0:T(8,128)(2,1)S(1)}, bf16[512,128]{1,0:T(8,128)(2,1)S(1)}, u32[]{:S(2)}, u32[]{:S(2)}) collective-permute-start(bf16[512,128]{1,0:T(8,128)(2,1)S(1)} %get-tuple-element.26), channel_id=1, source_target_pairs={{0,8},{8,0},{16,24},{24,16},{1,9},{9,1},{17,25},{25,17},{2,10},{10... | collective-permute-start | bytes 393224 | tf_op jit(solution)/shard_map/ppermute | solution.py:33
  36.7 0.5 %collective-permute-start.11 = (bf16[512,128]{1,0:T(8,128)(2,1)S(1)}, bf16[512,128]{1,0:T(8,128)(2,1)S(1)}, u32[]{:S(2)}, u32[]{:S(2)}) collective-permute-start(bf16[512,128]{1,0:T(8,128)(2,1)S(1)} %get-tuple-element.27), channel_id=1, source_target_pairs={{0,16},{8,24},{16,0},{24,8},{1,17},{9,25},{17,1},{25,9},{2,18},{10... | collective-permute-start | bytes 393224 | tf_op jit(solution)/shard_map/ppermute | solution.py:33
  37.2 2.4 %collective-permute-start.12 = (bf16[512,128]{1,0:T(8,128)(2,1)S(1)}, bf16[512,128]{1,0:T(8,128)(2,1)S(1)}, u32[]{:S(2)}, u32[]{:S(2)}) collective-permute-start(bf16[512,128]{1,0:T(8,128)(2,1)S(1)} %get-tuple-element.28), channel_id=1, source_target_pairs={{0,24},{8,16},{16,8},{24,0},{1,25},{9,17},{17,9},{25,1},{2,26},{10... | collective-permute-start | bytes 393224 | tf_op jit(solution)/shard_map/ppermute | solution.py:33
  39.6 1.5 %collective-permute-done.10.refs_1_ = bf16[512,128]{1,0:T(8,128)(2,1)S(1)} collective-permute-done((bf16[512,128]{1,0:T(8,128)(2,1)S(1)}, bf16[512,128]{1,0:T(8,128)(2,1)S(1)}, u32[]{:S(2)}, u32[]{:S(2)}) %collective-permute-start.10) | collective-permute-done | bytes 131104 | tf_op jit(solution)/shard_map/ppermute | solution.py:33
  41.1 0.5 %collective-permute-done.11.refs_2_ = bf16[512,128]{1,0:T(8,128)(2,1)S(1)} collective-permute-done((bf16[512,128]{1,0:T(8,128)(2,1)S(1)}, bf16[512,128]{1,0:T(8,128)(2,1)S(1)}, u32[]{:S(2)}, u32[]{:S(2)}) %collective-permute-start.11) | collective-permute-done | bytes 131104 | tf_op jit(solution)/shard_map/ppermute | solution.py:33
  41.7 1.4 %collective-permute-done.12.refs_3_ = bf16[512,128]{1,0:T(8,128)(2,1)S(1)} collective-permute-done((bf16[512,128]{1,0:T(8,128)(2,1)S(1)}, bf16[512,128]{1,0:T(8,128)(2,1)S(1)}, u32[]{:S(2)}, u32[]{:S(2)}) %collective-permute-start.12) | collective-permute-done | bytes 131104 | tf_op jit(solution)/shard_map/ppermute | solution.py:33
  43.1 0.8 %place.1 = bf16[2048,128]{1,0:T(8,128)(2,1)} custom-call(bf16[512,128]{1,0:T(8,128)(2,1)S(1)} %get-tuple-element.25.refs_0_, bf16[512,128]{1,0:T(8,128)(2,1)S(1)} %collective-permute-done.10.refs_1_, bf16[512,128]{1,0:T(8,128)(2,1)S(1)} %collective-permute-done.11.refs_2_, bf16[512,128]{1,0:T(8,128)(2,1)S(1)} %collective-permute-done.12.refs_3_), custom_call_target="tpu_custom_call" | custom-call | tf_op jit(solution)/shard_map/place/pallas_call | solution.py:227
  (31 shorter events, 1.4 us)
Async XLA Ops:
  0.0 11.1 %collective-permute-start.3 = (bf16[2048,128]{1,0:T(8,128)(2,1)}, bf16[2048,128]{1,0:T(8,128)(2,1)S(1)}, u32[]{:S(2)}, u32[]{:S(2)}) collective-permute-start(bf16[2048,128]{1,0:T(8,128)(2,1)} %refs_4_.3), channel_id=1, source_target_pairs={{0,1},{1,0},{2,3},{3,2},{4,5},{5,4},{6,7},{7,6},{8,9},{9,8},{10,11... | collective-permute-start | bytes 1572872 | tf_op jit(solution)/shard_map/ppermute | solution.py:33
  0.5 5.2 %collective-permute-start = (s32[1,4]{1,0:T(1,128)}, s32[1,4]{1,0:T(1,128)S(1)}, u32[]{:S(2)}, u32[]{:S(2)}) collective-permute-start(s32[1,4]{1,0:T(1,128)} %refs_0_.3), channel_id=1, source_target_pairs={{0,2},{1,3},{2,0},{3,1},{4,6},{5,7},{6,4},{7,5},{8,10},{9,11},{10,... | collective-permute-start | bytes 56 | tf_op jit(solution)/shard_map/ppermute | solution.py:33
  3.0 4.6 %collective-permute-start.1 = (s32[1,4]{1,0:T(1,128)}, s32[1,4]{1,0:T(1,128)S(1)}, u32[]{:S(2)}, u32[]{:S(2)}) collective-permute-start(s32[1,4]{1,0:T(1,128)} %refs_0_.3), channel_id=1, source_target_pairs={{0,4},{1,5},{2,6},{3,7},{4,0},{5,1},{6,2},{7,3},{8,12},{9,13},{10,... | collective-permute-start | bytes 56 | tf_op jit(solution)/shard_map/ppermute | solution.py:33
  5.6 5.5 %collective-permute-start.2 = (s32[1,4]{1,0:T(1,128)}, s32[1,4]{1,0:T(1,128)S(1)}, u32[]{:S(2)}, u32[]{:S(2)}) collective-permute-start(s32[1,4]{1,0:T(1,128)} %refs_0_.3), channel_id=1, source_target_pairs={{0,6},{1,7},{2,4},{3,5},{4,2},{5,3},{6,0},{7,1},{8,14},{9,15},{10,... | collective-permute-start | bytes 56 | tf_op jit(solution)/shard_map/ppermute | solution.py:33
  11.1 1.0 %copy-start = (bf16[2048,128]{1,0:T(8,128)(2,1)S(1)}, bf16[2048,128]{1,0:T(8,128)(2,1)}, u32[]{:S(2)}) copy-start(bf16[2048,128]{1,0:T(8,128)(2,1)} %refs_4_.3) | copy-start | bytes 1572868
  12.1 0.7 %copy-start.5 = (s32[1,4]{1,0:T(1,128)S(1)}, s32[1,4]{1,0:T(1,128)}, u32[]{:S(2)}) copy-start(s32[1,4]{1,0:T(1,128)} %refs_0_.3) | copy-start | bytes 52
  12.8 8.4 %copy-start.1 = (bf16[2048,128]{1,0:T(8,128)(2,1)S(1)}, bf16[2048,128]{1,0:T(8,128)(2,1)}, u32[]{:S(2)}) copy-start(bf16[2048,128]{1,0:T(8,128)(2,1)} %refs_4_.3) | copy-start | bytes 1572868
  13.5 7.7 %collective-permute-start.4 = (bf16[128,128]{1,0:T(8,128)(2,1)S(1)}, bf16[128,128]{1,0:T(8,128)(2,1)S(1)}, u32[]{:S(2)}, u32[]{:S(2)}) collective-permute-start(bf16[128,128]{1,0:T(8,128)(2,1)S(1)} %get-tuple-element.18), channel_id=1, source_target_pairs={{0,2},{1,3},{2,0},{3,1},{4,6},{5,7},{6,4},{7,5},{8,10},{9,11},{10,... | collective-permute-start | bytes 98312 | tf_op jit(solution)/shard_map/ppermute | solution.py:33
  13.5 7.6 %collective-permute-start.5 = (bf16[128,128]{1,0:T(8,128)(2,1)S(1)}, bf16[128,128]{1,0:T(8,128)(2,1)S(1)}, u32[]{:S(2)}, u32[]{:S(2)}) collective-permute-start(bf16[128,128]{1,0:T(8,128)(2,1)S(1)} %get-tuple-element.19), channel_id=1, source_target_pairs={{0,4},{1,5},{2,6},{3,7},{4,0},{5,1},{6,2},{7,3},{8,12},{9,13},{10,... | collective-permute-start | bytes 98312 | tf_op jit(solution)/shard_map/ppermute | solution.py:33
  14.1 7.1 %collective-permute-start.6 = (bf16[128,128]{1,0:T(8,128)(2,1)S(1)}, bf16[128,128]{1,0:T(8,128)(2,1)S(1)}, u32[]{:S(2)}, u32[]{:S(2)}) collective-permute-start(bf16[128,128]{1,0:T(8,128)(2,1)S(1)} %get-tuple-element.20), channel_id=1, source_target_pairs={{0,6},{1,7},{2,4},{3,5},{4,2},{5,3},{6,0},{7,1},{8,14},{9,15},{10,... | collective-permute-start | bytes 98312 | tf_op jit(solution)/shard_map/ppermute | solution.py:33
  18.6 6.9 %copy-start.7 = (bf16[128,128]{1,0:T(8,128)(2,1)S(1)}, bf16[128,128]{1,0:T(8,128)(2,1)}, u32[]{:S(2)}) copy-start(bf16[128,128]{1,0:T(8,128)(2,1)} %param.19) | copy-start | bytes 98308
  18.6 7.0 %copy-start.8 = (bf16[128,128]{1,0:T(8,128)(2,1)S(1)}, bf16[128,128]{1,0:T(8,128)(2,1)}, u32[]{:S(2)}) copy-start(bf16[128,128]{1,0:T(8,128)(2,1)} %param.20) | copy-start | bytes 98308
  18.6 7.1 %copy-start.9 = (bf16[128,128]{1,0:T(8,128)(2,1)S(1)}, bf16[128,128]{1,0:T(8,128)(2,1)}, u32[]{:S(2)}) copy-start(bf16[128,128]{1,0:T(8,128)(2,1)} %param.21) | copy-start | bytes 98308
  18.6 12.3 %copy-start.2 = (bf16[128,512]{1,0:T(8,128)(2,1)S(1)}, bf16[128,512]{1,0:T(8,128)(2,1)}, u32[]{:S(2)}) copy-start(bf16[128,512]{1,0:T(8,128)(2,1)} %refs_7_.1) | copy-start | bytes 393220
  18.6 12.3 %copy-start.3 = (bf16[512,128]{1,0:T(8,128)(2,1)S(1)}, bf16[512,128]{1,0:T(8,128)(2,1)}, u32[]{:S(2)}) copy-start(bf16[512,128]{1,0:T(8,128)(2,1)} %refs_8_.1) | copy-start | bytes 393220
  18.6 12.2 %copy-start.4 = (bf16[128,128]{1,0:T(8,128)(2,1)S(1)}, bf16[128,128]{1,0:T(8,128)(2,1)}, u32[]{:S(2)}) copy-start(bf16[128,128]{1,0:T(8,128)(2,1)} %refs_5_.1) | copy-start | bytes 98308
  18.6 12.2 %copy-start.6 = (f32[128]{0:T(128)S(1)}, f32[128]{0:T(128)}, u32[]{:S(2)}) copy-start(f32[128]{0:T(128)} %param.23) | copy-start | bytes 1540
  21.9 5.8 %collective-permute-start.7 = (bf16[512,128]{1,0:T(8,128)(2,1)S(1)}, bf16[512,128]{1,0:T(8,128)(2,1)S(1)}, u32[]{:S(2)}, u32[]{:S(2)}) collective-permute-start(bf16[512,128]{1,0:T(8,128)(2,1)S(1)} %get-tuple-element.22), channel_id=1, source_target_pairs={{0,8},{8,0},{16,24},{24,16},{1,9},{9,1},{17,25},{25,17},{2,10},{10... | collective-permute-start | bytes 393224 | tf_op jit(solution)/shard_map/ppermute | solution.py:33
  23.5 5.5 %collective-permute-start.8 = (bf16[512,128]{1,0:T(8,128)(2,1)S(1)}, bf16[512,128]{1,0:T(8,128)(2,1)S(1)}, u32[]{:S(2)}, u32[]{:S(2)}) collective-permute-start(bf16[512,128]{1,0:T(8,128)(2,1)S(1)} %get-tuple-element.23), channel_id=1, source_target_pairs={{0,16},{8,24},{16,0},{24,8},{1,17},{9,25},{17,1},{25,9},{2,18},{10... | collective-permute-start | bytes 393224 | tf_op jit(solution)/shard_map/ppermute | solution.py:33
  25.0 5.9 %collective-permute-start.9 = (bf16[512,128]{1,0:T(8,128)(2,1)S(1)}, bf16[512,128]{1,0:T(8,128)(2,1)S(1)}, u32[]{:S(2)}, u32[]{:S(2)}) collective-permute-start(bf16[512,128]{1,0:T(8,128)(2,1)S(1)} %get-tuple-element.24), channel_id=1, source_target_pairs={{0,24},{8,16},{16,8},{24,0},{1,25},{9,17},{17,9},{25,1},{2,26},{10... | collective-permute-start | bytes 393224 | tf_op jit(solution)/shard_map/ppermute | solution.py:33
  36.1 5.0 %collective-permute-start.10 = (bf16[512,128]{1,0:T(8,128)(2,1)S(1)}, bf16[512,128]{1,0:T(8,128)(2,1)S(1)}, u32[]{:S(2)}, u32[]{:S(2)}) collective-permute-start(bf16[512,128]{1,0:T(8,128)(2,1)S(1)} %get-tuple-element.26), channel_id=1, source_target_pairs={{0,8},{8,0},{16,24},{24,16},{1,9},{9,1},{17,25},{25,17},{2,10},{10... | collective-permute-start | bytes 393224 | tf_op jit(solution)/shard_map/ppermute | solution.py:33
  36.7 5.0 %collective-permute-start.11 = (bf16[512,128]{1,0:T(8,128)(2,1)S(1)}, bf16[512,128]{1,0:T(8,128)(2,1)S(1)}, u32[]{:S(2)}, u32[]{:S(2)}) collective-permute-start(bf16[512,128]{1,0:T(8,128)(2,1)S(1)} %get-tuple-element.27), channel_id=1, source_target_pairs={{0,16},{8,24},{16,0},{24,8},{1,17},{9,25},{17,1},{25,9},{2,18},{10... | collective-permute-start | bytes 393224 | tf_op jit(solution)/shard_map/ppermute | solution.py:33
  37.2 5.9 %collective-permute-start.12 = (bf16[512,128]{1,0:T(8,128)(2,1)S(1)}, bf16[512,128]{1,0:T(8,128)(2,1)S(1)}, u32[]{:S(2)}, u32[]{:S(2)}) collective-permute-start(bf16[512,128]{1,0:T(8,128)(2,1)S(1)} %get-tuple-element.28), channel_id=1, source_target_pairs={{0,24},{8,16},{16,8},{24,0},{1,25},{9,17},{17,9},{25,1},{2,26},{10... | collective-permute-start | bytes 393224 | tf_op jit(solution)/shard_map/ppermute | solution.py:33

commit v3 on v2

--- a/solution.py
+++ b/solution.py
@@ -31,6 +31,24 @@
 def exchange(value, axis, mask):
     pairs = [(source, source ^ mask) for source in range(lax.axis_size(axis))]
     return lax.ppermute(value, axis, pairs)
+
+
+def beh_masks(parts):
+    first, *rest = range(parts - 1, 0, -1)
+    return [(0, 0), (first, first)] + list(zip(rest[::-1], rest))
+
+
+def exchange_beh(value, masks):
+    peers = lax.axis_size("node")
+    pairs = [
+        (b * peers + n, (b ^ masks[n % 2]) * peers + n) for b in range(lax.axis_size("beh")) for n in range(peers)
+    ]
+    return lax.ppermute(value, ("beh", "node"), pairs)
+
+
+def part_of(k, parts):
+    even, odd = beh_masks(parts)[k]
+    return lax.axis_index("beh") ^ jnp.where(lax.axis_index("node") % 2 == 0, even, odd)
 
 
 def params(**more):
@@ -89,6 +107,25 @@
     )(*hbm(rows, cols), count, *hbm(tiles))
 
 
+def load_kernel(source, out, sem):
+    copy = pltpu.make_async_copy(source, out, sem)
+    copy.start()
+    copy.wait()
+
+
+def load(source):
+    return pl.pallas_call(
+        load_kernel,
+        in_specs=[HBM],
+        out_specs=VMEM,
+        out_shape=jax.ShapeDtypeStruct(source.shape, source.dtype),
+        scratch_shapes=[pltpu.SemaphoreType.DMA],
+        compiler_params=params(),
+        cost_estimate=cost(0, source.size * 2),
+        name="load",
+    )(*hbm(source))
+
+
 def serve_kernel(block_count, pairs, *refs):
     asks, (own, other), outs = refs[:pairs], refs[pairs : pairs + 2], refs[pairs + 2 : 2 * pairs + 2]
     lists, sems = refs[2 * pairs + 2 : -1], refs[-1]
@@ -130,17 +167,17 @@
 
 def spread_kernel(pairs, cells, *refs):
     sources, own, outs = refs[:pairs], refs[pairs], refs[pairs + 1 :]
-    me = lax.axis_index("beh")
     stack = jnp.concatenate([s[...] for s in sources], axis=0)
     size = outs[0].shape[0]
     for k, out in enumerate(outs):
-        start = pl.multiple_of((me ^ k) * size, size)
-        block = (me ^ k) * (size // TB)
+        part = part_of(k, len(outs))
+        start = pl.multiple_of(part * size, size)
+        block = part * (size // TB)
         for r in range(size // TB):
             lhs = jnp.concatenate([cells[(block + r) * pairs + m] for m in range(pairs)], axis=1)
-            part = jnp.dot(lhs, stack, preferred_element_type=F32)
+            total = jnp.dot(lhs, stack, preferred_element_type=F32)
             rows = own[pl.ds(start + r * TB, TB), :].astype(F32)
-            out[r * TB : (r + 1) * TB, :] = (part + rows).astype(BF16)
+            out[r * TB : (r + 1) * TB, :] = (total + rows).astype(BF16)
 
 
 def spread_cells(cells, sources, own, parts):
@@ -155,67 +192,80 @@
     )(cells, *sources, own)
 
 
-def merge_kernel(count, tile, *refs):
-    xs = refs[:count]
-    w_qkv, w_out, gain, w_up, w_down = refs[count : count + 5]
-    outs = refs[count + 5 :]
+def project_kernel(w_qkv, x, out):
+    feature = x.shape[1]
+    full = lax.dot_general(w_qkv[...], x[...], (((1,), (1,)), ((), ())), preferred_element_type=F32)
+    scale = math.log2(math.e) / math.sqrt(HEAD)
+    out[:feature] = full[:feature] * scale
+    out[feature:] = full[feature:]
+
+
+def project(w_qkv, x):
+    return pl.pallas_call(
+        project_kernel,
+        in_specs=[VMEM] * 2,
+        out_specs=VMEM,
+        out_shape=jax.ShapeDtypeStruct((w_qkv.shape[0], x.shape[0]), F32),
+        compiler_params=params(),
+        cost_estimate=cost(2 * w_qkv.size * x.shape[0], w_qkv.size),
+        name="project",
+    )(w_qkv, x)
+
+
+def merge_kernel(count, which, tile, *refs):
+    x = refs[0]
+    projected = refs[1 : count + 1]
+    w_out, gain, w_up, w_down, out = refs[count + 1 :]
     feature = w_out.shape[0]
-    scale = math.log2(math.e) / math.sqrt(HEAD)
-
-    def body(step, carry):
-        start = pl.multiple_of(step * tile, tile)
-        rows = pl.ds(start, tile)
-        queries, keys, values = [], [], []
-        for x in xs:
-            full = lax.dot_general(
-                w_qkv[...], x[rows, :], (((1,), (1,)), ((), ())), preferred_element_type=F32
-            )
-            queries.append(full[:feature].reshape(HEADS, HEAD, tile) * scale)
-            keys.append(full[feature : 2 * feature].reshape(HEADS, HEAD, tile))
-            values.append(full[2 * feature :].reshape(HEADS, HEAD, tile))
-        for x, query, out in zip(xs, queries, outs):
-            scores = [jnp.sum(query * key, axis=1, keepdims=True) for key in keys]
-            top = functools.reduce(jnp.maximum, scores)
-            weights = [jnp.exp2(s - top) for s in scores]
-            inverse = 1.0 / functools.reduce(jnp.add, weights)
-            mixture = functools.reduce(
-                jnp.add, [(w * inverse) * value for w, value in zip(weights, values)]
-            )
-            mixture = mixture.reshape(feature, tile).astype(BF16)
-            residual = x[rows, :].astype(F32) + lax.dot_general(
-                mixture, w_out[...], (((0,), (0,)), ((), ())), preferred_element_type=F32
-            )
-            meansq = jnp.mean(residual * residual, axis=-1, keepdims=True)
-            normed = (residual * lax.rsqrt(meansq + 1e-06) * gain[...]).astype(BF16)
-            half = 0.5 * jnp.dot(normed, w_up[...], preferred_element_type=F32)
-            hidden = (half + half * jnp.tanh(half)).astype(BF16)
-            result = residual + jnp.dot(hidden, w_down[...], preferred_element_type=F32)
-            out[rows, :] = result.astype(BF16)
-        return carry
-
-    lax.fori_loop(0, xs[0].shape[0] // tile, body, 0)
-
-
-def merge(xs, w_qkv, w_out, gain, w_up, w_down):
-    size, feature = xs[0].shape
-    tile = math.gcd(size, 256)
-    return pl.pallas_call(
-        functools.partial(merge_kernel, len(xs), tile),
-        in_specs=[VMEM] * (len(xs) + 5),
-        out_specs=[VMEM] * len(xs),
-        out_shape=[jax.ShapeDtypeStruct((size, feature), BF16)] * len(xs),
-        compiler_params=params(),
+    for step in range(x.shape[0] // tile):
+        rows = pl.ds(step * tile, tile)
+        query = projected[which][:feature, rows].reshape(HEADS, HEAD, tile)
+        scores = [
+            jnp.sum(query * p[feature : 2 * feature, rows].reshape(HEADS, HEAD, tile), axis=1, keepdims=True)
+            for p in projected
+        ]
+        top = functools.reduce(jnp.maximum, scores)
+        weights = [jnp.exp2(s - top) for s in scores]
+        inverse = 1.0 / functools.reduce(jnp.add, weights)
+        mixture = functools.reduce(
+            jnp.add,
+            [
+                (w * inverse) * p[2 * feature :, rows].reshape(HEADS, HEAD, tile)
+                for w, p in zip(weights, projected)
+            ],
+        )
+        mixture = mixture.reshape(feature, tile).astype(BF16)
+        residual = x[rows, :].astype(F32) + lax.dot_general(
+            mixture, w_out[...], (((0,), (0,)), ((), ())), preferred_element_type=F32
+        )
+        meansq = jnp.mean(residual * residual, axis=-1, keepdims=True)
+        normed = (residual * lax.rsqrt(meansq + 1e-06) * gain[...]).astype(BF16)
+        half = 0.5 * jnp.dot(normed, w_up[...], preferred_element_type=F32)
+        hidden = (half + half * jnp.tanh(half)).astype(BF16)
+        result = residual + jnp.dot(hidden, w_down[...], preferred_element_type=F32)
+        out[rows, :] = result.astype(BF16)
+
+
+def merge(x, projected, which, w_out, gain, w_up, w_down):
+    size, feature = x.shape
+    tile = math.gcd(size, 512)
+    return pl.pallas_call(
+        functools.partial(merge_kernel, len(projected), which, tile),
+        in_specs=[VMEM] * (len(projected) + 5),
+        out_specs=VMEM,
+        out_shape=jax.ShapeDtypeStruct((size, feature), BF16),
+        compiler_params=params(),
+        cost_estimate=cost(8 * size * w_up.size, w_up.size),
         name="merge",
-    )(*xs, w_qkv, w_out, gain, w_up, w_down)
+    )(x, *projected, w_out, gain, w_up, w_down)
 
 
 def place_kernel(*refs):
-    me = lax.axis_index("beh")
     parts, out, sems = refs[:-2], refs[-2], refs[-1]
     size = parts[0].shape[0]
     copies = []
     for k, part in enumerate(parts):
-        start = pl.multiple_of((me ^ k) * size, size)
+        start = pl.multiple_of(part_of(k, len(parts)) * size, size)
         copies.append(pltpu.make_async_copy(part, out.at[pl.ds(start, size), :], sems.at[k]))
         copies[-1].start()
     for copy in copies:
@@ -320,23 +370,27 @@
     pairs = lax.axis_size("node") // 2
     block_count = embeddings.shape[0] // TB
     tiles = adjacency[0]
-    me = lax.axis_index("beh")
     if pairs * block_count <= tiles.shape[0]:
-        asks = [need_ids] + [exchange(need_ids, "node", 2 * k) for k in range(1, pairs)]
+        far = range(pairs - 1, 0, -1)
+        asks = [exchange(need_ids, "node", 2 * k) for k in far] + hbm(need_ids)
         other = exchange(embeddings, "node", 1)
+        own = load(embeddings)
         cells = sum_cells(tile_rows, tile_cols, tile_count, tiles, pairs, block_count)
-        served = serve(asks, embeddings, other, block_count)
-        sources = [served[0]] + [exchange(served[k], "node", 2 * k) for k in range(1, pairs)]
-        quarters = spread_cells(cells, sources, embeddings, parts)
+        served = serve(asks[:1], own, other, block_count)
+        *more, here = serve(asks[1:], own, other, block_count)
+        sources = [here] + [exchange(block, "node", 2 * k) for k, block in zip(far, [*served, *more])][::-1]
+        quarters = spread_cells(cells, sources, own, parts)
     else:
         sources = fetch_many(embeddings, need_ids, block_count)
         spread = spread_tiles(tile_rows, tile_cols, tile_count, tiles, sources, embeddings)
         size = spread.shape[0] // parts
-        quarters = [lax.dynamic_slice_in_dim(spread, (me ^ k) * size, size, 0) for k in range(parts)]
-    xs = [quarters[0]] + [exchange(quarters[k], "beh", k) for k in range(1, parts)]
+        quarters = [lax.dynamic_slice_in_dim(spread, part_of(k, parts) * size, size, 0) for k in range(parts)]
+    masks = beh_masks(parts)
+    xs = [quarters[0]] + [exchange_beh(quarters[k], masks[k]) for k in range(1, parts)]
     w_qkv = jnp.concatenate([w_query, w_key, w_value], axis=1).T
-    merged = merge(xs, w_qkv, w_out, mlp_gain[None], w_up, w_down)
-    back = [merged[0]] + [exchange(merged[k], "beh", k) for k in range(1, parts)]
+    projected = [project(w_qkv, x) for x in xs]
+    merged = [merge(xs[k], projected, k, w_out, mlp_gain[None], w_up, w_down) for k in range(parts)]
+    back = [merged[0]] + [exchange_beh(merged[k], masks[k]) for k in range(1, parts)]
     return place_parts(back)[None]
 
 

time: 44.1 us -> 39 us (0.88)
  waiting for transfers between devices: 13.9 us -> 9.29 us
  local copies, waits for them, and re-layouts: 2.08 us -> 0.38 us
  Pallas kernels: 9.89 us -> 10.9 us
    ppermute x13 -> x7, waiting for transfers between devices: 13.9 us -> 2.55 us  [exchange(): return lax.ppermute(value, axis, pairs)]
    ppermute x0 -> x6, starting transfers between devices: none -> 7.24 us  [exchange_beh(): return lax.ppermute(value, ('beh', 'node'), pairs)]
    ppermute x13 -> x7, starting transfers between devices: 17.2 us -> 10.1 us  [exchange(): return lax.ppermute(value, axis, pairs)]
    ppermute x0 -> x6, waiting for transfers between devices: none -> 6.75 us  [exchange_beh(): return lax.ppermute(value, ('beh', 'node'), pairs)]
    unnamed x23 -> x17, local copies, waits for them, and re-layouts: 2.08 us -> 0.38 us
    pallas_call x1 -> x2, Pallas kernels: 0.66 us -> 1.32 us  [serve(): pl.pallas_call(functools.partial(serve_kernel, block_count, pairs), in_sp...]
    pallas_call x1 -> x9, Pallas kernels: 5.2 us -> 5.62 us  [the longest x4 3.54 us: merge(): pl.pallas_call(functools.partial(merge_kernel, len(projected), which, til...]
  transfers between devices with their start and end apart: 13 -> 13, of which waited for: 8 -> 6; matrix products, arithmetic and copies ran while one was open for 1% -> 1% of each run, Pallas kernels for 6% -> 21%
where the time goes in v3:
time: 39 us; the launch traced here: 38.8 us
  starting transfers between devices  17.4 us (45%)
  Pallas kernels  10.9 us (28%)
  waiting for transfers between devices  9.29 us (24%)
  between operations  0.9 us (2%)
    ppermute x7, starting transfers between devices, exchange(): return lax.ppermute(value, axis, pairs)  10.1 us
    ppermute x6, starting transfers between devices, exchange_beh(): return lax.ppermute(value, ('beh', 'node'), pairs)  7.24 us
    ppermute x6, waiting for transfers between devices, exchange_beh(): return lax.ppermute(value, ('beh', 'node'), pairs)  6.75 us
    pallas_call x4, Pallas kernels, merge(): pl.pallas_call(functools.partial(merge_kernel, len(projected), which, til...  3.54 us
    ppermute x7, waiting for transfers between devices, exchange(): return lax.ppermute(value, axis, pairs)  2.55 us
    pallas_call x1, Pallas kernels, sum_cells(): pl.pallas_call(functools.partial(cells_kernel, chunk, pairs, cell_count),...  2.43 us
    pallas_call x2, Pallas kernels, serve(): pl.pallas_call(functools.partial(serve_kernel, block_count, pairs), in_sp...  1.32 us
    pallas_call x1, Pallas kernels, load(): pl.pallas_call(load_kernel, in_specs=[HBM], out_specs=VMEM, out_shape=jax...  1.05 us
  transfers between devices with their start and end apart: 13, of which 6 were waited for; matrix products, arithmetic and copies ran while one was open for 1% of the time, Pallas kernels for 21%

profile of v3, /device:TPU:0, one launch (start us, length us, event | category | flops | bytes accessed | tf_op | source)
XLA Modules:
  0.0 38.8 jit_solution(16907534209825794071)
XLA Ops:
  0.5 2.6 %collective-permute-start.1 = (s32[1,4]{1,0:T(1,128)}, s32[1,4]{1,0:T(1,128)S(1)}, u32[]{:S(2)}, u32[]{:S(2)}) collective-permute-start(s32[1,4]{1,0:T(1,128)} %refs_2_.2), channel_id=1, source_target_pairs={{0,2},{1,3},{2,0},{3,1},{4,6},{5,7},{6,4},{7,5},{8,10},{9,11},{10,... | collective-permute-start | bytes 56 | tf_op jit(solution)/shard_map/ppermute | solution.py:33
  3.0 2.6 %collective-permute-start = (s32[1,4]{1,0:T(1,128)}, s32[1,4]{1,0:T(1,128)S(1)}, u32[]{:S(2)}, u32[]{:S(2)}) collective-permute-start(s32[1,4]{1,0:T(1,128)} %refs_2_.2), channel_id=1, source_target_pairs={{0,4},{1,5},{2,6},{3,7},{4,0},{5,1},{6,2},{7,3},{8,12},{9,13},{10,... | collective-permute-start | bytes 56 | tf_op jit(solution)/shard_map/ppermute | solution.py:33
  5.6 1.0 %load.1.refs_3_.refs_1_.refs_4_ = bf16[2048,128]{1,0:T(8,128)(2,1)S(1)} custom-call(bf16[2048,128]{1,0:T(8,128)(2,1)} %source.1), custom_call_target="tpu_custom_call" | custom-call | bytes 524288 | tf_op jit(solution)/shard_map/load/pallas_call | solution.py:117
  6.7 0.9 %collective-permute-done.refs_0_ = s32[1,4]{1,0:T(1,128)S(1)} collective-permute-done((s32[1,4]{1,0:T(1,128)}, s32[1,4]{1,0:T(1,128)S(1)}, u32[]{:S(2)}, u32[]{:S(2)}) %collective-permute-start) | collective-permute-done | bytes 48 | tf_op jit(solution)/shard_map/ppermute | solution.py:33
  7.6 0.8 %serve.2 = (bf16[128,128]{1,0:T(8,128)(2,1)S(1)}, bf16[128,128]{1,0:T(8,128)(2,1)S(1)}, bf16[128,128]{1,0:T(8,128)(2,1)S(1)}) custom-call(s32[1,4]{1,0:T(1,128)S(1)} %collective-permute-done.refs_0_, s32[1,4]{1,0:T(1,128)S(1)} %collective-permute-done.1.refs_1_, s32[1,4]{1,0:T(1,128)} %refs_2_.2, bf16[2048,128]{1,0:T(8,128)(2,1)S(1)} %load.1.refs_3_.refs_1_.refs_4_, ...), custom_call_target="tpu_custom_call" | custom-call | tf_op jit(solution)/shard_map/serve/pallas_call | solution.py:157
  8.6 3.3 %collective-permute-start.4 = (bf16[128,128]{1,0:T(8,128)(2,1)S(1)}, bf16[128,128]{1,0:T(8,128)(2,1)S(1)}, u32[]{:S(2)}, u32[]{:S(2)}) collective-permute-start(bf16[128,128]{1,0:T(8,128)(2,1)S(1)} %get-tuple-element.14), channel_id=1, source_target_pairs={{0,4},{1,5},{2,6},{3,7},{4,0},{5,1},{6,2},{7,3},{8,12},{9,13},{10,... | collective-permute-start | bytes 98312 | tf_op jit(solution)/shard_map/ppermute | solution.py:33
  12.5 1.0 %collective-permute-start.6 = (bf16[128,128]{1,0:T(8,128)(2,1)S(1)}, bf16[128,128]{1,0:T(8,128)(2,1)S(1)}, u32[]{:S(2)}, u32[]{:S(2)}) collective-permute-start(bf16[128,128]{1,0:T(8,128)(2,1)S(1)} %serve.3), channel_id=1, source_target_pairs={{0,6},{1,7},{2,4},{3,5},{4,2},{5,3},{6,0},{7,1},{8,14},{9,15},{10,... | collective-permute-start | bytes 98312 | tf_op jit(solution)/shard_map/ppermute | solution.py:33
  14.1 2.4 %cells.1 = bf16[64,128,128]{2,1,0:T(8,128)(2,1)S(1)} custom-call(s32[1,112]{1,0:T(1,128)} %refs_0_.1, s32[1,112]{1,0:T(1,128)} %refs_1_.1, s32[1,1]{1,0:T(1,128)S(6)} %copy.17.refs_2_, bf16[112,128,128]{2,1,0:T(8,128)(2,1)} %bitcast.9), custom_call_target="tpu_custom_call" | custom-call | bytes 3670016 | tf_op jit(solution)/shard_map/cells/pallas_call | solution.py:92
  16.7 1.6 %collective-permute-done.6.refs_3_ = bf16[128,128]{1,0:T(8,128)(2,1)S(1)} collective-permute-done((bf16[128,128]{1,0:T(8,128)(2,1)S(1)}, bf16[128,128]{1,0:T(8,128)(2,1)S(1)}, u32[]{:S(2)}, u32[]{:S(2)}) %collective-permute-start.6) | collective-permute-done | bytes 32800 | tf_op jit(solution)/shard_map/ppermute | solution.py:33
  18.3 0.7 %spread.1 = (bf16[512,128]{1,0:T(8,128)(2,1)S(1)}, bf16[512,128]{1,0:T(8,128)(2,1)S(1)}, bf16[512,128]{1,0:T(8,128)(2,1)S(1)}, bf16[512,128]{1,0:T(8,128)(2,1)S(1)}) custom-call(bf16[64,128,128]{2,1,0:T(8,128)(2,1)S(1)} %cells.1, bf16[128,128]{1,0:T(8,128)(2,1)S(1)} %get-tuple-element.12.refs_0_, bf16[128,128]{1,0:T(8,128)(2,1)S(1)} %collective-permute-done.3.refs_1_, ...), custom_call_target="tpu_custom_call" | custom-call | tf_op jit(solution)/shard_map/spread/pallas_call | solution.py:185
  19.0 1.6 %collective-permute-start.9 = (bf16[512,128]{1,0:T(8,128)(2,1)S(1)}, bf16[512,128]{1,0:T(8,128)(2,1)S(1)}, u32[]{:S(2)}, u32[]{:S(2)}) collective-permute-start(bf16[512,128]{1,0:T(8,128)(2,1)S(1)} %get-tuple-element.18), channel_id=1, source_target_pairs={{0,16},{1,9},{2,18},{3,11},{4,20},{5,13},{6,22},{7,15},{8,24},{9,1... | collective-permute-start | bytes 393224 | tf_op jit(solution)/shard_map/ppermute | solution.py:46
  20.6 1.5 %collective-permute-start.8 = (bf16[512,128]{1,0:T(8,128)(2,1)S(1)}, bf16[512,128]{1,0:T(8,128)(2,1)S(1)}, u32[]{:S(2)}, u32[]{:S(2)}) collective-permute-start(bf16[512,128]{1,0:T(8,128)(2,1)S(1)} %get-tuple-element.17), channel_id=1, source_target_pairs={{0,8},{1,17},{2,10},{3,19},{4,12},{5,21},{6,14},{7,23},{8,0},{9,25... | collective-permute-start | bytes 393224 | tf_op jit(solution)/shard_map/ppermute | solution.py:46
  23.2 2.2 %collective-permute-done.9.x.refs_0_ = bf16[512,128]{1,0:T(8,128)(2,1)S(1)} collective-permute-done((bf16[512,128]{1,0:T(8,128)(2,1)S(1)}, bf16[512,128]{1,0:T(8,128)(2,1)S(1)}, u32[]{:S(2)}, u32[]{:S(2)}) %collective-permute-start.9) | collective-permute-done | bytes 131104 | tf_op jit(solution)/shard_map/ppermute | solution.py:46
  26.0 2.0 %collective-permute-done.7.x.refs_0_ = bf16[512,128]{1,0:T(8,128)(2,1)S(1)} collective-permute-done((bf16[512,128]{1,0:T(8,128)(2,1)S(1)}, bf16[512,128]{1,0:T(8,128)(2,1)S(1)}, u32[]{:S(2)}, u32[]{:S(2)}) %collective-permute-start.7) | collective-permute-done | bytes 131104 | tf_op jit(solution)/shard_map/ppermute | solution.py:46
  28.2 0.9 %merge.5 = bf16[512,128]{1,0:T(8,128)(2,1)S(1)} custom-call(bf16[512,128]{1,0:T(8,128)(2,1)S(1)} %collective-permute-done.7.x.refs_0_, f32[384,512]{1,0:T(8,128)S(1)} %project.4.refs_1_, f32[384,512]{1,0:T(8,128)S(1)} %project.5.refs_2_, f32[384,512]{1,0:T(8,128)S(1)} %project.6.refs_3_, f32[384,512]{1,0:T(8,128)S(1)} %project.7.refs_4_, ...), custom_call_target="tpu_custom_call" | custom-call | flops 268435456 | bytes 65536 | tf_op jit(solution)/shard_map/merge/pallas_call | solution.py:252
  29.1 1.5 %collective-permute-start.10 = (bf16[512,128]{1,0:T(8,128)(2,1)S(1)}, bf16[512,128]{1,0:T(8,128)(2,1)S(1)}, u32[]{:S(2)}, u32[]{:S(2)}) collective-permute-start(bf16[512,128]{1,0:T(8,128)(2,1)S(1)} %merge.5), channel_id=1, source_target_pairs={{0,24},{1,25},{2,26},{3,27},{4,28},{5,29},{6,30},{7,31},{8,16},{9,... | collective-permute-start | bytes 393224 | tf_op jit(solution)/shard_map/ppermute | solution.py:46
  30.6 0.9 %merge.6 = bf16[512,128]{1,0:T(8,128)(2,1)S(1)} custom-call(bf16[512,128]{1,0:T(8,128)(2,1)S(1)} %collective-permute-done.8.x.refs_0_, f32[384,512]{1,0:T(8,128)S(1)} %project.4.refs_1_, f32[384,512]{1,0:T(8,128)S(1)} %project.5.refs_2_, f32[384,512]{1,0:T(8,128)S(1)} %project.6.refs_3_, f32[384,512]{1,0:T(8,128)S(1)} %project.7.refs_4_, ...), custom_call_target="tpu_custom_call" | custom-call | flops 268435456 | bytes 65536 | tf_op jit(solution)/shard_map/merge/pallas_call | solution.py:252
  31.5 0.6 %collective-permute-start.11 = (bf16[512,128]{1,0:T(8,128)(2,1)S(1)}, bf16[512,128]{1,0:T(8,128)(2,1)S(1)}, u32[]{:S(2)}, u32[]{:S(2)}) collective-permute-start(bf16[512,128]{1,0:T(8,128)(2,1)S(1)} %merge.6), channel_id=1, source_target_pairs={{0,8},{1,17},{2,10},{3,19},{4,12},{5,21},{6,14},{7,23},{8,0},{9,25... | collective-permute-start | bytes 393224 | tf_op jit(solution)/shard_map/ppermute | solution.py:46
  32.1 0.9 %merge.7 = bf16[512,128]{1,0:T(8,128)(2,1)S(1)} custom-call(bf16[512,128]{1,0:T(8,128)(2,1)S(1)} %collective-permute-done.9.x.refs_0_, f32[384,512]{1,0:T(8,128)S(1)} %project.4.refs_1_, f32[384,512]{1,0:T(8,128)S(1)} %project.5.refs_2_, f32[384,512]{1,0:T(8,128)S(1)} %project.6.refs_3_, f32[384,512]{1,0:T(8,128)S(1)} %project.7.refs_4_, ...), custom_call_target="tpu_custom_call" | custom-call | flops 268435456 | bytes 65536 | tf_op jit(solution)/shard_map/merge/pallas_call | solution.py:252
  33.0 1.6 %collective-permute-start.12 = (bf16[512,128]{1,0:T(8,128)(2,1)S(1)}, bf16[512,128]{1,0:T(8,128)(2,1)S(1)}, u32[]{:S(2)}, u32[]{:S(2)}) collective-permute-start(bf16[512,128]{1,0:T(8,128)(2,1)S(1)} %merge.7), channel_id=1, source_target_pairs={{0,16},{1,9},{2,18},{3,11},{4,20},{5,13},{6,22},{7,15},{8,24},{9,1... | collective-permute-start | bytes 393224 | tf_op jit(solution)/shard_map/ppermute | solution.py:46
  34.6 0.9 %merge.4.refs_0_ = bf16[512,128]{1,0:T(8,128)(2,1)S(1)} custom-call(bf16[512,128]{1,0:T(8,128)(2,1)S(1)} %get-tuple-element.15.x.refs_0_, f32[384,512]{1,0:T(8,128)S(1)} %project.4.refs_1_, f32[384,512]{1,0:T(8,128)S(1)} %project.5.refs_2_, f32[384,512]{1,0:T(8,128)S(1)} %project.6.refs_3_, f32[384,512]{1,0:T(8,128)S(1)} %project.7.refs_4_, ...), custom_call_target="tpu_custom_call" | custom-call | flops 268435456 | bytes 65536 | tf_op jit(solution)/shard_map/merge/pallas_call | solution.py:252
  35.5 1.0 %collective-permute-done.11.refs_2_ = bf16[512,128]{1,0:T(8,128)(2,1)S(1)} collective-permute-done((bf16[512,128]{1,0:T(8,128)(2,1)S(1)}, bf16[512,128]{1,0:T(8,128)(2,1)S(1)}, u32[]{:S(2)}, u32[]{:S(2)}) %collective-permute-start.11) | collective-permute-done | bytes 131104 | tf_op jit(solution)/shard_map/ppermute | solution.py:46
  36.5 1.5 %collective-permute-done.12.refs_3_ = bf16[512,128]{1,0:T(8,128)(2,1)S(1)} collective-permute-done((bf16[512,128]{1,0:T(8,128)(2,1)S(1)}, bf16[512,128]{1,0:T(8,128)(2,1)S(1)}, u32[]{:S(2)}, u32[]{:S(2)}) %collective-permute-start.12) | collective-permute-done | bytes 131104 | tf_op jit(solution)/shard_map/ppermute | solution.py:46
  38.0 0.8 %place.1 = bf16[2048,128]{1,0:T(8,128)(2,1)} custom-call(bf16[512,128]{1,0:T(8,128)(2,1)S(1)} %merge.4.refs_0_, bf16[512,128]{1,0:T(8,128)(2,1)S(1)} %collective-permute-done.10.refs_1_, bf16[512,128]{1,0:T(8,128)(2,1)S(1)} %collective-permute-done.11.refs_2_, bf16[512,128]{1,0:T(8,128)(2,1)S(1)} %collective-permute-done.12.refs_3_), custom_call_target="tpu_custom_call" | custom-call | tf_op jit(solution)/shard_map/place/pallas_call | solution.py:277
  (34 shorter events, 3.2 us)
Async XLA Ops:
  0.0 7.6 %collective-permute-start.2 = (bf16[2048,128]{1,0:T(8,128)(2,1)}, bf16[2048,128]{1,0:T(8,128)(2,1)S(1)}, u32[]{:S(2)}, u32[]{:S(2)}) collective-permute-start(bf16[2048,128]{1,0:T(8,128)(2,1)} %source.1), channel_id=1, source_target_pairs={{0,1},{1,0},{2,3},{3,2},{4,5},{5,4},{6,7},{7,6},{8,9},{9,8},{10,11... | collective-permute-start | bytes 1572872 | tf_op jit(solution)/shard_map/ppermute | solution.py:33
  0.5 6.2 %collective-permute-start.1 = (s32[1,4]{1,0:T(1,128)}, s32[1,4]{1,0:T(1,128)S(1)}, u32[]{:S(2)}, u32[]{:S(2)}) collective-permute-start(s32[1,4]{1,0:T(1,128)} %refs_2_.2), channel_id=1, source_target_pairs={{0,2},{1,3},{2,0},{3,1},{4,6},{5,7},{6,4},{7,5},{8,10},{9,11},{10,... | collective-permute-start | bytes 56 | tf_op jit(solution)/shard_map/ppermute | solution.py:33
  3.0 4.6 %collective-permute-start = (s32[1,4]{1,0:T(1,128)}, s32[1,4]{1,0:T(1,128)S(1)}, u32[]{:S(2)}, u32[]{:S(2)}) collective-permute-start(s32[1,4]{1,0:T(1,128)} %refs_2_.2), channel_id=1, source_target_pairs={{0,4},{1,5},{2,6},{3,7},{4,0},{5,1},{6,2},{7,3},{8,12},{9,13},{10,... | collective-permute-start | bytes 56 | tf_op jit(solution)/shard_map/ppermute | solution.py:33
  5.6 6.3 %collective-permute-start.5 = (s32[1,4]{1,0:T(1,128)}, s32[1,4]{1,0:T(1,128)S(1)}, u32[]{:S(2)}, u32[]{:S(2)}) collective-permute-start(s32[1,4]{1,0:T(1,128)} %refs_2_.2), channel_id=1, source_target_pairs={{0,6},{1,7},{2,4},{3,5},{4,2},{5,3},{6,0},{7,1},{8,14},{9,15},{10,... | collective-permute-start | bytes 56 | tf_op jit(solution)/shard_map/ppermute | solution.py:33
  8.4 8.3 %collective-permute-start.3 = (bf16[128,128]{1,0:T(8,128)(2,1)S(1)}, bf16[128,128]{1,0:T(8,128)(2,1)S(1)}, u32[]{:S(2)}, u32[]{:S(2)}) collective-permute-start(bf16[128,128]{1,0:T(8,128)(2,1)S(1)} %get-tuple-element.13), channel_id=1, source_target_pairs={{0,2},{1,3},{2,0},{3,1},{4,6},{5,7},{6,4},{7,5},{8,10},{9,11},{10,... | collective-permute-start | bytes 98312 | tf_op jit(solution)/shard_map/ppermute | solution.py:33
  8.6 8.1 %collective-permute-start.4 = (bf16[128,128]{1,0:T(8,128)(2,1)S(1)}, bf16[128,128]{1,0:T(8,128)(2,1)S(1)}, u32[]{:S(2)}, u32[]{:S(2)}) collective-permute-start(bf16[128,128]{1,0:T(8,128)(2,1)S(1)} %get-tuple-element.14), channel_id=1, source_target_pairs={{0,4},{1,5},{2,6},{3,7},{4,0},{5,1},{6,2},{7,3},{8,12},{9,13},{10,... | collective-permute-start | bytes 98312 | tf_op jit(solution)/shard_map/ppermute | solution.py:33
  12.5 5.8 %collective-permute-start.6 = (bf16[128,128]{1,0:T(8,128)(2,1)S(1)}, bf16[128,128]{1,0:T(8,128)(2,1)S(1)}, u32[]{:S(2)}, u32[]{:S(2)}) collective-permute-start(bf16[128,128]{1,0:T(8,128)(2,1)S(1)} %serve.3), channel_id=1, source_target_pairs={{0,6},{1,7},{2,4},{3,5},{4,2},{5,3},{6,0},{7,1},{8,14},{9,15},{10,... | collective-permute-start | bytes 98312 | tf_op jit(solution)/shard_map/ppermute | solution.py:33
  14.1 8.4 %copy-start.4 = (bf16[128,128]{1,0:T(8,128)(2,1)S(1)}, bf16[128,128]{1,0:T(8,128)(2,1)}, u32[]{:S(2)}) copy-start(bf16[128,128]{1,0:T(8,128)(2,1)} %param.19) | copy-start | bytes 98308
  14.1 8.5 %copy-start.5 = (bf16[128,128]{1,0:T(8,128)(2,1)S(1)}, bf16[128,128]{1,0:T(8,128)(2,1)}, u32[]{:S(2)}) copy-start(bf16[128,128]{1,0:T(8,128)(2,1)} %param.20) | copy-start | bytes 98308
  14.1 8.6 %copy-start.6 = (bf16[128,128]{1,0:T(8,128)(2,1)S(1)}, bf16[128,128]{1,0:T(8,128)(2,1)}, u32[]{:S(2)}) copy-start(bf16[128,128]{1,0:T(8,128)(2,1)} %param.21) | copy-start | bytes 98308
  16.6 11.6 %copy-start = (bf16[128,512]{1,0:T(8,128)(2,1)S(1)}, bf16[128,512]{1,0:T(8,128)(2,1)}, u32[]{:S(2)}) copy-start(bf16[128,512]{1,0:T(8,128)(2,1)} %refs_7_.7) | copy-start | bytes 393220
  16.6 11.6 %copy-start.1 = (bf16[512,128]{1,0:T(8,128)(2,1)S(1)}, bf16[512,128]{1,0:T(8,128)(2,1)}, u32[]{:S(2)}) copy-start(bf16[512,128]{1,0:T(8,128)(2,1)} %refs_8_.7) | copy-start | bytes 393220
  16.6 11.6 %copy-start.2 = (bf16[128,128]{1,0:T(8,128)(2,1)S(1)}, bf16[128,128]{1,0:T(8,128)(2,1)}, u32[]{:S(2)}) copy-start(bf16[128,128]{1,0:T(8,128)(2,1)} %refs_5_.7) | copy-start | bytes 98308
  16.6 11.6 %copy-start.3 = (f32[128]{0:T(128)S(1)}, f32[128]{0:T(128)}, u32[]{:S(2)}) copy-start(f32[128]{0:T(128)} %param.23) | copy-start | bytes 1540
  19.0 6.4 %collective-permute-start.9 = (bf16[512,128]{1,0:T(8,128)(2,1)S(1)}, bf16[512,128]{1,0:T(8,128)(2,1)S(1)}, u32[]{:S(2)}, u32[]{:S(2)}) collective-permute-start(bf16[512,128]{1,0:T(8,128)(2,1)S(1)} %get-tuple-element.18), channel_id=1, source_target_pairs={{0,16},{1,9},{2,18},{3,11},{4,20},{5,13},{6,22},{7,15},{8,24},{9,1... | collective-permute-start | bytes 393224 | tf_op jit(solution)/shard_map/ppermute | solution.py:46
  20.6 5.1 %collective-permute-start.8 = (bf16[512,128]{1,0:T(8,128)(2,1)S(1)}, bf16[512,128]{1,0:T(8,128)(2,1)S(1)}, u32[]{:S(2)}, u32[]{:S(2)}) collective-permute-start(bf16[512,128]{1,0:T(8,128)(2,1)S(1)} %get-tuple-element.17), channel_id=1, source_target_pairs={{0,8},{1,17},{2,10},{3,19},{4,12},{5,21},{6,14},{7,23},{8,0},{9,25... | collective-permute-start | bytes 393224 | tf_op jit(solution)/shard_map/ppermute | solution.py:46
  22.1 5.9 %collective-permute-start.7 = (bf16[512,128]{1,0:T(8,128)(2,1)S(1)}, bf16[512,128]{1,0:T(8,128)(2,1)S(1)}, u32[]{:S(2)}, u32[]{:S(2)}) collective-permute-start(bf16[512,128]{1,0:T(8,128)(2,1)S(1)} %get-tuple-element.16), channel_id=1, source_target_pairs={{0,24},{1,25},{2,26},{3,27},{4,28},{5,29},{6,30},{7,31},{8,16},{9,... | collective-permute-start | bytes 393224 | tf_op jit(solution)/shard_map/ppermute | solution.py:46
  29.1 6.4 %collective-permute-start.10 = (bf16[512,128]{1,0:T(8,128)(2,1)S(1)}, bf16[512,128]{1,0:T(8,128)(2,1)S(1)}, u32[]{:S(2)}, u32[]{:S(2)}) collective-permute-start(bf16[512,128]{1,0:T(8,128)(2,1)S(1)} %merge.5), channel_id=1, source_target_pairs={{0,24},{1,25},{2,26},{3,27},{4,28},{5,29},{6,30},{7,31},{8,16},{9,... | collective-permute-start | bytes 393224 | tf_op jit(solution)/shard_map/ppermute | solution.py:46
  31.5 5.0 %collective-permute-start.11 = (bf16[512,128]{1,0:T(8,128)(2,1)S(1)}, bf16[512,128]{1,0:T(8,128)(2,1)S(1)}, u32[]{:S(2)}, u32[]{:S(2)}) collective-permute-start(bf16[512,128]{1,0:T(8,128)(2,1)S(1)} %merge.6), channel_id=1, source_target_pairs={{0,8},{1,17},{2,10},{3,19},{4,12},{5,21},{6,14},{7,23},{8,0},{9,25... | collective-permute-start | bytes 393224 | tf_op jit(solution)/shard_map/ppermute | solution.py:46
  33.0 5.0 %collective-permute-start.12 = (bf16[512,128]{1,0:T(8,128)(2,1)S(1)}, bf16[512,128]{1,0:T(8,128)(2,1)S(1)}, u32[]{:S(2)}, u32[]{:S(2)}) collective-permute-start(bf16[512,128]{1,0:T(8,128)(2,1)S(1)} %merge.7), channel_id=1, source_target_pairs={{0,16},{1,9},{2,18},{3,11},{4,20},{5,13},{6,22},{7,15},{8,24},{9,1... | collective-permute-start | bytes 393224 | tf_op jit(solution)/shard_map/ppermute | solution.py:46

commit v4 on v3

--- a/solution.py
+++ b/solution.py
@@ -35,7 +35,7 @@
 
 def beh_masks(parts):
     first, *rest = range(parts - 1, 0, -1)
-    return [(0, 0), (first, first)] + list(zip(rest[::-1], rest))
+    return [(0, 0)] + list(zip(rest, rest)) + [(first, first)]
 
 
 def exchange_beh(value, masks):
@@ -165,12 +165,12 @@
     )(*asks, own, other)
 
 
-def spread_kernel(pairs, cells, *refs):
+def spread_kernel(pairs, which, parts, cells, *refs):
     sources, own, outs = refs[:pairs], refs[pairs], refs[pairs + 1 :]
     stack = jnp.concatenate([s[...] for s in sources], axis=0)
     size = outs[0].shape[0]
-    for k, out in enumerate(outs):
-        part = part_of(k, len(outs))
+    for k, out in zip(which, outs):
+        part = part_of(k, parts)
         start = pl.multiple_of(part * size, size)
         block = part * (size // TB)
         for r in range(size // TB):
@@ -180,19 +180,20 @@
             out[r * TB : (r + 1) * TB, :] = (total + rows).astype(BF16)
 
 
-def spread_cells(cells, sources, own, parts):
+def spread_cells(cells, sources, own, which, parts):
     size = own.shape[0] // parts
     return pl.pallas_call(
-        functools.partial(spread_kernel, len(sources)),
+        functools.partial(spread_kernel, len(sources), which, parts),
         in_specs=[VMEM] * (len(sources) + 2),
-        out_specs=[VMEM] * parts,
-        out_shape=[jax.ShapeDtypeStruct((size, own.shape[1]), BF16)] * parts,
+        out_specs=[VMEM] * len(which),
+        out_shape=[jax.ShapeDtypeStruct((size, own.shape[1]), BF16)] * len(which),
         compiler_params=params(),
         name="spread",
     )(cells, *sources, own)
 
 
-def project_kernel(w_qkv, x, out):
+def project_kernel(w_qkv, x, *refs):
+    out = refs[-1]
     feature = x.shape[1]
     full = lax.dot_general(w_qkv[...], x[...], (((1,), (1,)), ((), ())), preferred_element_type=F32)
     scale = math.log2(math.e) / math.sqrt(HEAD)
@@ -200,16 +201,16 @@
     out[feature:] = full[feature:]
 
 
-def project(w_qkv, x):
+def project(w_qkv, x, *before):
     return pl.pallas_call(
         project_kernel,
-        in_specs=[VMEM] * 2,
+        in_specs=[VMEM] * (2 + len(before)),
         out_specs=VMEM,
         out_shape=jax.ShapeDtypeStruct((w_qkv.shape[0], x.shape[0]), F32),
         compiler_params=params(),
         cost_estimate=cost(2 * w_qkv.size * x.shape[0], w_qkv.size),
         name="project",
-    )(w_qkv, x)
+    )(w_qkv, x, *before)
 
 
 def merge_kernel(count, which, tile, *refs):
@@ -260,28 +261,30 @@
     )(x, *projected, w_out, gain, w_up, w_down)
 
 
-def place_kernel(*refs):
-    parts, out, sems = refs[:-2], refs[-2], refs[-1]
-    size = parts[0].shape[0]
+def place_kernel(which, parts, *refs):
+    pieces, out, sems = refs[: len(which)], refs[-2], refs[-1]
+    size = pieces[0].shape[0]
     copies = []
-    for k, part in enumerate(parts):
-        start = pl.multiple_of(part_of(k, len(parts)) * size, size)
-        copies.append(pltpu.make_async_copy(part, out.at[pl.ds(start, size), :], sems.at[k]))
+    for slot, (k, piece) in enumerate(zip(which, pieces)):
+        start = pl.multiple_of(part_of(k, parts) * size, size)
+        copies.append(pltpu.make_async_copy(piece, out.at[pl.ds(start, size), :], sems.at[slot]))
         copies[-1].start()
     for copy in copies:
         copy.wait()
 
 
-def place_parts(parts):
-    size, feature = parts[0].shape
-    return pl.pallas_call(
-        place_kernel,
-        in_specs=[VMEM] * len(parts),
+def place_parts(pieces, which, parts, *begun):
+    size, feature = pieces[0].shape
+    return pl.pallas_call(
+        functools.partial(place_kernel, which, parts),
+        in_specs=[VMEM] * len(pieces) + [HBM] * len(begun),
         out_specs=HBM,
-        out_shape=jax.ShapeDtypeStruct((size * len(parts), feature), BF16),
-        scratch_shapes=[pltpu.SemaphoreType.DMA((len(parts),))],
+        out_shape=jax.ShapeDtypeStruct((size * parts, feature), BF16),
+        scratch_shapes=[pltpu.SemaphoreType.DMA((len(pieces),))],
+        input_output_aliases={len(pieces): 0} if begun else {},
+        compiler_params=params(),
         name="place",
-    )(*vmem(*parts))
+    )(*vmem(*pieces), *begun)
 
 
 def tiles_kernel(chunk, rows, cols, count, tiles, sources, own, out, total):
@@ -379,7 +382,8 @@
         served = serve(asks[:1], own, other, block_count)
         *more, here = serve(asks[1:], own, other, block_count)
         sources = [here] + [exchange(block, "node", 2 * k) for k, block in zip(far, [*served, *more])][::-1]
-        quarters = spread_cells(cells, sources, own, parts)
+        last = spread_cells(cells, sources, own, [parts - 1], parts)
+        quarters = spread_cells(cells, sources, own, list(range(parts - 1)), parts) + last
     else:
         sources = fetch_many(embeddings, need_ids, block_count)
         spread = spread_tiles(tile_rows, tile_cols, tile_count, tiles, sources, embeddings)
@@ -388,10 +392,15 @@
     masks = beh_masks(parts)
     xs = [quarters[0]] + [exchange_beh(quarters[k], masks[k]) for k in range(1, parts)]
     w_qkv = jnp.concatenate([w_query, w_key, w_value], axis=1).T
-    projected = [project(w_qkv, x) for x in xs]
-    merged = [merge(xs[k], projected, k, w_out, mlp_gain[None], w_up, w_down) for k in range(parts)]
-    back = [merged[0]] + [exchange_beh(merged[k], masks[k]) for k in range(1, parts)]
-    return place_parts(back)[None]
+    order = [parts - 1, *range(1, parts - 1), 0]
+    projected = [project(w_qkv, xs[0])] * parts
+    for k, before in zip(order[:-1], order[-1:] + order):
+        projected[k] = project(w_qkv, xs[k], projected[before])
+    merged = [merge(xs[k], projected, k, w_out, mlp_gain[None], w_up, w_down) for k in order]
+    back = [exchange_beh(part, masks[k]) if k else part for k, part in zip(order, merged)]
+    late = parts - 2
+    begun = place_parts(back[:late] + back[late + 1 :], order[:late] + order[late + 1 :], parts)
+    return place_parts(back[late : late + 1], order[late : late + 1], parts, begun)[None]
 
 
 def solution(mesh):

time: 39 us -> 38.7 us (level)
  waiting for transfers between devices: 9.29 us -> 8.13 us
  Pallas kernels: 10.9 us -> 11.6 us
    ppermute x6, waiting for transfers between devices: 6.75 us -> 5.54 us  [exchange_beh(): return lax.ppermute(value, ('beh', 'node'), pairs)]
    pallas_call x6 -> x8, Pallas kernels: 2.55 us -> 3.32 us  [the longest x2 1.43 us: place_parts(): pl.pallas_call(functools.partial(place_kernel, which, parts), in_specs=[V...]
  transfers between devices with their start and end apart: 13 -> 13, of which waited for: 6 -> 7; matrix products, arithmetic and copies ran while one was open for 1% -> 1% of each run, Pallas kernels for 21% -> 25%
where the time goes in v4:
time: 38.7 us; the launch traced here: 38.5 us
  starting transfers between devices  17.4 us (45%)
  Pallas kernels  11.6 us (30%)
  waiting for transfers between devices  8.13 us (21%)
  between operations  0.9 us (2%)
    ppermute x7, starting transfers between devices, exchange(): return lax.ppermute(value, axis, pairs)  10.1 us
    ppermute x6, starting transfers between devices, exchange_beh(): return lax.ppermute(value, ('beh', 'node'), pairs)  7.3 us
    ppermute x6, waiting for transfers between devices, exchange_beh(): return lax.ppermute(value, ('beh', 'node'), pairs)  5.54 us
    pallas_call x4, Pallas kernels, merge(): pl.pallas_call(functools.partial(merge_kernel, len(projected), which, til...  3.5 us
    ppermute x7, waiting for transfers between devices, exchange(): return lax.ppermute(value, axis, pairs)  2.6 us
    pallas_call x1, Pallas kernels, sum_cells(): pl.pallas_call(functools.partial(cells_kernel, chunk, pairs, cell_count),...  2.43 us
    pallas_call x2, Pallas kernels, place_parts(): pl.pallas_call(functools.partial(place_kernel, which, parts), in_specs=[V...  1.43 us
    pallas_call x2, Pallas kernels, serve(): pl.pallas_call(functools.partial(serve_kernel, block_count, pairs), in_sp...  1.32 us
  transfers between devices with their start and end apart: 13, of which 7 were waited for; matrix products, arithmetic and copies ran while one was open for 1% of the time, Pallas kernels for 25%

profile of v4, /device:TPU:0, one launch (start us, length us, event | category | flops | bytes accessed | tf_op | source)
XLA Modules:
  0.0 38.5 jit_solution(12807108038950762943)
XLA Ops:
  0.5 2.6 %collective-permute-start.1 = (s32[1,4]{1,0:T(1,128)}, s32[1,4]{1,0:T(1,128)S(1)}, u32[]{:S(2)}, u32[]{:S(2)}) collective-permute-start(s32[1,4]{1,0:T(1,128)} %refs_2_.2), channel_id=1, source_target_pairs={{0,2},{1,3},{2,0},{3,1},{4,6},{5,7},{6,4},{7,5},{8,10},{9,11},{10,... | collective-permute-start | bytes 56 | tf_op jit(solution)/shard_map/ppermute | solution.py:33
  3.0 2.6 %collective-permute-start = (s32[1,4]{1,0:T(1,128)}, s32[1,4]{1,0:T(1,128)S(1)}, u32[]{:S(2)}, u32[]{:S(2)}) collective-permute-start(s32[1,4]{1,0:T(1,128)} %refs_2_.2), channel_id=1, source_target_pairs={{0,4},{1,5},{2,6},{3,7},{4,0},{5,1},{6,2},{7,3},{8,12},{9,13},{10,... | collective-permute-start | bytes 56 | tf_op jit(solution)/shard_map/ppermute | solution.py:33
  5.6 1.0 %load.1.refs_3_.refs_1_.refs_4_ = bf16[2048,128]{1,0:T(8,128)(2,1)S(1)} custom-call(bf16[2048,128]{1,0:T(8,128)(2,1)} %source.1), custom_call_target="tpu_custom_call" | custom-call | bytes 524288 | tf_op jit(solution)/shard_map/load/pallas_call | solution.py:117
  6.7 0.9 %collective-permute-done.refs_0_ = s32[1,4]{1,0:T(1,128)S(1)} collective-permute-done((s32[1,4]{1,0:T(1,128)}, s32[1,4]{1,0:T(1,128)S(1)}, u32[]{:S(2)}, u32[]{:S(2)}) %collective-permute-start) | collective-permute-done | bytes 48 | tf_op jit(solution)/shard_map/ppermute | solution.py:33
  7.6 0.8 %serve.2 = (bf16[128,128]{1,0:T(8,128)(2,1)S(1)}, bf16[128,128]{1,0:T(8,128)(2,1)S(1)}, bf16[128,128]{1,0:T(8,128)(2,1)S(1)}) custom-call(s32[1,4]{1,0:T(1,128)S(1)} %collective-permute-done.refs_0_, s32[1,4]{1,0:T(1,128)S(1)} %collective-permute-done.1.refs_1_, s32[1,4]{1,0:T(1,128)} %refs_2_.2, bf16[2048,128]{1,0:T(8,128)(2,1)S(1)} %load.1.refs_3_.refs_1_.refs_4_, ...), custom_call_target="tpu_custom_call" | custom-call | tf_op jit(solution)/shard_map/serve/pallas_call | solution.py:157
  8.6 3.3 %collective-permute-start.4 = (bf16[128,128]{1,0:T(8,128)(2,1)S(1)}, bf16[128,128]{1,0:T(8,128)(2,1)S(1)}, u32[]{:S(2)}, u32[]{:S(2)}) collective-permute-start(bf16[128,128]{1,0:T(8,128)(2,1)S(1)} %get-tuple-element.13), channel_id=1, source_target_pairs={{0,4},{1,5},{2,6},{3,7},{4,0},{5,1},{6,2},{7,3},{8,12},{9,13},{10,... | collective-permute-start | bytes 98312 | tf_op jit(solution)/shard_map/ppermute | solution.py:33
  12.5 1.0 %collective-permute-start.6 = (bf16[128,128]{1,0:T(8,128)(2,1)S(1)}, bf16[128,128]{1,0:T(8,128)(2,1)S(1)}, u32[]{:S(2)}, u32[]{:S(2)}) collective-permute-start(bf16[128,128]{1,0:T(8,128)(2,1)S(1)} %serve.3), channel_id=1, source_target_pairs={{0,6},{1,7},{2,4},{3,5},{4,2},{5,3},{6,0},{7,1},{8,14},{9,15},{10,... | collective-permute-start | bytes 98312 | tf_op jit(solution)/shard_map/ppermute | solution.py:33
  14.1 2.4 %cells.1 = bf16[64,128,128]{2,1,0:T(8,128)(2,1)S(1)} custom-call(s32[1,112]{1,0:T(1,128)} %refs_0_.1, s32[1,112]{1,0:T(1,128)} %refs_1_.1, s32[1,1]{1,0:T(1,128)S(6)} %copy.19.refs_2_, bf16[112,128,128]{2,1,0:T(8,128)(2,1)} %bitcast.9), custom_call_target="tpu_custom_call" | custom-call | bytes 3670016 | tf_op jit(solution)/shard_map/cells/pallas_call | solution.py:92
  16.6 1.7 %collective-permute-done.6.refs_3_ = bf16[128,128]{1,0:T(8,128)(2,1)S(1)} collective-permute-done((bf16[128,128]{1,0:T(8,128)(2,1)S(1)}, bf16[128,128]{1,0:T(8,128)(2,1)S(1)}, u32[]{:S(2)}, u32[]{:S(2)}) %collective-permute-start.6) | collective-permute-done | bytes 32800 | tf_op jit(solution)/shard_map/ppermute | solution.py:33
  18.6 2.5 %collective-permute-start.9 = (bf16[512,128]{1,0:T(8,128)(2,1)S(1)}, bf16[512,128]{1,0:T(8,128)(2,1)S(1)}, u32[]{:S(2)}, u32[]{:S(2)}) collective-permute-start(bf16[512,128]{1,0:T(8,128)(2,1)S(1)} %spread.3), channel_id=1, source_target_pairs={{0,24},{1,25},{2,26},{3,27},{4,28},{5,29},{6,30},{7,31},{8,16},{9,... | collective-permute-start | bytes 393224 | tf_op jit(solution)/shard_map/ppermute | solution.py:46
  21.7 0.6 %collective-permute-start.8 = (bf16[512,128]{1,0:T(8,128)(2,1)S(1)}, bf16[512,128]{1,0:T(8,128)(2,1)S(1)}, u32[]{:S(2)}, u32[]{:S(2)}) collective-permute-start(bf16[512,128]{1,0:T(8,128)(2,1)S(1)} %get-tuple-element.16), channel_id=1, source_target_pairs={{0,16},{1,17},{2,18},{3,19},{4,20},{5,21},{6,22},{7,23},{8,24},{9,... | collective-permute-start | bytes 393224 | tf_op jit(solution)/shard_map/ppermute | solution.py:46
  23.5 2.3 %collective-permute-done.9.x.refs_0_ = bf16[512,128]{1,0:T(8,128)(2,1)S(1)} collective-permute-done((bf16[512,128]{1,0:T(8,128)(2,1)S(1)}, bf16[512,128]{1,0:T(8,128)(2,1)S(1)}, u32[]{:S(2)}, u32[]{:S(2)}) %collective-permute-start.9) | collective-permute-done | bytes 131104 | tf_op jit(solution)/shard_map/ppermute | solution.py:46
  26.0 0.9 %collective-permute-done.8.x.refs_0_ = bf16[512,128]{1,0:T(8,128)(2,1)S(1)} collective-permute-done((bf16[512,128]{1,0:T(8,128)(2,1)S(1)}, bf16[512,128]{1,0:T(8,128)(2,1)S(1)}, u32[]{:S(2)}, u32[]{:S(2)}) %collective-permute-start.8) | collective-permute-done | bytes 131104 | tf_op jit(solution)/shard_map/ppermute | solution.py:46
  27.5 0.9 %merge.5 = bf16[512,128]{1,0:T(8,128)(2,1)S(1)} custom-call(bf16[512,128]{1,0:T(8,128)(2,1)S(1)} %collective-permute-done.9.x.refs_0_, f32[384,512]{1,0:T(8,128)S(1)} %project.4.refs_0_.refs_1_, f32[384,512]{1,0:T(8,128)S(1)} %project.6.refs_0_.refs_2_, f32[384,512]{1,0:T(8,128)S(1)} %project.7.refs_3_, f32[384,512]{1,0:T(8,128)S(1)} %project.5.refs_0_.refs_4_, ...), custom_call_target="tpu_custom_call" | custom-call | flops 268435456 | bytes 65536 | tf_op jit(solution)/shard_map/merge/pallas_call | solution.py:253
  28.4 1.6 %collective-permute-start.11 = (bf16[512,128]{1,0:T(8,128)(2,1)S(1)}, bf16[512,128]{1,0:T(8,128)(2,1)S(1)}, u32[]{:S(2)}, u32[]{:S(2)}) collective-permute-start(bf16[512,128]{1,0:T(8,128)(2,1)S(1)} %merge.5), channel_id=1, source_target_pairs={{0,24},{1,25},{2,26},{3,27},{4,28},{5,29},{6,30},{7,31},{8,16},{9,... | collective-permute-start | bytes 393224 | tf_op jit(solution)/shard_map/ppermute | solution.py:46
  30.0 0.9 %merge.6 = bf16[512,128]{1,0:T(8,128)(2,1)S(1)} custom-call(bf16[512,128]{1,0:T(8,128)(2,1)S(1)} %collective-permute-done.8.x.refs_0_, f32[384,512]{1,0:T(8,128)S(1)} %project.4.refs_0_.refs_1_, f32[384,512]{1,0:T(8,128)S(1)} %project.6.refs_0_.refs_2_, f32[384,512]{1,0:T(8,128)S(1)} %project.7.refs_3_, f32[384,512]{1,0:T(8,128)S(1)} %project.5.refs_0_.refs_4_, ...), custom_call_target="tpu_custom_call" | custom-call | flops 268435456 | bytes 65536 | tf_op jit(solution)/shard_map/merge/pallas_call | solution.py:253
  30.9 1.0 %collective-permute-start.12 = (bf16[512,128]{1,0:T(8,128)(2,1)S(1)}, bf16[512,128]{1,0:T(8,128)(2,1)S(1)}, u32[]{:S(2)}, u32[]{:S(2)}) collective-permute-start(bf16[512,128]{1,0:T(8,128)(2,1)S(1)} %merge.6), channel_id=1, source_target_pairs={{0,16},{1,17},{2,18},{3,19},{4,20},{5,21},{6,22},{7,23},{8,24},{9,... | collective-permute-start | bytes 393224 | tf_op jit(solution)/shard_map/ppermute | solution.py:46
  31.9 0.9 %merge.4 = bf16[512,128]{1,0:T(8,128)(2,1)S(1)} custom-call(bf16[512,128]{1,0:T(8,128)(2,1)S(1)} %collective-permute-done.7.x.refs_0_, f32[384,512]{1,0:T(8,128)S(1)} %project.4.refs_0_.refs_1_, f32[384,512]{1,0:T(8,128)S(1)} %project.6.refs_0_.refs_2_, f32[384,512]{1,0:T(8,128)S(1)} %project.7.refs_3_, f32[384,512]{1,0:T(8,128)S(1)} %project.5.refs_0_.refs_4_, ...), custom_call_target="tpu_custom_call" | custom-call | flops 268435456 | bytes 65536 | tf_op jit(solution)/shard_map/merge/pallas_call | solution.py:253
  32.8 1.1 %collective-permute-start.10 = (bf16[512,128]{1,0:T(8,128)(2,1)S(1)}, bf16[512,128]{1,0:T(8,128)(2,1)S(1)}, u32[]{:S(2)}, u32[]{:S(2)}) collective-permute-start(bf16[512,128]{1,0:T(8,128)(2,1)S(1)} %merge.4), channel_id=1, source_target_pairs={{0,8},{1,9},{2,10},{3,11},{4,12},{5,13},{6,14},{7,15},{8,0},{9,1},... | collective-permute-start | bytes 393224 | tf_op jit(solution)/shard_map/ppermute | solution.py:46
  33.9 0.9 %merge.7.refs_2_ = bf16[512,128]{1,0:T(8,128)(2,1)S(1)} custom-call(bf16[512,128]{1,0:T(8,128)(2,1)S(1)} %get-tuple-element.15.x.refs_0_, f32[384,512]{1,0:T(8,128)S(1)} %project.4.refs_0_.refs_1_, f32[384,512]{1,0:T(8,128)S(1)} %project.6.refs_0_.refs_2_, f32[384,512]{1,0:T(8,128)S(1)} %project.7.refs_3_, f32[384,512]{1,0:T(8,128)S(1)} %project.5.refs_0_.refs_4_, ...), custom_call_target="tpu_custom_call" | custom-call | flops 268435456 | bytes 65536 | tf_op jit(solution)/shard_map/merge/pallas_call | solution.py:253
  34.7 1.1 %collective-permute-done.11.refs_0_ = bf16[512,128]{1,0:T(8,128)(2,1)S(1)} collective-permute-done((bf16[512,128]{1,0:T(8,128)(2,1)S(1)}, bf16[512,128]{1,0:T(8,128)(2,1)S(1)}, u32[]{:S(2)}, u32[]{:S(2)}) %collective-permute-start.11) | collective-permute-done | bytes 131104 | tf_op jit(solution)/shard_map/ppermute | solution.py:46
  35.8 0.7 %collective-permute-done.12.refs_1_ = bf16[512,128]{1,0:T(8,128)(2,1)S(1)} collective-permute-done((bf16[512,128]{1,0:T(8,128)(2,1)S(1)}, bf16[512,128]{1,0:T(8,128)(2,1)S(1)}, u32[]{:S(2)}, u32[]{:S(2)}) %collective-permute-start.12) | collective-permute-done | bytes 131104 | tf_op jit(solution)/shard_map/ppermute | solution.py:46
  36.5 0.8 %place.2.refs_1_ = bf16[2048,128]{1,0:T(8,128)(2,1)} custom-call(bf16[512,128]{1,0:T(8,128)(2,1)S(1)} %collective-permute-done.11.refs_0_, bf16[512,128]{1,0:T(8,128)(2,1)S(1)} %collective-permute-done.12.refs_1_, bf16[512,128]{1,0:T(8,128)(2,1)S(1)} %merge.7.refs_2_), custom_call_target="tpu_custom_call" | custom-call | tf_op jit(solution)/shard_map/place/pallas_call | solution.py:278
  37.8 0.7 %place.3 = bf16[2048,128]{1,0:T(8,128)(2,1)} custom-call(bf16[512,128]{1,0:T(8,128)(2,1)S(1)} %collective-permute-done.10.refs_0_, bf16[2048,128]{1,0:T(8,128)(2,1)} %place.2.refs_1_), custom_call_target="tpu_custom_call", output_to_operand_aliasing={{}: (1, {})} | custom-call | tf_op jit(solution)/shard_map/place/pallas_call | solution.py:278
  (36 shorter events, 4.6 us)
Async XLA Ops:
  0.0 7.6 %collective-permute-start.2 = (bf16[2048,128]{1,0:T(8,128)(2,1)}, bf16[2048,128]{1,0:T(8,128)(2,1)S(1)}, u32[]{:S(2)}, u32[]{:S(2)}) collective-permute-start(bf16[2048,128]{1,0:T(8,128)(2,1)} %source.1), channel_id=1, source_target_pairs={{0,1},{1,0},{2,3},{3,2},{4,5},{5,4},{6,7},{7,6},{8,9},{9,8},{10,11... | collective-permute-start | bytes 1572872 | tf_op jit(solution)/shard_map/ppermute | solution.py:33
  0.5 6.2 %collective-permute-start.1 = (s32[1,4]{1,0:T(1,128)}, s32[1,4]{1,0:T(1,128)S(1)}, u32[]{:S(2)}, u32[]{:S(2)}) collective-permute-start(s32[1,4]{1,0:T(1,128)} %refs_2_.2), channel_id=1, source_target_pairs={{0,2},{1,3},{2,0},{3,1},{4,6},{5,7},{6,4},{7,5},{8,10},{9,11},{10,... | collective-permute-start | bytes 56 | tf_op jit(solution)/shard_map/ppermute | solution.py:33
  3.0 4.6 %collective-permute-start = (s32[1,4]{1,0:T(1,128)}, s32[1,4]{1,0:T(1,128)S(1)}, u32[]{:S(2)}, u32[]{:S(2)}) collective-permute-start(s32[1,4]{1,0:T(1,128)} %refs_2_.2), channel_id=1, source_target_pairs={{0,4},{1,5},{2,6},{3,7},{4,0},{5,1},{6,2},{7,3},{8,12},{9,13},{10,... | collective-permute-start | bytes 56 | tf_op jit(solution)/shard_map/ppermute | solution.py:33
  5.6 6.3 %collective-permute-start.5 = (s32[1,4]{1,0:T(1,128)}, s32[1,4]{1,0:T(1,128)S(1)}, u32[]{:S(2)}, u32[]{:S(2)}) collective-permute-start(s32[1,4]{1,0:T(1,128)} %refs_2_.2), channel_id=1, source_target_pairs={{0,6},{1,7},{2,4},{3,5},{4,2},{5,3},{6,0},{7,1},{8,14},{9,15},{10,... | collective-permute-start | bytes 56 | tf_op jit(solution)/shard_map/ppermute | solution.py:33
  8.4 8.2 %collective-permute-start.3 = (bf16[128,128]{1,0:T(8,128)(2,1)S(1)}, bf16[128,128]{1,0:T(8,128)(2,1)S(1)}, u32[]{:S(2)}, u32[]{:S(2)}) collective-permute-start(bf16[128,128]{1,0:T(8,128)(2,1)S(1)} %get-tuple-element.12), channel_id=1, source_target_pairs={{0,2},{1,3},{2,0},{3,1},{4,6},{5,7},{6,4},{7,5},{8,10},{9,11},{10,... | collective-permute-start | bytes 98312 | tf_op jit(solution)/shard_map/ppermute | solution.py:33
  8.6 8.0 %collective-permute-start.4 = (bf16[128,128]{1,0:T(8,128)(2,1)S(1)}, bf16[128,128]{1,0:T(8,128)(2,1)S(1)}, u32[]{:S(2)}, u32[]{:S(2)}) collective-permute-start(bf16[128,128]{1,0:T(8,128)(2,1)S(1)} %get-tuple-element.13), channel_id=1, source_target_pairs={{0,4},{1,5},{2,6},{3,7},{4,0},{5,1},{6,2},{7,3},{8,12},{9,13},{10,... | collective-permute-start | bytes 98312 | tf_op jit(solution)/shard_map/ppermute | solution.py:33
  12.5 5.8 %collective-permute-start.6 = (bf16[128,128]{1,0:T(8,128)(2,1)S(1)}, bf16[128,128]{1,0:T(8,128)(2,1)S(1)}, u32[]{:S(2)}, u32[]{:S(2)}) collective-permute-start(bf16[128,128]{1,0:T(8,128)(2,1)S(1)} %serve.3), channel_id=1, source_target_pairs={{0,6},{1,7},{2,4},{3,5},{4,2},{5,3},{6,0},{7,1},{8,14},{9,15},{10,... | collective-permute-start | bytes 98312 | tf_op jit(solution)/shard_map/ppermute | solution.py:33
  16.5 6.3 %copy-start.4 = (bf16[128,128]{1,0:T(8,128)(2,1)S(1)}, bf16[128,128]{1,0:T(8,128)(2,1)}, u32[]{:S(2)}) copy-start(bf16[128,128]{1,0:T(8,128)(2,1)} %param.19) | copy-start | bytes 98308
  16.6 6.4 %copy-start.5 = (bf16[128,128]{1,0:T(8,128)(2,1)S(1)}, bf16[128,128]{1,0:T(8,128)(2,1)}, u32[]{:S(2)}) copy-start(bf16[128,128]{1,0:T(8,128)(2,1)} %param.20) | copy-start | bytes 98308
  16.6 6.5 %copy-start.6 = (bf16[128,128]{1,0:T(8,128)(2,1)S(1)}, bf16[128,128]{1,0:T(8,128)(2,1)}, u32[]{:S(2)}) copy-start(bf16[128,128]{1,0:T(8,128)(2,1)} %param.21) | copy-start | bytes 98308
  18.6 7.2 %collective-permute-start.9 = (bf16[512,128]{1,0:T(8,128)(2,1)S(1)}, bf16[512,128]{1,0:T(8,128)(2,1)S(1)}, u32[]{:S(2)}, u32[]{:S(2)}) collective-permute-start(bf16[512,128]{1,0:T(8,128)(2,1)S(1)} %spread.3), channel_id=1, source_target_pairs={{0,24},{1,25},{2,26},{3,27},{4,28},{5,29},{6,30},{7,31},{8,16},{9,... | collective-permute-start | bytes 393224 | tf_op jit(solution)/shard_map/ppermute | solution.py:46
  21.6 5.9 %copy-start = (bf16[128,512]{1,0:T(8,128)(2,1)S(1)}, bf16[128,512]{1,0:T(8,128)(2,1)}, u32[]{:S(2)}) copy-start(bf16[128,512]{1,0:T(8,128)(2,1)} %refs_7_.7) | copy-start | bytes 393220
  21.7 5.9 %copy-start.1 = (bf16[512,128]{1,0:T(8,128)(2,1)S(1)}, bf16[512,128]{1,0:T(8,128)(2,1)}, u32[]{:S(2)}) copy-start(bf16[512,128]{1,0:T(8,128)(2,1)} %refs_8_.7) | copy-start | bytes 393220
  21.7 5.9 %copy-start.2 = (bf16[128,128]{1,0:T(8,128)(2,1)S(1)}, bf16[128,128]{1,0:T(8,128)(2,1)}, u32[]{:S(2)}) copy-start(bf16[128,128]{1,0:T(8,128)(2,1)} %refs_5_.7) | copy-start | bytes 98308
  21.7 5.9 %copy-start.3 = (f32[128]{0:T(128)S(1)}, f32[128]{0:T(128)}, u32[]{:S(2)}) copy-start(f32[128]{0:T(128)} %param.23) | copy-start | bytes 1540
  21.7 5.3 %collective-permute-start.8 = (bf16[512,128]{1,0:T(8,128)(2,1)S(1)}, bf16[512,128]{1,0:T(8,128)(2,1)S(1)}, u32[]{:S(2)}, u32[]{:S(2)}) collective-permute-start(bf16[512,128]{1,0:T(8,128)(2,1)S(1)} %get-tuple-element.16), channel_id=1, source_target_pairs={{0,16},{1,17},{2,18},{3,19},{4,20},{5,21},{6,22},{7,23},{8,24},{9,... | collective-permute-start | bytes 393224 | tf_op jit(solution)/shard_map/ppermute | solution.py:46
  22.3 5.0 %collective-permute-start.7 = (bf16[512,128]{1,0:T(8,128)(2,1)S(1)}, bf16[512,128]{1,0:T(8,128)(2,1)S(1)}, u32[]{:S(2)}, u32[]{:S(2)}) collective-permute-start(bf16[512,128]{1,0:T(8,128)(2,1)S(1)} %get-tuple-element.14), channel_id=1, source_target_pairs={{0,8},{1,9},{2,10},{3,11},{4,12},{5,13},{6,14},{7,15},{8,0},{9,1},... | collective-permute-start | bytes 393224 | tf_op jit(solution)/shard_map/ppermute | solution.py:46
  28.4 7.4 %collective-permute-start.11 = (bf16[512,128]{1,0:T(8,128)(2,1)S(1)}, bf16[512,128]{1,0:T(8,128)(2,1)S(1)}, u32[]{:S(2)}, u32[]{:S(2)}) collective-permute-start(bf16[512,128]{1,0:T(8,128)(2,1)S(1)} %merge.5), channel_id=1, source_target_pairs={{0,24},{1,25},{2,26},{3,27},{4,28},{5,29},{6,30},{7,31},{8,16},{9,... | collective-permute-start | bytes 393224 | tf_op jit(solution)/shard_map/ppermute | solution.py:46
  30.9 5.7 %collective-permute-start.12 = (bf16[512,128]{1,0:T(8,128)(2,1)S(1)}, bf16[512,128]{1,0:T(8,128)(2,1)S(1)}, u32[]{:S(2)}, u32[]{:S(2)}) collective-permute-start(bf16[512,128]{1,0:T(8,128)(2,1)S(1)} %merge.6), channel_id=1, source_target_pairs={{0,16},{1,17},{2,18},{3,19},{4,20},{5,21},{6,22},{7,23},{8,24},{9,... | collective-permute-start | bytes 393224 | tf_op jit(solution)/shard_map/ppermute | solution.py:46
  32.8 5.0 %collective-permute-start.10 = (bf16[512,128]{1,0:T(8,128)(2,1)S(1)}, bf16[512,128]{1,0:T(8,128)(2,1)S(1)}, u32[]{:S(2)}, u32[]{:S(2)}) collective-permute-start(bf16[512,128]{1,0:T(8,128)(2,1)S(1)} %merge.4), channel_id=1, source_target_pairs={{0,8},{1,9},{2,10},{3,11},{4,12},{5,13},{6,14},{7,15},{8,0},{9,1},... | collective-permute-start | bytes 393224 | tf_op jit(solution)/shard_map/ppermute | solution.py:46

commit v5 on v4

--- a/solution.py
+++ b/solution.py
@@ -107,23 +107,27 @@
     )(*hbm(rows, cols), count, *hbm(tiles))
 
 
-def load_kernel(source, out, sem):
-    copy = pltpu.make_async_copy(source, out, sem)
-    copy.start()
-    copy.wait()
-
-
-def load(source):
+def load_kernel(*refs):
+    half = len(refs) // 2
+    sems = refs[-1]
+    copies = [pltpu.make_async_copy(refs[k], refs[half + k], sems.at[k]) for k in range(half)]
+    for copy in copies:
+        copy.start()
+    for copy in copies:
+        copy.wait()
+
+
+def load(*sources):
     return pl.pallas_call(
         load_kernel,
-        in_specs=[HBM],
-        out_specs=VMEM,
-        out_shape=jax.ShapeDtypeStruct(source.shape, source.dtype),
-        scratch_shapes=[pltpu.SemaphoreType.DMA],
-        compiler_params=params(),
-        cost_estimate=cost(0, source.size * 2),
+        in_specs=[HBM] * len(sources),
+        out_specs=[VMEM] * len(sources),
+        out_shape=[jax.ShapeDtypeStruct(s.shape, s.dtype) for s in sources],
+        scratch_shapes=[pltpu.SemaphoreType.DMA((len(sources),))],
+        compiler_params=params(),
+        cost_estimate=cost(0, sum(s.size * 2 for s in sources)),
         name="load",
-    )(*hbm(source))
+    )(*hbm(*sources))
 
 
 def serve_kernel(block_count, pairs, *refs):
@@ -152,7 +156,7 @@
             out[...] = other[pl.ds(start, TB), :]
 
 
-def serve(asks, own, other, block_count):
+def serve(asks, own, other, block_count, weight):
     pairs = len(asks)
     return pl.pallas_call(
         functools.partial(serve_kernel, block_count, pairs),
@@ -161,12 +165,34 @@
         out_shape=[jax.ShapeDtypeStruct((TB, own.shape[1]), own.dtype)] * pairs,
         scratch_shapes=[pltpu.SMEM(asks[0].shape, jnp.int32)] * pairs + [pltpu.SemaphoreType.DMA((pairs,))],
         compiler_params=params(),
+        cost_estimate=cost(weight, own.size),
         name="serve",
     )(*asks, own, other)
 
 
-def spread_kernel(pairs, which, parts, cells, *refs):
-    sources, own, outs = refs[:pairs], refs[pairs], refs[pairs + 1 :]
+def begin_kernel(pairs, columns, cells, *refs):
+    sources, own, out = refs[: len(columns)], refs[-2], refs[-1]
+    stack = jnp.concatenate([s[...] for s in sources], axis=0)
+    for r in range(own.shape[0] // TB):
+        rows = pl.ds(r * TB, TB)
+        lhs = jnp.concatenate([cells[r * pairs + m] for m in columns], axis=1)
+        out[rows, :] = own[rows, :].astype(F32) + jnp.dot(lhs, stack, preferred_element_type=F32)
+
+
+def begin_spread(cells, sources, columns, own, pairs):
+    return pl.pallas_call(
+        functools.partial(begin_kernel, pairs, columns),
+        in_specs=[VMEM] * (len(sources) + 2),
+        out_specs=VMEM,
+        out_shape=jax.ShapeDtypeStruct(own.shape, F32),
+        compiler_params=params(),
+        cost_estimate=cost(2 * own.size * TB * len(columns), own.size * 2),
+        name="begin",
+    )(cells, *sources, own)
+
+
+def spread_kernel(pairs, columns, which, parts, cells, *refs):
+    sources, begun, outs = refs[: len(columns)], refs[len(columns)], refs[len(columns) + 1 :]
     stack = jnp.concatenate([s[...] for s in sources], axis=0)
     size = outs[0].shape[0]
     for k, out in zip(which, outs):
@@ -174,22 +200,21 @@
         start = pl.multiple_of(part * size, size)
         block = part * (size // TB)
         for r in range(size // TB):
-            lhs = jnp.concatenate([cells[(block + r) * pairs + m] for m in range(pairs)], axis=1)
+            lhs = jnp.concatenate([cells[(block + r) * pairs + m] for m in columns], axis=1)
             total = jnp.dot(lhs, stack, preferred_element_type=F32)
-            rows = own[pl.ds(start + r * TB, TB), :].astype(F32)
-            out[r * TB : (r + 1) * TB, :] = (total + rows).astype(BF16)
-
-
-def spread_cells(cells, sources, own, which, parts):
-    size = own.shape[0] // parts
-    return pl.pallas_call(
-        functools.partial(spread_kernel, len(sources), which, parts),
+            out[r * TB : (r + 1) * TB, :] = (begun[pl.ds(start + r * TB, TB), :] + total).astype(BF16)
+
+
+def spread_cells(cells, sources, columns, begun, which, parts, pairs):
+    size = begun.shape[0] // parts
+    return pl.pallas_call(
+        functools.partial(spread_kernel, pairs, columns, which, parts),
         in_specs=[VMEM] * (len(sources) + 2),
         out_specs=[VMEM] * len(which),
-        out_shape=[jax.ShapeDtypeStruct((size, own.shape[1]), BF16)] * len(which),
+        out_shape=[jax.ShapeDtypeStruct((size, begun.shape[1]), BF16)] * len(which),
         compiler_params=params(),
         name="spread",
-    )(cells, *sources, own)
+    )(cells, *sources, begun)
 
 
 def project_kernel(w_qkv, x, *refs):
@@ -375,15 +400,17 @@
     tiles = adjacency[0]
     if pairs * block_count <= tiles.shape[0]:
         far = range(pairs - 1, 0, -1)
-        asks = [exchange(need_ids, "node", 2 * k) for k in far] + hbm(need_ids)
+        own, ids = load(embeddings, need_ids)
+        asks = [exchange(need_ids if k == pairs - 1 else ids, "node", 2 * k) for k in far] + [ids]
         other = exchange(embeddings, "node", 1)
-        own = load(embeddings)
         cells = sum_cells(tile_rows, tile_cols, tile_count, tiles, pairs, block_count)
-        served = serve(asks[:1], own, other, block_count)
-        *more, here = serve(asks[1:], own, other, block_count)
-        sources = [here] + [exchange(block, "node", 2 * k) for k, block in zip(far, [*served, *more])][::-1]
-        last = spread_cells(cells, sources, own, [parts - 1], parts)
-        quarters = spread_cells(cells, sources, own, list(range(parts - 1)), parts) + last
+        served = serve(asks[:1], own, other, block_count, 10**10)
+        *more, here = serve(asks[1:], own, other, block_count, 10**10)
+        first, *rest = [exchange(block, "node", 2 * k) for k, block in zip(far, [*served, *more])]
+        begun = begin_spread(cells, [first, here], [pairs - 1, 0], own, pairs)
+        arms = (cells, rest, list(far)[1:], begun)
+        last = spread_cells(*arms, [parts - 1], parts, pairs)
+        quarters = spread_cells(*arms, list(range(parts - 1)), parts, pairs) + last
     else:
         sources = fetch_many(embeddings, need_ids, block_count)
         spread = spread_tiles(tile_rows, tile_cols, tile_count, tiles, sources, embeddings)

time: 38.7 us -> 37.2 us (0.961)
  waiting for transfers between devices: 8.13 us -> 5.69 us
  starting transfers between devices: 17.4 us -> 18.4 us
    ppermute x7, waiting for transfers between devices: 2.6 us -> 0.02 us  [exchange(): return lax.ppermute(value, axis, pairs)]
    ppermute x7, starting transfers between devices: 10.1 us -> 11.1 us  [exchange(): return lax.ppermute(value, axis, pairs)]
    pallas_call x3 -> x4, Pallas kernels: 1.9 us -> 2.06 us  [the longest x1 1.06 us: load(): pl.pallas_call(load_kernel, in_specs=[HBM] * len(sources), out_specs=[VME...]
  transfers between devices with their start and end apart: 13 -> 13, of which waited for: 7 -> 5; matrix products, arithmetic and copies ran while one was open for 1% -> 1% of each run, Pallas kernels for 25% -> 26%
where the time goes in v5:
time: 37.2 us; the launch traced here: 37.1 us
  starting transfers between devices  18.4 us (49%)
  Pallas kernels  11.6 us (31%)
  waiting for transfers between devices  5.69 us (15%)
  between operations  0.92 us (2%)
  local copies, waits for them, and re-layouts  0.38 us (1%)
    ppermute x7, starting transfers between devices, exchange(): return lax.ppermute(value, axis, pairs)  11.1 us
    ppermute x6, starting transfers between devices, exchange_beh(): return lax.ppermute(value, ('beh', 'node'), pairs)  7.29 us
    ppermute x6, waiting for transfers between devices, exchange_beh(): return lax.ppermute(value, ('beh', 'node'), pairs)  5.67 us
    pallas_call x4, Pallas kernels, merge(): pl.pallas_call(functools.partial(merge_kernel, len(projected), which, til...  3.5 us
    pallas_call x1, Pallas kernels, sum_cells(): pl.pallas_call(functools.partial(cells_kernel, chunk, pairs, cell_count),...  2.43 us
    pallas_call x2, Pallas kernels, place_parts(): pl.pallas_call(functools.partial(place_kernel, which, parts), in_specs=[V...  1.43 us
    pallas_call x2, Pallas kernels, serve(): pl.pallas_call(functools.partial(serve_kernel, block_count, pairs), in_sp...  1.2 us
    pallas_call x1, Pallas kernels, load(): pl.pallas_call(load_kernel, in_specs=[HBM] * len(sources), out_specs=[VME...  1.06 us
  transfers between devices with their start and end apart: 13, of which 5 were waited for; matrix products, arithmetic and copies ran while one was open for 1% of the time, Pallas kernels for 26%

profile of v5, /device:TPU:0, one launch (start us, length us, event | category | flops | bytes accessed | tf_op | source)
XLA Modules:
  0.0 37.1 jit_solution(7065538262613948925)
XLA Ops:
  0.5 4.6 %collective-permute-start.5 = (s32[1,4]{1,0:T(1,128)}, s32[1,4]{1,0:T(1,128)S(1)}, u32[]{:S(2)}, u32[]{:S(2)}) collective-permute-start(s32[1,4]{1,0:T(1,128)} %refs_1_.3), channel_id=1, source_target_pairs={{0,6},{1,7},{2,4},{3,5},{4,2},{5,3},{6,0},{7,1},{8,14},{9,15},{10,... | collective-permute-start | bytes 56 | tf_op jit(solution)/shard_map/ppermute | solution.py:33
  5.1 1.1 %load.1 = (bf16[2048,128]{1,0:T(8,128)(2,1)S(1)}, s32[1,4]{1,0:T(1,128)S(1)}) custom-call(bf16[2048,128]{1,0:T(8,128)(2,1)} %refs_0_.3, s32[1,4]{1,0:T(1,128)} %refs_1_.3), custom_call_target="tpu_custom_call" | custom-call | bytes 524296 | tf_op jit(solution)/shard_map/load/pallas_call | solution.py:121
  6.2 0.6 %collective-permute-start = (s32[1,4]{1,0:T(1,128)S(1)}, s32[1,4]{1,0:T(1,128)S(1)}, u32[]{:S(2)}, u32[]{:S(2)}) collective-permute-start(s32[1,4]{1,0:T(1,128)S(1)} %get-tuple-element.13.refs_2_), channel_id=1, source_target_pairs={{0,4},{1,5},{2,6},{3,7},{4,0},{5,1},{6,2},{7,3},{8,12},{9,13},{10,... | collective-permute-start | bytes 56 | tf_op jit(solution)/shard_map/ppermute | solution.py:33
  6.8 0.6 %serve.3 = bf16[128,128]{1,0:T(8,128)(2,1)S(1)} custom-call(s32[1,4]{1,0:T(1,128)S(1)} %collective-permute-done.5.refs_0_, bf16[2048,128]{1,0:T(8,128)(2,1)S(1)} %get-tuple-element.14.refs_3_.refs_1_.refs_2_, bf16[2048,128]{1,0:T(8,128)(2,1)S(1)} %collective-permute-done.2.refs_4_.refs_2_), custom_call_target="tpu_custom_call" | custom-call | flops 10000000000 | bytes 262144 | tf_op jit(solution)/shard_map/serve/pallas_call | solution.py:161
  7.3 3.9 %collective-permute-start.6 = (bf16[128,128]{1,0:T(8,128)(2,1)S(1)}, bf16[128,128]{1,0:T(8,128)(2,1)S(1)}, u32[]{:S(2)}, u32[]{:S(2)}) collective-permute-start(bf16[128,128]{1,0:T(8,128)(2,1)S(1)} %serve.3), channel_id=1, source_target_pairs={{0,6},{1,7},{2,4},{3,5},{4,2},{5,3},{6,0},{7,1},{8,14},{9,15},{10,... | collective-permute-start | bytes 98312 | tf_op jit(solution)/shard_map/ppermute | solution.py:33
  11.2 0.6 %serve.2 = (bf16[128,128]{1,0:T(8,128)(2,1)S(1)}, bf16[128,128]{1,0:T(8,128)(2,1)S(1)}, bf16[128,128]{1,0:T(8,128)(2,1)S(1)}) custom-call(s32[1,4]{1,0:T(1,128)S(1)} %collective-permute-done.refs_0_, s32[1,4]{1,0:T(1,128)S(1)} %collective-permute-done.1.refs_1_, s32[1,4]{1,0:T(1,128)S(1)} %get-tuple-element.13.refs_2_, ...), custom_call_target="tpu_custom_call" | custom-call | flops 10000000000 | bytes 262144 | tf_op jit(solution)/shard_map/serve/pallas_call | solution.py:161
  11.9 1.5 %collective-permute-start.4 = (bf16[128,128]{1,0:T(8,128)(2,1)S(1)}, bf16[128,128]{1,0:T(8,128)(2,1)S(1)}, u32[]{:S(2)}, u32[]{:S(2)}) collective-permute-start(bf16[128,128]{1,0:T(8,128)(2,1)S(1)} %get-tuple-element.16), channel_id=1, source_target_pairs={{0,2},{1,3},{2,0},{3,1},{4,6},{5,7},{6,4},{7,5},{8,10},{9,11},{10,... | collective-permute-start | bytes 98312 | tf_op jit(solution)/shard_map/ppermute | solution.py:33
  14.1 2.4 %cells.1 = bf16[64,128,128]{2,1,0:T(8,128)(2,1)S(1)} custom-call(s32[1,112]{1,0:T(1,128)} %refs_0_.2, s32[1,112]{1,0:T(1,128)} %refs_1_.2, s32[1,1]{1,0:T(1,128)S(6)} %copy.19.refs_2_, bf16[112,128,128]{2,1,0:T(8,128)(2,1)} %bitcast.9), custom_call_target="tpu_custom_call" | custom-call | bytes 3670016 | tf_op jit(solution)/shard_map/cells/pallas_call | solution.py:92
  17.2 2.5 %collective-permute-start.9 = (bf16[512,128]{1,0:T(8,128)(2,1)S(1)}, bf16[512,128]{1,0:T(8,128)(2,1)S(1)}, u32[]{:S(2)}, u32[]{:S(2)}) collective-permute-start(bf16[512,128]{1,0:T(8,128)(2,1)S(1)} %spread.3), channel_id=1, source_target_pairs={{0,24},{1,25},{2,26},{3,27},{4,28},{5,29},{6,30},{7,31},{8,16},{9,... | collective-permute-start | bytes 393224 | tf_op jit(solution)/shard_map/ppermute | solution.py:46
  20.2 0.6 %collective-permute-start.8 = (bf16[512,128]{1,0:T(8,128)(2,1)S(1)}, bf16[512,128]{1,0:T(8,128)(2,1)S(1)}, u32[]{:S(2)}, u32[]{:S(2)}) collective-permute-start(bf16[512,128]{1,0:T(8,128)(2,1)S(1)} %get-tuple-element.20), channel_id=1, source_target_pairs={{0,16},{1,17},{2,18},{3,19},{4,20},{5,21},{6,22},{7,23},{8,24},{9,... | collective-permute-start | bytes 393224 | tf_op jit(solution)/shard_map/ppermute | solution.py:46
  21.9 2.3 %collective-permute-done.9.x.refs_0_ = bf16[512,128]{1,0:T(8,128)(2,1)S(1)} collective-permute-done((bf16[512,128]{1,0:T(8,128)(2,1)S(1)}, bf16[512,128]{1,0:T(8,128)(2,1)S(1)}, u32[]{:S(2)}, u32[]{:S(2)}) %collective-permute-start.9) | collective-permute-done | bytes 131104 | tf_op jit(solution)/shard_map/ppermute | solution.py:46
  24.4 0.9 %collective-permute-done.8.x.refs_0_ = bf16[512,128]{1,0:T(8,128)(2,1)S(1)} collective-permute-done((bf16[512,128]{1,0:T(8,128)(2,1)S(1)}, bf16[512,128]{1,0:T(8,128)(2,1)S(1)}, u32[]{:S(2)}, u32[]{:S(2)}) %collective-permute-start.8) | collective-permute-done | bytes 131104 | tf_op jit(solution)/shard_map/ppermute | solution.py:46
  26.0 0.9 %merge.5 = bf16[512,128]{1,0:T(8,128)(2,1)S(1)} custom-call(bf16[512,128]{1,0:T(8,128)(2,1)S(1)} %collective-permute-done.9.x.refs_0_, f32[384,512]{1,0:T(8,128)S(1)} %project.4.refs_0_.refs_1_, f32[384,512]{1,0:T(8,128)S(1)} %project.6.refs_0_.refs_2_, f32[384,512]{1,0:T(8,128)S(1)} %project.7.refs_3_, f32[384,512]{1,0:T(8,128)S(1)} %project.5.refs_0_.refs_4_, ...), custom_call_target="tpu_custom_call" | custom-call | flops 268435456 | bytes 65536 | tf_op jit(solution)/shard_map/merge/pallas_call | solution.py:278
  26.9 1.8 %collective-permute-start.11 = (bf16[512,128]{1,0:T(8,128)(2,1)S(1)}, bf16[512,128]{1,0:T(8,128)(2,1)S(1)}, u32[]{:S(2)}, u32[]{:S(2)}) collective-permute-start(bf16[512,128]{1,0:T(8,128)(2,1)S(1)} %merge.5), channel_id=1, source_target_pairs={{0,24},{1,25},{2,26},{3,27},{4,28},{5,29},{6,30},{7,31},{8,16},{9,... | collective-permute-start | bytes 393224 | tf_op jit(solution)/shard_map/ppermute | solution.py:46
  28.7 0.9 %merge.6 = bf16[512,128]{1,0:T(8,128)(2,1)S(1)} custom-call(bf16[512,128]{1,0:T(8,128)(2,1)S(1)} %collective-permute-done.8.x.refs_0_, f32[384,512]{1,0:T(8,128)S(1)} %project.4.refs_0_.refs_1_, f32[384,512]{1,0:T(8,128)S(1)} %project.6.refs_0_.refs_2_, f32[384,512]{1,0:T(8,128)S(1)} %project.7.refs_3_, f32[384,512]{1,0:T(8,128)S(1)} %project.5.refs_0_.refs_4_, ...), custom_call_target="tpu_custom_call" | custom-call | flops 268435456 | bytes 65536 | tf_op jit(solution)/shard_map/merge/pallas_call | solution.py:278
  29.6 0.9 %collective-permute-start.12 = (bf16[512,128]{1,0:T(8,128)(2,1)S(1)}, bf16[512,128]{1,0:T(8,128)(2,1)S(1)}, u32[]{:S(2)}, u32[]{:S(2)}) collective-permute-start(bf16[512,128]{1,0:T(8,128)(2,1)S(1)} %merge.6), channel_id=1, source_target_pairs={{0,16},{1,17},{2,18},{3,19},{4,20},{5,21},{6,22},{7,23},{8,24},{9,... | collective-permute-start | bytes 393224 | tf_op jit(solution)/shard_map/ppermute | solution.py:46
  30.5 0.9 %merge.4 = bf16[512,128]{1,0:T(8,128)(2,1)S(1)} custom-call(bf16[512,128]{1,0:T(8,128)(2,1)S(1)} %collective-permute-done.7.x.refs_0_, f32[384,512]{1,0:T(8,128)S(1)} %project.4.refs_0_.refs_1_, f32[384,512]{1,0:T(8,128)S(1)} %project.6.refs_0_.refs_2_, f32[384,512]{1,0:T(8,128)S(1)} %project.7.refs_3_, f32[384,512]{1,0:T(8,128)S(1)} %project.5.refs_0_.refs_4_, ...), custom_call_target="tpu_custom_call" | custom-call | flops 268435456 | bytes 65536 | tf_op jit(solution)/shard_map/merge/pallas_call | solution.py:278
  31.4 1.0 %collective-permute-start.10 = (bf16[512,128]{1,0:T(8,128)(2,1)S(1)}, bf16[512,128]{1,0:T(8,128)(2,1)S(1)}, u32[]{:S(2)}, u32[]{:S(2)}) collective-permute-start(bf16[512,128]{1,0:T(8,128)(2,1)S(1)} %merge.4), channel_id=1, source_target_pairs={{0,8},{1,9},{2,10},{3,11},{4,12},{5,13},{6,14},{7,15},{8,0},{9,1},... | collective-permute-start | bytes 393224 | tf_op jit(solution)/shard_map/ppermute | solution.py:46
  32.3 0.9 %merge.7.refs_2_ = bf16[512,128]{1,0:T(8,128)(2,1)S(1)} custom-call(bf16[512,128]{1,0:T(8,128)(2,1)S(1)} %get-tuple-element.19.x.refs_0_, f32[384,512]{1,0:T(8,128)S(1)} %project.4.refs_0_.refs_1_, f32[384,512]{1,0:T(8,128)S(1)} %project.6.refs_0_.refs_2_, f32[384,512]{1,0:T(8,128)S(1)} %project.7.refs_3_, f32[384,512]{1,0:T(8,128)S(1)} %project.5.refs_0_.refs_4_, ...), custom_call_target="tpu_custom_call" | custom-call | flops 268435456 | bytes 65536 | tf_op jit(solution)/shard_map/merge/pallas_call | solution.py:278
  33.2 0.6 %collective-permute-done.11.refs_0_ = bf16[512,128]{1,0:T(8,128)(2,1)S(1)} collective-permute-done((bf16[512,128]{1,0:T(8,128)(2,1)S(1)}, bf16[512,128]{1,0:T(8,128)(2,1)S(1)}, u32[]{:S(2)}, u32[]{:S(2)}) %collective-permute-start.11) | collective-permute-done | bytes 131104 | tf_op jit(solution)/shard_map/ppermute | solution.py:46
  33.8 1.1 %collective-permute-done.12.refs_1_ = bf16[512,128]{1,0:T(8,128)(2,1)S(1)} collective-permute-done((bf16[512,128]{1,0:T(8,128)(2,1)S(1)}, bf16[512,128]{1,0:T(8,128)(2,1)S(1)}, u32[]{:S(2)}, u32[]{:S(2)}) %collective-permute-start.12) | collective-permute-done | bytes 131104 | tf_op jit(solution)/shard_map/ppermute | solution.py:46
  34.9 0.8 %place.2.refs_1_ = bf16[2048,128]{1,0:T(8,128)(2,1)} custom-call(bf16[512,128]{1,0:T(8,128)(2,1)S(1)} %collective-permute-done.11.refs_0_, bf16[512,128]{1,0:T(8,128)(2,1)S(1)} %collective-permute-done.12.refs_1_, bf16[512,128]{1,0:T(8,128)(2,1)S(1)} %merge.7.refs_2_), custom_call_target="tpu_custom_call" | custom-call | tf_op jit(solution)/shard_map/place/pallas_call | solution.py:303
  35.7 0.7 %collective-permute-done.10.refs_0_ = bf16[512,128]{1,0:T(8,128)(2,1)S(1)} collective-permute-done((bf16[512,128]{1,0:T(8,128)(2,1)S(1)}, bf16[512,128]{1,0:T(8,128)(2,1)S(1)}, u32[]{:S(2)}, u32[]{:S(2)}) %collective-permute-start.10) | collective-permute-done | bytes 131104 | tf_op jit(solution)/shard_map/ppermute | solution.py:46
  36.4 0.7 %place.3 = bf16[2048,128]{1,0:T(8,128)(2,1)} custom-call(bf16[512,128]{1,0:T(8,128)(2,1)S(1)} %collective-permute-done.10.refs_0_, bf16[2048,128]{1,0:T(8,128)(2,1)} %place.2.refs_1_), custom_call_target="tpu_custom_call", output_to_operand_aliasing={{}: (1, {})} | custom-call | tf_op jit(solution)/shard_map/place/pallas_call | solution.py:303
  (37 shorter events, 3.6 us)
Async XLA Ops:
  0.0 6.8 %collective-permute-start.2 = (bf16[2048,128]{1,0:T(8,128)(2,1)}, bf16[2048,128]{1,0:T(8,128)(2,1)S(1)}, u32[]{:S(2)}, u32[]{:S(2)}) collective-permute-start(bf16[2048,128]{1,0:T(8,128)(2,1)} %refs_0_.3), channel_id=1, source_target_pairs={{0,1},{1,0},{2,3},{3,2},{4,5},{5,4},{6,7},{7,6},{8,9},{9,8},{10,11... | collective-permute-start | bytes 1572872 | tf_op jit(solution)/shard_map/ppermute | solution.py:33
  0.5 6.3 %collective-permute-start.5 = (s32[1,4]{1,0:T(1,128)}, s32[1,4]{1,0:T(1,128)S(1)}, u32[]{:S(2)}, u32[]{:S(2)}) collective-permute-start(s32[1,4]{1,0:T(1,128)} %refs_1_.3), channel_id=1, source_target_pairs={{0,6},{1,7},{2,4},{3,5},{4,2},{5,3},{6,0},{7,1},{8,14},{9,15},{10,... | collective-permute-start | bytes 56 | tf_op jit(solution)/shard_map/ppermute | solution.py:33
  6.1 5.1 %collective-permute-start.1 = (s32[1,4]{1,0:T(1,128)S(1)}, s32[1,4]{1,0:T(1,128)S(1)}, u32[]{:S(2)}, u32[]{:S(2)}) collective-permute-start(s32[1,4]{1,0:T(1,128)S(1)} %get-tuple-element.13.refs_2_), channel_id=1, source_target_pairs={{0,2},{1,3},{2,0},{3,1},{4,6},{5,7},{6,4},{7,5},{8,10},{9,11},{10,... | collective-permute-start | bytes 56 | tf_op jit(solution)/shard_map/ppermute | solution.py:33
  6.2 5.0 %collective-permute-start = (s32[1,4]{1,0:T(1,128)S(1)}, s32[1,4]{1,0:T(1,128)S(1)}, u32[]{:S(2)}, u32[]{:S(2)}) collective-permute-start(s32[1,4]{1,0:T(1,128)S(1)} %get-tuple-element.13.refs_2_), channel_id=1, source_target_pairs={{0,4},{1,5},{2,6},{3,7},{4,0},{5,1},{6,2},{7,3},{8,12},{9,13},{10,... | collective-permute-start | bytes 56 | tf_op jit(solution)/shard_map/ppermute | solution.py:33
  7.3 9.2 %collective-permute-start.6 = (bf16[128,128]{1,0:T(8,128)(2,1)S(1)}, bf16[128,128]{1,0:T(8,128)(2,1)S(1)}, u32[]{:S(2)}, u32[]{:S(2)}) collective-permute-start(bf16[128,128]{1,0:T(8,128)(2,1)S(1)} %serve.3), channel_id=1, source_target_pairs={{0,6},{1,7},{2,4},{3,5},{4,2},{5,3},{6,0},{7,1},{8,14},{9,15},{10,... | collective-permute-start | bytes 98312 | tf_op jit(solution)/shard_map/ppermute | solution.py:33
  11.9 5.1 %collective-permute-start.3 = (bf16[128,128]{1,0:T(8,128)(2,1)S(1)}, bf16[128,128]{1,0:T(8,128)(2,1)S(1)}, u32[]{:S(2)}, u32[]{:S(2)}) collective-permute-start(bf16[128,128]{1,0:T(8,128)(2,1)S(1)} %get-tuple-element.15), channel_id=1, source_target_pairs={{0,4},{1,5},{2,6},{3,7},{4,0},{5,1},{6,2},{7,3},{8,12},{9,13},{10,... | collective-permute-start | bytes 98312 | tf_op jit(solution)/shard_map/ppermute | solution.py:33
  11.9 5.1 %collective-permute-start.4 = (bf16[128,128]{1,0:T(8,128)(2,1)S(1)}, bf16[128,128]{1,0:T(8,128)(2,1)S(1)}, u32[]{:S(2)}, u32[]{:S(2)}) collective-permute-start(bf16[128,128]{1,0:T(8,128)(2,1)S(1)} %get-tuple-element.16), channel_id=1, source_target_pairs={{0,2},{1,3},{2,0},{3,1},{4,6},{5,7},{6,4},{7,5},{8,10},{9,11},{10,... | collective-permute-start | bytes 98312 | tf_op jit(solution)/shard_map/ppermute | solution.py:33
  17.0 4.3 %copy-start.4 = (bf16[128,128]{1,0:T(8,128)(2,1)S(1)}, bf16[128,128]{1,0:T(8,128)(2,1)}, u32[]{:S(2)}) copy-start(bf16[128,128]{1,0:T(8,128)(2,1)} %param.19) | copy-start | bytes 98308
  17.0 4.4 %copy-start.5 = (bf16[128,128]{1,0:T(8,128)(2,1)S(1)}, bf16[128,128]{1,0:T(8,128)(2,1)}, u32[]{:S(2)}) copy-start(bf16[128,128]{1,0:T(8,128)(2,1)} %param.20) | copy-start | bytes 98308
  17.0 4.5 %copy-start.6 = (bf16[128,128]{1,0:T(8,128)(2,1)S(1)}, bf16[128,128]{1,0:T(8,128)(2,1)}, u32[]{:S(2)}) copy-start(bf16[128,128]{1,0:T(8,128)(2,1)} %param.21) | copy-start | bytes 98308
  17.2 6.9 %collective-permute-start.9 = (bf16[512,128]{1,0:T(8,128)(2,1)S(1)}, bf16[512,128]{1,0:T(8,128)(2,1)S(1)}, u32[]{:S(2)}, u32[]{:S(2)}) collective-permute-start(bf16[512,128]{1,0:T(8,128)(2,1)S(1)} %spread.3), channel_id=1, source_target_pairs={{0,24},{1,25},{2,26},{3,27},{4,28},{5,29},{6,30},{7,31},{8,16},{9,... | collective-permute-start | bytes 393224 | tf_op jit(solution)/shard_map/ppermute | solution.py:46
  20.1 5.9 %copy-start = (bf16[128,512]{1,0:T(8,128)(2,1)S(1)}, bf16[128,512]{1,0:T(8,128)(2,1)}, u32[]{:S(2)}) copy-start(bf16[128,512]{1,0:T(8,128)(2,1)} %refs_7_.7) | copy-start | bytes 393220
  20.1 5.8 %copy-start.1 = (bf16[512,128]{1,0:T(8,128)(2,1)S(1)}, bf16[512,128]{1,0:T(8,128)(2,1)}, u32[]{:S(2)}) copy-start(bf16[512,128]{1,0:T(8,128)(2,1)} %refs_8_.7) | copy-start | bytes 393220
  20.1 5.8 %copy-start.2 = (bf16[128,128]{1,0:T(8,128)(2,1)S(1)}, bf16[128,128]{1,0:T(8,128)(2,1)}, u32[]{:S(2)}) copy-start(bf16[128,128]{1,0:T(8,128)(2,1)} %refs_5_.7) | copy-start | bytes 98308
  20.2 5.8 %copy-start.3 = (f32[128]{0:T(128)S(1)}, f32[128]{0:T(128)}, u32[]{:S(2)}) copy-start(f32[128]{0:T(128)} %param.23) | copy-start | bytes 1540
  20.2 5.2 %collective-permute-start.8 = (bf16[512,128]{1,0:T(8,128)(2,1)S(1)}, bf16[512,128]{1,0:T(8,128)(2,1)S(1)}, u32[]{:S(2)}, u32[]{:S(2)}) collective-permute-start(bf16[512,128]{1,0:T(8,128)(2,1)S(1)} %get-tuple-element.20), channel_id=1, source_target_pairs={{0,16},{1,17},{2,18},{3,19},{4,20},{5,21},{6,22},{7,23},{8,24},{9,... | collective-permute-start | bytes 393224 | tf_op jit(solution)/shard_map/ppermute | solution.py:46
  20.7 5.0 %collective-permute-start.7 = (bf16[512,128]{1,0:T(8,128)(2,1)S(1)}, bf16[512,128]{1,0:T(8,128)(2,1)S(1)}, u32[]{:S(2)}, u32[]{:S(2)}) collective-permute-start(bf16[512,128]{1,0:T(8,128)(2,1)S(1)} %get-tuple-element.18), channel_id=1, source_target_pairs={{0,8},{1,9},{2,10},{3,11},{4,12},{5,13},{6,14},{7,15},{8,0},{9,1},... | collective-permute-start | bytes 393224 | tf_op jit(solution)/shard_map/ppermute | solution.py:46
  26.9 6.9 %collective-permute-start.11 = (bf16[512,128]{1,0:T(8,128)(2,1)S(1)}, bf16[512,128]{1,0:T(8,128)(2,1)S(1)}, u32[]{:S(2)}, u32[]{:S(2)}) collective-permute-start(bf16[512,128]{1,0:T(8,128)(2,1)S(1)} %merge.5), channel_id=1, source_target_pairs={{0,24},{1,25},{2,26},{3,27},{4,28},{5,29},{6,30},{7,31},{8,16},{9,... | collective-permute-start | bytes 393224 | tf_op jit(solution)/shard_map/ppermute | solution.py:46
  29.6 5.3 %collective-permute-start.12 = (bf16[512,128]{1,0:T(8,128)(2,1)S(1)}, bf16[512,128]{1,0:T(8,128)(2,1)S(1)}, u32[]{:S(2)}, u32[]{:S(2)}) collective-permute-start(bf16[512,128]{1,0:T(8,128)(2,1)S(1)} %merge.6), channel_id=1, source_target_pairs={{0,16},{1,17},{2,18},{3,19},{4,20},{5,21},{6,22},{7,23},{8,24},{9,... | collective-permute-start | bytes 393224 | tf_op jit(solution)/shard_map/ppermute | solution.py:46
  31.4 5.0 %collective-permute-start.10 = (bf16[512,128]{1,0:T(8,128)(2,1)S(1)}, bf16[512,128]{1,0:T(8,128)(2,1)S(1)}, u32[]{:S(2)}, u32[]{:S(2)}) collective-permute-start(bf16[512,128]{1,0:T(8,128)(2,1)S(1)} %merge.4), channel_id=1, source_target_pairs={{0,8},{1,9},{2,10},{3,11},{4,12},{5,13},{6,14},{7,15},{8,0},{9,1},... | collective-permute-start | bytes 393224 | tf_op jit(solution)/shard_map/ppermute | solution.py:46

commit v6 on v5

--- a/solution.py
+++ b/solution.py
@@ -59,9 +59,11 @@
     return pl.CostEstimate(flops=flops, bytes_accessed=moved, transcendentals=0)
 
 
-def cells_kernel(chunk, pairs, cell_count, *refs):
-    rows, cols, count, tiles, out, total, held, row_list, col_list, sems = refs
+def cells_kernel(chunk, pairs, columns, rows, cols, count, tiles, *refs):
+    sources, refs = refs[: len(columns)], refs[len(columns) :]
+    own, out, begun, total, held, row_list, col_list, sems = refs
     steps = tiles.shape[0] // chunk
+    block_count = own.shape[0] // TB
     here = lax.axis_index("node") // 2
     lists = [
         pltpu.make_async_copy(source, target, sems.at[steps + k])
@@ -70,32 +72,48 @@
     loads = [
         pltpu.make_async_copy(tiles.at[pl.ds(s * chunk, chunk)], held.at[s], sems.at[s]) for s in range(steps)
     ]
-    for copy in lists + loads:
+    for copy in lists:
         copy.start()
+    for step, load in enumerate(loads):
+        pl.when(step * chunk < count[0, 0])(load.start)
     total[...] = jnp.zeros_like(total)
     for copy in lists:
         copy.wait()
     for step, load in enumerate(loads):
-        load.wait()
-        for i in range(chunk):
-            slot = step * chunk + i
-            cell = row_list[0, slot] * pairs + (col_list[0, slot] ^ here)
-            cell = jnp.where(slot < count[0, 0], cell, cell_count)
-            total[cell] += held[step, i].astype(F32)
-    out[...] = total[:cell_count].astype(BF16)
-
-
-def sum_cells(rows, cols, count, tiles, pairs, block_count):
+
+        @pl.when(step * chunk < count[0, 0])
+        def _():
+            load.wait()
+            for i in range(chunk):
+                slot = step * chunk + i
+                cell = row_list[0, slot] * pairs + (col_list[0, slot] ^ here)
+                cell = jnp.where(slot < count[0, 0], cell, block_count * pairs)
+                total[cell] += held[step, i].astype(F32)
+
+    stack = jnp.concatenate([s[...] for s in sources], axis=0)
+    others = [m for m in range(pairs) if m not in columns]
+    for r in range(block_count):
+        rows_of = pl.ds(r * TB, TB)
+        lhs = jnp.concatenate([total[r * pairs + m].astype(BF16) for m in columns], axis=1)
+        begun[rows_of, :] = own[rows_of, :].astype(F32) + jnp.dot(lhs, stack, preferred_element_type=F32)
+        for k, m in enumerate(others):
+            out[r * len(others) + k] = total[r * pairs + m].astype(BF16)
+
+
+def begin_spread(rows, cols, count, tiles, sources, columns, own, pairs):
     slots = tiles.shape[0]
     chunk = math.gcd(slots, 16)
-    cell_count = pairs * block_count
-    return pl.pallas_call(
-        functools.partial(cells_kernel, chunk, pairs, cell_count),
-        in_specs=[HBM, HBM, SMEM, HBM],
-        out_specs=VMEM,
-        out_shape=jax.ShapeDtypeStruct((cell_count, TB, TB), BF16),
+    block_count = own.shape[0] // TB
+    return pl.pallas_call(
+        functools.partial(cells_kernel, chunk, pairs, columns),
+        in_specs=[HBM, HBM, SMEM, HBM] + [VMEM] * (len(sources) + 1),
+        out_specs=[VMEM] * 2,
+        out_shape=[
+            jax.ShapeDtypeStruct((block_count * (pairs - len(columns)), TB, TB), BF16),
+            jax.ShapeDtypeStruct(own.shape, F32),
+        ],
         scratch_shapes=[
-            pltpu.VMEM((cell_count + 1, TB, TB), F32),
+            pltpu.VMEM((block_count * pairs + 1, TB, TB), F32),
             pltpu.VMEM((slots // chunk, chunk, TB, TB), BF16),
             pltpu.SMEM(rows.shape, jnp.int32),
             pltpu.SMEM(cols.shape, jnp.int32),
@@ -104,7 +122,7 @@
         compiler_params=params(),
         cost_estimate=cost(0, tiles.size * 2),
         name="cells",
-    )(*hbm(rows, cols), count, *hbm(tiles))
+    )(*hbm(rows, cols), count, *hbm(tiles), *sources, own)
 
 
 def load_kernel(*refs):
@@ -131,19 +149,14 @@
 
 
 def serve_kernel(block_count, pairs, *refs):
-    asks, (own, other), outs = refs[:pairs], refs[pairs : pairs + 2], refs[pairs + 2 : 2 * pairs + 2]
-    lists, sems = refs[2 * pairs + 2 : -1], refs[-1]
+    asks, (own, other), outs = refs[:pairs], refs[pairs : pairs + 2], refs[pairs + 2 :]
     here = lax.axis_index("node") // 2
     core = lax.axis_index("node") % 2
-    copies = [
-        pltpu.make_async_copy(ask, target, sems.at[k]) for k, (ask, target) in enumerate(zip(asks, lists))
-    ]
-    for copy in copies:
-        copy.start()
-    for copy in copies:
-        copy.wait()
-    for k, out in enumerate(outs):
-        block = lists[k][0, here] - 2 * here * block_count
+    blocks = []
+    for ask in asks:
+        lanes = lax.broadcasted_iota(jnp.int32, ask.shape, 1)
+        blocks.append(jnp.sum(jnp.where(lanes == here, ask[...], 0)) - 2 * here * block_count)
+    for block, out in zip(blocks, outs):
         upper = (block >= block_count).astype(jnp.int32)
         start = pl.multiple_of((block - upper * block_count) * TB, TB)
 
@@ -160,55 +173,33 @@
     pairs = len(asks)
     return pl.pallas_call(
         functools.partial(serve_kernel, block_count, pairs),
-        in_specs=[ANY] * pairs + [VMEM] * 2,
+        in_specs=[VMEM] * (pairs + 2),
         out_specs=[VMEM] * pairs,
         out_shape=[jax.ShapeDtypeStruct((TB, own.shape[1]), own.dtype)] * pairs,
-        scratch_shapes=[pltpu.SMEM(asks[0].shape, jnp.int32)] * pairs + [pltpu.SemaphoreType.DMA((pairs,))],
         compiler_params=params(),
         cost_estimate=cost(weight, own.size),
         name="serve",
     )(*asks, own, other)
 
 
-def begin_kernel(pairs, columns, cells, *refs):
-    sources, own, out = refs[: len(columns)], refs[-2], refs[-1]
-    stack = jnp.concatenate([s[...] for s in sources], axis=0)
-    for r in range(own.shape[0] // TB):
-        rows = pl.ds(r * TB, TB)
-        lhs = jnp.concatenate([cells[r * pairs + m] for m in columns], axis=1)
-        out[rows, :] = own[rows, :].astype(F32) + jnp.dot(lhs, stack, preferred_element_type=F32)
-
-
-def begin_spread(cells, sources, columns, own, pairs):
-    return pl.pallas_call(
-        functools.partial(begin_kernel, pairs, columns),
-        in_specs=[VMEM] * (len(sources) + 2),
-        out_specs=VMEM,
-        out_shape=jax.ShapeDtypeStruct(own.shape, F32),
-        compiler_params=params(),
-        cost_estimate=cost(2 * own.size * TB * len(columns), own.size * 2),
-        name="begin",
-    )(cells, *sources, own)
-
-
-def spread_kernel(pairs, columns, which, parts, cells, *refs):
-    sources, begun, outs = refs[: len(columns)], refs[len(columns)], refs[len(columns) + 1 :]
-    stack = jnp.concatenate([s[...] for s in sources], axis=0)
+def spread_kernel(columns, which, parts, cells, *refs):
+    sources, begun, outs = refs[:columns], refs[columns], refs[columns + 1 :]
+    stack = jnp.concatenate([s[...] for s in sources[::-1]], axis=0)
     size = outs[0].shape[0]
     for k, out in zip(which, outs):
         part = part_of(k, parts)
         start = pl.multiple_of(part * size, size)
         block = part * (size // TB)
         for r in range(size // TB):
-            lhs = jnp.concatenate([cells[(block + r) * pairs + m] for m in columns], axis=1)
+            lhs = jnp.concatenate([cells[(block + r) * columns + m] for m in range(columns)], axis=1)
             total = jnp.dot(lhs, stack, preferred_element_type=F32)
             out[r * TB : (r + 1) * TB, :] = (begun[pl.ds(start + r * TB, TB), :] + total).astype(BF16)
 
 
-def spread_cells(cells, sources, columns, begun, which, parts, pairs):
+def spread_cells(cells, sources, begun, which, parts):
     size = begun.shape[0] // parts
     return pl.pallas_call(
-        functools.partial(spread_kernel, pairs, columns, which, parts),
+        functools.partial(spread_kernel, len(sources), which, parts),
         in_specs=[VMEM] * (len(sources) + 2),
         out_specs=[VMEM] * len(which),
         out_shape=[jax.ShapeDtypeStruct((size, begun.shape[1]), BF16)] * len(which),
@@ -403,14 +394,13 @@
         own, ids = load(embeddings, need_ids)
         asks = [exchange(need_ids if k == pairs - 1 else ids, "node", 2 * k) for k in far] + [ids]
         other = exchange(embeddings, "node", 1)
-        cells = sum_cells(tile_rows, tile_cols, tile_count, tiles, pairs, block_count)
         served = serve(asks[:1], own, other, block_count, 10**10)
         *more, here = serve(asks[1:], own, other, block_count, 10**10)
         first, *rest = [exchange(block, "node", 2 * k) for k, block in zip(far, [*served, *more])]
-        begun = begin_spread(cells, [first, here], [pairs - 1, 0], own, pairs)
-        arms = (cells, rest, list(far)[1:], begun)
-        last = spread_cells(*arms, [parts - 1], parts, pairs)
-        quarters = spread_cells(*arms, list(range(parts - 1)), parts, pairs) + last
+        arrays = (tile_rows, tile_cols, tile_count, tiles)
+        cells, begun = begin_spread(*arrays, [first, here], [pairs - 1, 0], own, pairs)
+        last = spread_cells(cells, rest, begun, [parts - 1], parts)
+        quarters = spread_cells(cells, rest, begun, list(range(parts - 1)), parts) + last
     else:
         sources = fetch_many(embeddings, need_ids, block_count)
         spread = spread_tiles(tile_rows, tile_cols, tile_count, tiles, sources, embeddings)

time: 37.2 us -> 36.3 us (0.976)
  Pallas kernels: 11.6 us -> 9.94 us
  starting transfers between devices: 18.4 us -> 18.9 us
  waiting for transfers between devices: 5.69 us -> 6.13 us
    pallas_call x2, Pallas kernels: 1.2 us -> 0.31 us  [serve(): pl.pallas_call(functools.partial(serve_kernel, block_count, pairs), in_sp...]
    pallas_call x4 -> x3, Pallas kernels: 3.42 us -> 2.62 us  [the longest x1 2.05 us: begin_spread(): pl.pallas_call(functools.partial(cells_kernel, chunk, pairs, columns), in...]
    ppermute x7, starting transfers between devices: 11.1 us -> 11.6 us  [exchange(): return lax.ppermute(value, axis, pairs)]
  transfers between devices with their start and end apart: 13 -> 13, of which waited for: 5 -> 7; matrix products, arithmetic and copies ran while one was open for 1% -> 1% of each run, Pallas kernels for 26% -> 22%
where the time goes in v6:
time: 36.3 us
  starting transfers between devices  18.9 us (52%)
  Pallas kernels  9.94 us (27%)
  waiting for transfers between devices  6.13 us (17%)
  between operations  0.89 us (2%)
  local copies, waits for them, and re-layouts  0.38 us (1%)
    ppermute x7, starting transfers between devices, exchange(): return lax.ppermute(value, axis, pairs)  11.6 us
    ppermute x6, starting transfers between devices, exchange_beh(): return lax.ppermute(value, ('beh', 'node'), pairs)  7.38 us
    ppermute x6, waiting for transfers between devices, exchange_beh(): return lax.ppermute(value, ('beh', 'node'), pairs)  5.98 us
    pallas_call x4, Pallas kernels, merge(): pl.pallas_call(functools.partial(merge_kernel, len(projected), which, til...  3.49 us
    pallas_call x1, Pallas kernels, begin_spread(): pl.pallas_call(functools.partial(cells_kernel, chunk, pairs, columns), in...  2.05 us
    pallas_call x2, Pallas kernels, place_parts(): pl.pallas_call(functools.partial(place_kernel, which, parts), in_specs=[V...  1.43 us
    pallas_call x1, Pallas kernels, load(): pl.pallas_call(load_kernel, in_specs=[HBM] * len(sources), out_specs=[VME...  1.06 us
    pallas_call x4, Pallas kernels, project(): pl.pallas_call(project_kernel, in_specs=[VMEM] * (2 + len(before)), out_s...  1.03 us
  transfers between devices with their start and end apart: 13, of which 7 were waited for; matrix products, arithmetic and copies ran while one was open for 1% of the time, Pallas kernels for 22%

profile of v6, /device:TPU:0, one launch (start us, length us, event | category | flops | bytes accessed | tf_op | source)
XLA Modules:
  0.0 36.3 jit_solution(5150635247219220861)
XLA Ops:
  0.0 0.5 %collective-permute-start.1 = (bf16[2048,128]{1,0:T(8,128)(2,1)}, bf16[2048,128]{1,0:T(8,128)(2,1)S(1)}, u32[]{:S(2)}, u32[]{:S(2)}) collective-permute-start(bf16[2048,128]{1,0:T(8,128)(2,1)} %refs_0_.1), channel_id=1, source_target_pairs={{0,1},{1,0},{2,3},{3,2},{4,5},{5,4},{6,7},{7,6},{8,9},{9,8},{10,11... | collective-permute-start | bytes 1572872 | tf_op jit(solution)/shard_map/ppermute | solution.py:33
  0.5 4.6 %collective-permute-start = (s32[1,4]{1,0:T(1,128)}, s32[1,4]{1,0:T(1,128)S(1)}, u32[]{:S(2)}, u32[]{:S(2)}) collective-permute-start(s32[1,4]{1,0:T(1,128)} %refs_1_.1), channel_id=1, source_target_pairs={{0,6},{1,7},{2,4},{3,5},{4,2},{5,3},{6,0},{7,1},{8,14},{9,15},{10,... | collective-permute-start | bytes 56 | tf_op jit(solution)/shard_map/ppermute | solution.py:33
  5.1 1.1 %load.1 = (bf16[2048,128]{1,0:T(8,128)(2,1)S(1)}, s32[1,4]{1,0:T(1,128)S(1)}) custom-call(bf16[2048,128]{1,0:T(8,128)(2,1)} %refs_0_.1, s32[1,4]{1,0:T(1,128)} %refs_1_.1), custom_call_target="tpu_custom_call" | custom-call | bytes 524296 | tf_op jit(solution)/shard_map/load/pallas_call | solution.py:139
  6.2 0.6 %collective-permute-start.3 = (s32[1,4]{1,0:T(1,128)S(1)}, s32[1,4]{1,0:T(1,128)S(1)}, u32[]{:S(2)}, u32[]{:S(2)}) collective-permute-start(s32[1,4]{1,0:T(1,128)S(1)} %get-tuple-element.16.refs_2_), channel_id=1, source_target_pairs={{0,4},{1,5},{2,6},{3,7},{4,0},{5,1},{6,2},{7,3},{8,12},{9,13},{10,... | collective-permute-start | bytes 56 | tf_op jit(solution)/shard_map/ppermute | solution.py:33
  6.9 3.9 %collective-permute-start.2 = (bf16[128,128]{1,0:T(8,128)(2,1)S(1)}, bf16[128,128]{1,0:T(8,128)(2,1)S(1)}, u32[]{:S(2)}, u32[]{:S(2)}) collective-permute-start(bf16[128,128]{1,0:T(8,128)(2,1)S(1)} %serve.2), channel_id=1, source_target_pairs={{0,6},{1,7},{2,4},{3,5},{4,2},{5,3},{6,0},{7,1},{8,14},{9,15},{10,... | collective-permute-start | bytes 98312 | tf_op jit(solution)/shard_map/ppermute | solution.py:33
  11.0 0.5 %collective-permute-start.5 = (bf16[128,128]{1,0:T(8,128)(2,1)S(1)}, bf16[128,128]{1,0:T(8,128)(2,1)S(1)}, u32[]{:S(2)}, u32[]{:S(2)}) collective-permute-start(bf16[128,128]{1,0:T(8,128)(2,1)S(1)} %get-tuple-element.19), channel_id=1, source_target_pairs={{0,4},{1,5},{2,6},{3,7},{4,0},{5,1},{6,2},{7,3},{8,12},{9,13},{10,... | collective-permute-start | bytes 98312 | tf_op jit(solution)/shard_map/ppermute | solution.py:33
  11.4 1.5 %collective-permute-start.6 = (bf16[128,128]{1,0:T(8,128)(2,1)S(1)}, bf16[128,128]{1,0:T(8,128)(2,1)S(1)}, u32[]{:S(2)}, u32[]{:S(2)}) collective-permute-start(bf16[128,128]{1,0:T(8,128)(2,1)S(1)} %get-tuple-element.20), channel_id=1, source_target_pairs={{0,2},{1,3},{2,0},{3,1},{4,6},{5,7},{6,4},{7,5},{8,10},{9,11},{10,... | collective-permute-start | bytes 98312 | tf_op jit(solution)/shard_map/ppermute | solution.py:33
  13.7 2.1 %cells.1 = (bf16[32,128,128]{2,1,0:T(8,128)(2,1)S(1)}, f32[2048,128]{1,0:T(8,128)S(1)}) custom-call(s32[1,112]{1,0:T(1,128)} %rows.1, s32[1,112]{1,0:T(1,128)} %cols.1, s32[1,1]{1,0:T(1,128)S(6)} %copy.19.count, bf16[112,128,128]{2,1,0:T(8,128)(2,1)} %bitcast.9, bf16[128,128]{1,0:T(8,128)(2,1)S(1)} %collective-permute-done.2.refs_0_, ...), custom_call_target="tpu_custom_call" | custom-call | bytes 3670016 | tf_op jit(solution)/shard_map/cells/pallas_call | solution.py:107
  16.1 2.9 %collective-permute-start.9 = (bf16[512,128]{1,0:T(8,128)(2,1)S(1)}, bf16[512,128]{1,0:T(8,128)(2,1)S(1)}, u32[]{:S(2)}, u32[]{:S(2)}) collective-permute-start(bf16[512,128]{1,0:T(8,128)(2,1)S(1)} %spread.3), channel_id=1, source_target_pairs={{0,24},{1,25},{2,26},{3,27},{4,28},{5,29},{6,30},{7,31},{8,16},{9,... | collective-permute-start | bytes 393224 | tf_op jit(solution)/shard_map/ppermute | solution.py:46
  19.3 0.4 %collective-permute-start.8 = (bf16[512,128]{1,0:T(8,128)(2,1)S(1)}, bf16[512,128]{1,0:T(8,128)(2,1)S(1)}, u32[]{:S(2)}, u32[]{:S(2)}) collective-permute-start(bf16[512,128]{1,0:T(8,128)(2,1)S(1)} %get-tuple-element.24), channel_id=1, source_target_pairs={{0,16},{1,17},{2,18},{3,19},{4,20},{5,21},{6,22},{7,23},{8,24},{9,... | collective-permute-start | bytes 393224 | tf_op jit(solution)/shard_map/ppermute | solution.py:46
  19.7 0.4 %collective-permute-start.7 = (bf16[512,128]{1,0:T(8,128)(2,1)S(1)}, bf16[512,128]{1,0:T(8,128)(2,1)S(1)}, u32[]{:S(2)}, u32[]{:S(2)}) collective-permute-start(bf16[512,128]{1,0:T(8,128)(2,1)S(1)} %get-tuple-element.22), channel_id=1, source_target_pairs={{0,8},{1,9},{2,10},{3,11},{4,12},{5,13},{6,14},{7,15},{8,0},{9,1},... | collective-permute-start | bytes 393224 | tf_op jit(solution)/shard_map/ppermute | solution.py:46
  20.8 1.8 %collective-permute-done.9.x.refs_0_ = bf16[512,128]{1,0:T(8,128)(2,1)S(1)} collective-permute-done((bf16[512,128]{1,0:T(8,128)(2,1)S(1)}, bf16[512,128]{1,0:T(8,128)(2,1)S(1)}, u32[]{:S(2)}, u32[]{:S(2)}) %collective-permute-start.9) | collective-permute-done | bytes 131104 | tf_op jit(solution)/shard_map/ppermute | solution.py:46
  22.9 1.5 %collective-permute-done.8.x.refs_0_ = bf16[512,128]{1,0:T(8,128)(2,1)S(1)} collective-permute-done((bf16[512,128]{1,0:T(8,128)(2,1)S(1)}, bf16[512,128]{1,0:T(8,128)(2,1)S(1)}, u32[]{:S(2)}, u32[]{:S(2)}) %collective-permute-start.8) | collective-permute-done | bytes 131104 | tf_op jit(solution)/shard_map/ppermute | solution.py:46
  25.1 0.9 %merge.5 = bf16[512,128]{1,0:T(8,128)(2,1)S(1)} custom-call(bf16[512,128]{1,0:T(8,128)(2,1)S(1)} %collective-permute-done.9.x.refs_0_, f32[384,512]{1,0:T(8,128)S(1)} %project.4.refs_0_.refs_1_, f32[384,512]{1,0:T(8,128)S(1)} %project.6.refs_0_.refs_2_, f32[384,512]{1,0:T(8,128)S(1)} %project.7.refs_3_, f32[384,512]{1,0:T(8,128)S(1)} %project.5.refs_0_.refs_4_, ...), custom_call_target="tpu_custom_call" | custom-call | flops 268435456 | bytes 65536 | tf_op jit(solution)/shard_map/merge/pallas_call | solution.py:269
  26.0 1.8 %collective-permute-start.11 = (bf16[512,128]{1,0:T(8,128)(2,1)S(1)}, bf16[512,128]{1,0:T(8,128)(2,1)S(1)}, u32[]{:S(2)}, u32[]{:S(2)}) collective-permute-start(bf16[512,128]{1,0:T(8,128)(2,1)S(1)} %merge.5), channel_id=1, source_target_pairs={{0,24},{1,25},{2,26},{3,27},{4,28},{5,29},{6,30},{7,31},{8,16},{9,... | collective-permute-start | bytes 393224 | tf_op jit(solution)/shard_map/ppermute | solution.py:46
  27.8 0.9 %merge.6 = bf16[512,128]{1,0:T(8,128)(2,1)S(1)} custom-call(bf16[512,128]{1,0:T(8,128)(2,1)S(1)} %collective-permute-done.8.x.refs_0_, f32[384,512]{1,0:T(8,128)S(1)} %project.4.refs_0_.refs_1_, f32[384,512]{1,0:T(8,128)S(1)} %project.6.refs_0_.refs_2_, f32[384,512]{1,0:T(8,128)S(1)} %project.7.refs_3_, f32[384,512]{1,0:T(8,128)S(1)} %project.5.refs_0_.refs_4_, ...), custom_call_target="tpu_custom_call" | custom-call | flops 268435456 | bytes 65536 | tf_op jit(solution)/shard_map/merge/pallas_call | solution.py:269
  28.7 1.0 %collective-permute-start.12 = (bf16[512,128]{1,0:T(8,128)(2,1)S(1)}, bf16[512,128]{1,0:T(8,128)(2,1)S(1)}, u32[]{:S(2)}, u32[]{:S(2)}) collective-permute-start(bf16[512,128]{1,0:T(8,128)(2,1)S(1)} %merge.6), channel_id=1, source_target_pairs={{0,16},{1,17},{2,18},{3,19},{4,20},{5,21},{6,22},{7,23},{8,24},{9,... | collective-permute-start | bytes 393224 | tf_op jit(solution)/shard_map/ppermute | solution.py:46
  29.7 0.9 %merge.4 = bf16[512,128]{1,0:T(8,128)(2,1)S(1)} custom-call(bf16[512,128]{1,0:T(8,128)(2,1)S(1)} %collective-permute-done.7.x.refs_0_, f32[384,512]{1,0:T(8,128)S(1)} %project.4.refs_0_.refs_1_, f32[384,512]{1,0:T(8,128)S(1)} %project.6.refs_0_.refs_2_, f32[384,512]{1,0:T(8,128)S(1)} %project.7.refs_3_, f32[384,512]{1,0:T(8,128)S(1)} %project.5.refs_0_.refs_4_, ...), custom_call_target="tpu_custom_call" | custom-call | flops 268435456 | bytes 65536 | tf_op jit(solution)/shard_map/merge/pallas_call | solution.py:269
  30.6 0.9 %collective-permute-start.10 = (bf16[512,128]{1,0:T(8,128)(2,1)S(1)}, bf16[512,128]{1,0:T(8,128)(2,1)S(1)}, u32[]{:S(2)}, u32[]{:S(2)}) collective-permute-start(bf16[512,128]{1,0:T(8,128)(2,1)S(1)} %merge.4), channel_id=1, source_target_pairs={{0,8},{1,9},{2,10},{3,11},{4,12},{5,13},{6,14},{7,15},{8,0},{9,1},... | collective-permute-start | bytes 393224 | tf_op jit(solution)/shard_map/ppermute | solution.py:46
  31.5 0.9 %merge.7.refs_2_ = bf16[512,128]{1,0:T(8,128)(2,1)S(1)} custom-call(bf16[512,128]{1,0:T(8,128)(2,1)S(1)} %get-tuple-element.23.x.refs_0_, f32[384,512]{1,0:T(8,128)S(1)} %project.4.refs_0_.refs_1_, f32[384,512]{1,0:T(8,128)S(1)} %project.6.refs_0_.refs_2_, f32[384,512]{1,0:T(8,128)S(1)} %project.7.refs_3_, f32[384,512]{1,0:T(8,128)S(1)} %project.5.refs_0_.refs_4_, ...), custom_call_target="tpu_custom_call" | custom-call | flops 268435456 | bytes 65536 | tf_op jit(solution)/shard_map/merge/pallas_call | solution.py:269
  32.4 1.3 %collective-permute-done.12.refs_1_ = bf16[512,128]{1,0:T(8,128)(2,1)S(1)} collective-permute-done((bf16[512,128]{1,0:T(8,128)(2,1)S(1)}, bf16[512,128]{1,0:T(8,128)(2,1)S(1)}, u32[]{:S(2)}, u32[]{:S(2)}) %collective-permute-start.12) | collective-permute-done | bytes 131104 | tf_op jit(solution)/shard_map/ppermute | solution.py:46
  33.8 0.8 %place.2.refs_1_ = bf16[2048,128]{1,0:T(8,128)(2,1)} custom-call(bf16[512,128]{1,0:T(8,128)(2,1)S(1)} %collective-permute-done.11.refs_0_, bf16[512,128]{1,0:T(8,128)(2,1)S(1)} %collective-permute-done.12.refs_1_, bf16[512,128]{1,0:T(8,128)(2,1)S(1)} %merge.7.refs_2_), custom_call_target="tpu_custom_call" | custom-call | tf_op jit(solution)/shard_map/place/pallas_call | solution.py:294
  34.5 1.1 %collective-permute-done.10.refs_0_ = bf16[512,128]{1,0:T(8,128)(2,1)S(1)} collective-permute-done((bf16[512,128]{1,0:T(8,128)(2,1)S(1)}, bf16[512,128]{1,0:T(8,128)(2,1)S(1)}, u32[]{:S(2)}, u32[]{:S(2)}) %collective-permute-start.10) | collective-permute-done | bytes 131104 | tf_op jit(solution)/shard_map/ppermute | solution.py:46
  35.6 0.7 %place.3 = bf16[2048,128]{1,0:T(8,128)(2,1)} custom-call(bf16[512,128]{1,0:T(8,128)(2,1)S(1)} %collective-permute-done.10.refs_0_, bf16[2048,128]{1,0:T(8,128)(2,1)} %place.2.refs_1_), custom_call_target="tpu_custom_call", output_to_operand_aliasing={{}: (1, {})} | custom-call | tf_op jit(solution)/shard_map/place/pallas_call | solution.py:294
  (36 shorter events, 2.7 us)
Async XLA Ops:
  0.0 6.8 %collective-permute-start.1 = (bf16[2048,128]{1,0:T(8,128)(2,1)}, bf16[2048,128]{1,0:T(8,128)(2,1)S(1)}, u32[]{:S(2)}, u32[]{:S(2)}) collective-permute-start(bf16[2048,128]{1,0:T(8,128)(2,1)} %refs_0_.1), channel_id=1, source_target_pairs={{0,1},{1,0},{2,3},{3,2},{4,5},{5,4},{6,7},{7,6},{8,9},{9,8},{10,11... | collective-permute-start | bytes 1572872 | tf_op jit(solution)/shard_map/ppermute | solution.py:33
  0.5 6.3 %collective-permute-start = (s32[1,4]{1,0:T(1,128)}, s32[1,4]{1,0:T(1,128)S(1)}, u32[]{:S(2)}, u32[]{:S(2)}) collective-permute-start(s32[1,4]{1,0:T(1,128)} %refs_1_.1), channel_id=1, source_target_pairs={{0,6},{1,7},{2,4},{3,5},{4,2},{5,3},{6,0},{7,1},{8,14},{9,15},{10,... | collective-permute-start | bytes 56 | tf_op jit(solution)/shard_map/ppermute | solution.py:33
  6.1 4.7 %collective-permute-start.4 = (s32[1,4]{1,0:T(1,128)S(1)}, s32[1,4]{1,0:T(1,128)S(1)}, u32[]{:S(2)}, u32[]{:S(2)}) collective-permute-start(s32[1,4]{1,0:T(1,128)S(1)} %get-tuple-element.16.refs_2_), channel_id=1, source_target_pairs={{0,2},{1,3},{2,0},{3,1},{4,6},{5,7},{6,4},{7,5},{8,10},{9,11},{10,... | collective-permute-start | bytes 56 | tf_op jit(solution)/shard_map/ppermute | solution.py:33
  6.2 4.6 %collective-permute-start.3 = (s32[1,4]{1,0:T(1,128)S(1)}, s32[1,4]{1,0:T(1,128)S(1)}, u32[]{:S(2)}, u32[]{:S(2)}) collective-permute-start(s32[1,4]{1,0:T(1,128)S(1)} %get-tuple-element.16.refs_2_), channel_id=1, source_target_pairs={{0,4},{1,5},{2,6},{3,7},{4,0},{5,1},{6,2},{7,3},{8,12},{9,13},{10,... | collective-permute-start | bytes 56 | tf_op jit(solution)/shard_map/ppermute | solution.py:33
  6.9 6.7 %collective-permute-start.2 = (bf16[128,128]{1,0:T(8,128)(2,1)S(1)}, bf16[128,128]{1,0:T(8,128)(2,1)S(1)}, u32[]{:S(2)}, u32[]{:S(2)}) collective-permute-start(bf16[128,128]{1,0:T(8,128)(2,1)S(1)} %serve.2), channel_id=1, source_target_pairs={{0,6},{1,7},{2,4},{3,5},{4,2},{5,3},{6,0},{7,1},{8,14},{9,15},{10,... | collective-permute-start | bytes 98312 | tf_op jit(solution)/shard_map/ppermute | solution.py:33
  11.0 4.9 %collective-permute-start.5 = (bf16[128,128]{1,0:T(8,128)(2,1)S(1)}, bf16[128,128]{1,0:T(8,128)(2,1)S(1)}, u32[]{:S(2)}, u32[]{:S(2)}) collective-permute-start(bf16[128,128]{1,0:T(8,128)(2,1)S(1)} %get-tuple-element.19), channel_id=1, source_target_pairs={{0,4},{1,5},{2,6},{3,7},{4,0},{5,1},{6,2},{7,3},{8,12},{9,13},{10,... | collective-permute-start | bytes 98312 | tf_op jit(solution)/shard_map/ppermute | solution.py:33
  11.4 4.4 %collective-permute-start.6 = (bf16[128,128]{1,0:T(8,128)(2,1)S(1)}, bf16[128,128]{1,0:T(8,128)(2,1)S(1)}, u32[]{:S(2)}, u32[]{:S(2)}) collective-permute-start(bf16[128,128]{1,0:T(8,128)(2,1)S(1)} %get-tuple-element.20), channel_id=1, source_target_pairs={{0,2},{1,3},{2,0},{3,1},{4,6},{5,7},{6,4},{7,5},{8,10},{9,11},{10,... | collective-permute-start | bytes 98312 | tf_op jit(solution)/shard_map/ppermute | solution.py:33
  13.6 6.5 %copy-start.4 = (bf16[128,128]{1,0:T(8,128)(2,1)S(1)}, bf16[128,128]{1,0:T(8,128)(2,1)}, u32[]{:S(2)}) copy-start(bf16[128,128]{1,0:T(8,128)(2,1)} %param.19) | copy-start | bytes 98308
  13.6 6.7 %copy-start.5 = (bf16[128,128]{1,0:T(8,128)(2,1)S(1)}, bf16[128,128]{1,0:T(8,128)(2,1)}, u32[]{:S(2)}) copy-start(bf16[128,128]{1,0:T(8,128)(2,1)} %param.20) | copy-start | bytes 98308
  13.7 6.8 %copy-start.6 = (bf16[128,128]{1,0:T(8,128)(2,1)S(1)}, bf16[128,128]{1,0:T(8,128)(2,1)}, u32[]{:S(2)}) copy-start(bf16[128,128]{1,0:T(8,128)(2,1)} %param.21) | copy-start | bytes 98308
  16.1 6.6 %collective-permute-start.9 = (bf16[512,128]{1,0:T(8,128)(2,1)S(1)}, bf16[512,128]{1,0:T(8,128)(2,1)S(1)}, u32[]{:S(2)}, u32[]{:S(2)}) collective-permute-start(bf16[512,128]{1,0:T(8,128)(2,1)S(1)} %spread.3), channel_id=1, source_target_pairs={{0,24},{1,25},{2,26},{3,27},{4,28},{5,29},{6,30},{7,31},{8,16},{9,... | collective-permute-start | bytes 393224 | tf_op jit(solution)/shard_map/ppermute | solution.py:46
  19.3 5.8 %copy-start = (bf16[128,512]{1,0:T(8,128)(2,1)S(1)}, bf16[128,512]{1,0:T(8,128)(2,1)}, u32[]{:S(2)}) copy-start(bf16[128,512]{1,0:T(8,128)(2,1)} %refs_7_.7) | copy-start | bytes 393220
  19.3 5.8 %copy-start.1 = (bf16[512,128]{1,0:T(8,128)(2,1)S(1)}, bf16[512,128]{1,0:T(8,128)(2,1)}, u32[]{:S(2)}) copy-start(bf16[512,128]{1,0:T(8,128)(2,1)} %refs_8_.7) | copy-start | bytes 393220
  19.3 5.8 %copy-start.2 = (bf16[128,128]{1,0:T(8,128)(2,1)S(1)}, bf16[128,128]{1,0:T(8,128)(2,1)}, u32[]{:S(2)}) copy-start(bf16[128,128]{1,0:T(8,128)(2,1)} %refs_5_.7) | copy-start | bytes 98308
  19.3 5.8 %copy-start.3 = (f32[128]{0:T(128)S(1)}, f32[128]{0:T(128)}, u32[]{:S(2)}) copy-start(f32[128]{0:T(128)} %param.23) | copy-start | bytes 1540
  19.3 5.1 %collective-permute-start.8 = (bf16[512,128]{1,0:T(8,128)(2,1)S(1)}, bf16[512,128]{1,0:T(8,128)(2,1)S(1)}, u32[]{:S(2)}, u32[]{:S(2)}) collective-permute-start(bf16[512,128]{1,0:T(8,128)(2,1)S(1)} %get-tuple-element.24), channel_id=1, source_target_pairs={{0,16},{1,17},{2,18},{3,19},{4,20},{5,21},{6,22},{7,23},{8,24},{9,... | collective-permute-start | bytes 393224 | tf_op jit(solution)/shard_map/ppermute | solution.py:46
  19.7 5.1 %collective-permute-start.7 = (bf16[512,128]{1,0:T(8,128)(2,1)S(1)}, bf16[512,128]{1,0:T(8,128)(2,1)S(1)}, u32[]{:S(2)}, u32[]{:S(2)}) collective-permute-start(bf16[512,128]{1,0:T(8,128)(2,1)S(1)} %get-tuple-element.22), channel_id=1, source_target_pairs={{0,8},{1,9},{2,10},{3,11},{4,12},{5,13},{6,14},{7,15},{8,0},{9,1},... | collective-permute-start | bytes 393224 | tf_op jit(solution)/shard_map/ppermute | solution.py:46
  26.0 6.4 %collective-permute-start.11 = (bf16[512,128]{1,0:T(8,128)(2,1)S(1)}, bf16[512,128]{1,0:T(8,128)(2,1)S(1)}, u32[]{:S(2)}, u32[]{:S(2)}) collective-permute-start(bf16[512,128]{1,0:T(8,128)(2,1)S(1)} %merge.5), channel_id=1, source_target_pairs={{0,24},{1,25},{2,26},{3,27},{4,28},{5,29},{6,30},{7,31},{8,16},{9,... | collective-permute-start | bytes 393224 | tf_op jit(solution)/shard_map/ppermute | solution.py:46
  28.7 5.1 %collective-permute-start.12 = (bf16[512,128]{1,0:T(8,128)(2,1)S(1)}, bf16[512,128]{1,0:T(8,128)(2,1)S(1)}, u32[]{:S(2)}, u32[]{:S(2)}) collective-permute-start(bf16[512,128]{1,0:T(8,128)(2,1)S(1)} %merge.6), channel_id=1, source_target_pairs={{0,16},{1,17},{2,18},{3,19},{4,20},{5,21},{6,22},{7,23},{8,24},{9,... | collective-permute-start | bytes 393224 | tf_op jit(solution)/shard_map/ppermute | solution.py:46
  30.6 5.0 %collective-permute-start.10 = (bf16[512,128]{1,0:T(8,128)(2,1)S(1)}, bf16[512,128]{1,0:T(8,128)(2,1)S(1)}, u32[]{:S(2)}, u32[]{:S(2)}) collective-permute-start(bf16[512,128]{1,0:T(8,128)(2,1)S(1)} %merge.4), channel_id=1, source_target_pairs={{0,8},{1,9},{2,10},{3,11},{4,12},{5,13},{6,14},{7,15},{8,0},{9,1},... | collective-permute-start | bytes 393224 | tf_op jit(solution)/shard_map/ppermute | solution.py:46

commit v7 on v6

--- a/solution.py
+++ b/solution.py
@@ -35,7 +35,7 @@
 
 def beh_masks(parts):
     first, *rest = range(parts - 1, 0, -1)
-    return [(0, 0)] + list(zip(rest, rest)) + [(first, first)]
+    return [(0, 0)] + list(zip(rest[::-1], rest)) + [(first, first)]
 
 
 def exchange_beh(value, masks):

time: 36.3 us -> 36.2 us (level)
  transfers between devices with their start and end apart: 13 -> 13, of which waited for: 7 -> 6; matrix products, arithmetic and copies ran while one was open for 1% -> 1% of each run, Pallas kernels for 22% -> 23%
where the time goes in v7:
time: 36.2 us
  starting transfers between devices  18.8 us (52%)
  Pallas kernels  10.2 us (28%)
  waiting for transfers between devices  5.79 us (16%)
  between operations  0.91 us (3%)
  local copies, waits for them, and re-layouts  0.38 us (1%)
    ppermute x7, starting transfers between devices, exchange(): return lax.ppermute(value, axis, pairs)  11.5 us
    ppermute x6, starting transfers between devices, exchange_beh(): return lax.ppermute(value, ('beh', 'node'), pairs)  7.3 us
    ppermute x6, waiting for transfers between devices, exchange_beh(): return lax.ppermute(value, ('beh', 'node'), pairs)  5.77 us
    pallas_call x4, Pallas kernels, merge(): pl.pallas_call(functools.partial(merge_kernel, len(projected), which, til...  3.49 us
    pallas_call x1, Pallas kernels, begin_spread(): pl.pallas_call(functools.partial(cells_kernel, chunk, pairs, columns), in...  2.35 us
    pallas_call x2, Pallas kernels, place_parts(): pl.pallas_call(functools.partial(place_kernel, which, parts), in_specs=[V...  1.43 us
    pallas_call x1, Pallas kernels, load(): pl.pallas_call(load_kernel, in_specs=[HBM] * len(sources), out_specs=[VME...  1.06 us
    pallas_call x4, Pallas kernels, project(): pl.pallas_call(project_kernel, in_specs=[VMEM] * (2 + len(before)), out_s...  1.03 us
  transfers between devices with their start and end apart: 13, of which 6 were waited for; matrix products, arithmetic and copies ran while one was open for 1% of the time, Pallas kernels for 23%

profile of v7, /device:TPU:0, one launch (start us, length us, event | category | flops | bytes accessed | tf_op | source)
XLA Modules:
  0.0 36.2 jit_solution(15427042222335827784)
XLA Ops:
  0.0 0.5 %collective-permute-start.1 = (bf16[2048,128]{1,0:T(8,128)(2,1)}, bf16[2048,128]{1,0:T(8,128)(2,1)S(1)}, u32[]{:S(2)}, u32[]{:S(2)}) collective-permute-start(bf16[2048,128]{1,0:T(8,128)(2,1)} %refs_0_.1), channel_id=1, source_target_pairs={{0,1},{1,0},{2,3},{3,2},{4,5},{5,4},{6,7},{7,6},{8,9},{9,8},{10,11... | collective-permute-start | bytes 1572872 | tf_op jit(solution)/shard_map/ppermute | solution.py:33
  0.5 4.6 %collective-permute-start = (s32[1,4]{1,0:T(1,128)}, s32[1,4]{1,0:T(1,128)S(1)}, u32[]{:S(2)}, u32[]{:S(2)}) collective-permute-start(s32[1,4]{1,0:T(1,128)} %refs_1_.1), channel_id=1, source_target_pairs={{0,6},{1,7},{2,4},{3,5},{4,2},{5,3},{6,0},{7,1},{8,14},{9,15},{10,... | collective-permute-start | bytes 56 | tf_op jit(solution)/shard_map/ppermute | solution.py:33
  5.1 1.1 %load.1 = (bf16[2048,128]{1,0:T(8,128)(2,1)S(1)}, s32[1,4]{1,0:T(1,128)S(1)}) custom-call(bf16[2048,128]{1,0:T(8,128)(2,1)} %refs_0_.1, s32[1,4]{1,0:T(1,128)} %refs_1_.1), custom_call_target="tpu_custom_call" | custom-call | bytes 524296 | tf_op jit(solution)/shard_map/load/pallas_call | solution.py:139
  6.2 0.6 %collective-permute-start.3 = (s32[1,4]{1,0:T(1,128)S(1)}, s32[1,4]{1,0:T(1,128)S(1)}, u32[]{:S(2)}, u32[]{:S(2)}) collective-permute-start(s32[1,4]{1,0:T(1,128)S(1)} %get-tuple-element.16.refs_2_), channel_id=1, source_target_pairs={{0,4},{1,5},{2,6},{3,7},{4,0},{5,1},{6,2},{7,3},{8,12},{9,13},{10,... | collective-permute-start | bytes 56 | tf_op jit(solution)/shard_map/ppermute | solution.py:33
  6.9 3.9 %collective-permute-start.2 = (bf16[128,128]{1,0:T(8,128)(2,1)S(1)}, bf16[128,128]{1,0:T(8,128)(2,1)S(1)}, u32[]{:S(2)}, u32[]{:S(2)}) collective-permute-start(bf16[128,128]{1,0:T(8,128)(2,1)S(1)} %serve.2), channel_id=1, source_target_pairs={{0,6},{1,7},{2,4},{3,5},{4,2},{5,3},{6,0},{7,1},{8,14},{9,15},{10,... | collective-permute-start | bytes 98312 | tf_op jit(solution)/shard_map/ppermute | solution.py:33
  11.0 0.5 %collective-permute-start.5 = (bf16[128,128]{1,0:T(8,128)(2,1)S(1)}, bf16[128,128]{1,0:T(8,128)(2,1)S(1)}, u32[]{:S(2)}, u32[]{:S(2)}) collective-permute-start(bf16[128,128]{1,0:T(8,128)(2,1)S(1)} %get-tuple-element.19), channel_id=1, source_target_pairs={{0,4},{1,5},{2,6},{3,7},{4,0},{5,1},{6,2},{7,3},{8,12},{9,13},{10,... | collective-permute-start | bytes 98312 | tf_op jit(solution)/shard_map/ppermute | solution.py:33
  11.4 1.5 %collective-permute-start.6 = (bf16[128,128]{1,0:T(8,128)(2,1)S(1)}, bf16[128,128]{1,0:T(8,128)(2,1)S(1)}, u32[]{:S(2)}, u32[]{:S(2)}) collective-permute-start(bf16[128,128]{1,0:T(8,128)(2,1)S(1)} %get-tuple-element.20), channel_id=1, source_target_pairs={{0,2},{1,3},{2,0},{3,1},{4,6},{5,7},{6,4},{7,5},{8,10},{9,11},{10,... | collective-permute-start | bytes 98312 | tf_op jit(solution)/shard_map/ppermute | solution.py:33
  13.7 2.3 %cells.1 = (bf16[32,128,128]{2,1,0:T(8,128)(2,1)S(1)}, f32[2048,128]{1,0:T(8,128)S(1)}) custom-call(s32[1,112]{1,0:T(1,128)} %rows.1, s32[1,112]{1,0:T(1,128)} %cols.1, s32[1,1]{1,0:T(1,128)S(6)} %copy.19.count, bf16[112,128,128]{2,1,0:T(8,128)(2,1)} %bitcast.9, bf16[128,128]{1,0:T(8,128)(2,1)S(1)} %collective-permute-done.2.refs_0_, ...), custom_call_target="tpu_custom_call" | custom-call | bytes 3670016 | tf_op jit(solution)/shard_map/cells/pallas_call | solution.py:107
  16.3 2.8 %collective-permute-start.9 = (bf16[512,128]{1,0:T(8,128)(2,1)S(1)}, bf16[512,128]{1,0:T(8,128)(2,1)S(1)}, u32[]{:S(2)}, u32[]{:S(2)}) collective-permute-start(bf16[512,128]{1,0:T(8,128)(2,1)S(1)} %spread.3), channel_id=1, source_target_pairs={{0,24},{1,25},{2,26},{3,27},{4,28},{5,29},{6,30},{7,31},{8,16},{9,... | collective-permute-start | bytes 393224 | tf_op jit(solution)/shard_map/ppermute | solution.py:46
  19.5 0.4 %collective-permute-start.8 = (bf16[512,128]{1,0:T(8,128)(2,1)S(1)}, bf16[512,128]{1,0:T(8,128)(2,1)S(1)}, u32[]{:S(2)}, u32[]{:S(2)}) collective-permute-start(bf16[512,128]{1,0:T(8,128)(2,1)S(1)} %get-tuple-element.24), channel_id=1, source_target_pairs={{0,8},{1,17},{2,10},{3,19},{4,12},{5,21},{6,14},{7,23},{8,0},{9,25... | collective-permute-start | bytes 393224 | tf_op jit(solution)/shard_map/ppermute | solution.py:46
  20.9 2.2 %collective-permute-done.9.x.refs_0_ = bf16[512,128]{1,0:T(8,128)(2,1)S(1)} collective-permute-done((bf16[512,128]{1,0:T(8,128)(2,1)S(1)}, bf16[512,128]{1,0:T(8,128)(2,1)S(1)}, u32[]{:S(2)}, u32[]{:S(2)}) %collective-permute-start.9) | collective-permute-done | bytes 131104 | tf_op jit(solution)/shard_map/ppermute | solution.py:46
  23.5 1.1 %collective-permute-done.8.x.refs_0_ = bf16[512,128]{1,0:T(8,128)(2,1)S(1)} collective-permute-done((bf16[512,128]{1,0:T(8,128)(2,1)S(1)}, bf16[512,128]{1,0:T(8,128)(2,1)S(1)}, u32[]{:S(2)}, u32[]{:S(2)}) %collective-permute-start.8) | collective-permute-done | bytes 131104 | tf_op jit(solution)/shard_map/ppermute | solution.py:46
  25.2 0.9 %merge.5 = bf16[512,128]{1,0:T(8,128)(2,1)S(1)} custom-call(bf16[512,128]{1,0:T(8,128)(2,1)S(1)} %collective-permute-done.9.x.refs_0_, f32[384,512]{1,0:T(8,128)S(1)} %project.4.refs_0_.refs_1_, f32[384,512]{1,0:T(8,128)S(1)} %project.6.refs_0_.refs_2_, f32[384,512]{1,0:T(8,128)S(1)} %project.7.refs_3_, f32[384,512]{1,0:T(8,128)S(1)} %project.5.refs_0_.refs_4_, ...), custom_call_target="tpu_custom_call" | custom-call | flops 268435456 | bytes 65536 | tf_op jit(solution)/shard_map/merge/pallas_call | solution.py:269
  26.1 1.6 %collective-permute-start.11 = (bf16[512,128]{1,0:T(8,128)(2,1)S(1)}, bf16[512,128]{1,0:T(8,128)(2,1)S(1)}, u32[]{:S(2)}, u32[]{:S(2)}) collective-permute-start(bf16[512,128]{1,0:T(8,128)(2,1)S(1)} %merge.5), channel_id=1, source_target_pairs={{0,24},{1,25},{2,26},{3,27},{4,28},{5,29},{6,30},{7,31},{8,16},{9,... | collective-permute-start | bytes 393224 | tf_op jit(solution)/shard_map/ppermute | solution.py:46
  27.7 0.9 %merge.6 = bf16[512,128]{1,0:T(8,128)(2,1)S(1)} custom-call(bf16[512,128]{1,0:T(8,128)(2,1)S(1)} %collective-permute-done.8.x.refs_0_, f32[384,512]{1,0:T(8,128)S(1)} %project.4.refs_0_.refs_1_, f32[384,512]{1,0:T(8,128)S(1)} %project.6.refs_0_.refs_2_, f32[384,512]{1,0:T(8,128)S(1)} %project.7.refs_3_, f32[384,512]{1,0:T(8,128)S(1)} %project.5.refs_0_.refs_4_, ...), custom_call_target="tpu_custom_call" | custom-call | flops 268435456 | bytes 65536 | tf_op jit(solution)/shard_map/merge/pallas_call | solution.py:269
  28.6 1.0 %collective-permute-start.12 = (bf16[512,128]{1,0:T(8,128)(2,1)S(1)}, bf16[512,128]{1,0:T(8,128)(2,1)S(1)}, u32[]{:S(2)}, u32[]{:S(2)}) collective-permute-start(bf16[512,128]{1,0:T(8,128)(2,1)S(1)} %merge.6), channel_id=1, source_target_pairs={{0,8},{1,17},{2,10},{3,19},{4,12},{5,21},{6,14},{7,23},{8,0},{9,25... | collective-permute-start | bytes 393224 | tf_op jit(solution)/shard_map/ppermute | solution.py:46
  29.6 0.9 %merge.4 = bf16[512,128]{1,0:T(8,128)(2,1)S(1)} custom-call(bf16[512,128]{1,0:T(8,128)(2,1)S(1)} %collective-permute-done.7.x.refs_0_, f32[384,512]{1,0:T(8,128)S(1)} %project.4.refs_0_.refs_1_, f32[384,512]{1,0:T(8,128)S(1)} %project.6.refs_0_.refs_2_, f32[384,512]{1,0:T(8,128)S(1)} %project.7.refs_3_, f32[384,512]{1,0:T(8,128)S(1)} %project.5.refs_0_.refs_4_, ...), custom_call_target="tpu_custom_call" | custom-call | flops 268435456 | bytes 65536 | tf_op jit(solution)/shard_map/merge/pallas_call | solution.py:269
  30.5 1.0 %collective-permute-start.10 = (bf16[512,128]{1,0:T(8,128)(2,1)S(1)}, bf16[512,128]{1,0:T(8,128)(2,1)S(1)}, u32[]{:S(2)}, u32[]{:S(2)}) collective-permute-start(bf16[512,128]{1,0:T(8,128)(2,1)S(1)} %merge.4), channel_id=1, source_target_pairs={{0,16},{1,9},{2,18},{3,11},{4,20},{5,13},{6,22},{7,15},{8,24},{9,1... | collective-permute-start | bytes 393224 | tf_op jit(solution)/shard_map/ppermute | solution.py:46
  31.5 0.9 %merge.7.refs_2_ = bf16[512,128]{1,0:T(8,128)(2,1)S(1)} custom-call(bf16[512,128]{1,0:T(8,128)(2,1)S(1)} %get-tuple-element.23.x.refs_0_, f32[384,512]{1,0:T(8,128)S(1)} %project.4.refs_0_.refs_1_, f32[384,512]{1,0:T(8,128)S(1)} %project.6.refs_0_.refs_2_, f32[384,512]{1,0:T(8,128)S(1)} %project.7.refs_3_, f32[384,512]{1,0:T(8,128)S(1)} %project.5.refs_0_.refs_4_, ...), custom_call_target="tpu_custom_call" | custom-call | flops 268435456 | bytes 65536 | tf_op jit(solution)/shard_map/merge/pallas_call | solution.py:269
  32.4 0.7 %collective-permute-done.11.refs_0_ = bf16[512,128]{1,0:T(8,128)(2,1)S(1)} collective-permute-done((bf16[512,128]{1,0:T(8,128)(2,1)S(1)}, bf16[512,128]{1,0:T(8,128)(2,1)S(1)}, u32[]{:S(2)}, u32[]{:S(2)}) %collective-permute-start.11) | collective-permute-done | bytes 131104 | tf_op jit(solution)/shard_map/ppermute | solution.py:46
  33.1 1.3 %collective-permute-done.12.refs_1_ = bf16[512,128]{1,0:T(8,128)(2,1)S(1)} collective-permute-done((bf16[512,128]{1,0:T(8,128)(2,1)S(1)}, bf16[512,128]{1,0:T(8,128)(2,1)S(1)}, u32[]{:S(2)}, u32[]{:S(2)}) %collective-permute-start.12) | collective-permute-done | bytes 131104 | tf_op jit(solution)/shard_map/ppermute | solution.py:46
  34.3 0.8 %place.2.refs_1_ = bf16[2048,128]{1,0:T(8,128)(2,1)} custom-call(bf16[512,128]{1,0:T(8,128)(2,1)S(1)} %collective-permute-done.11.refs_0_, bf16[512,128]{1,0:T(8,128)(2,1)S(1)} %collective-permute-done.12.refs_1_, bf16[512,128]{1,0:T(8,128)(2,1)S(1)} %merge.7.refs_2_), custom_call_target="tpu_custom_call" | custom-call | tf_op jit(solution)/shard_map/place/pallas_call | solution.py:294
  35.1 0.4 %collective-permute-done.10.refs_0_ = bf16[512,128]{1,0:T(8,128)(2,1)S(1)} collective-permute-done((bf16[512,128]{1,0:T(8,128)(2,1)S(1)}, bf16[512,128]{1,0:T(8,128)(2,1)S(1)}, u32[]{:S(2)}, u32[]{:S(2)}) %collective-permute-start.10) | collective-permute-done | bytes 131104 | tf_op jit(solution)/shard_map/ppermute | solution.py:46
  35.5 0.7 %place.3 = bf16[2048,128]{1,0:T(8,128)(2,1)} custom-call(bf16[512,128]{1,0:T(8,128)(2,1)S(1)} %collective-permute-done.10.refs_0_, bf16[2048,128]{1,0:T(8,128)(2,1)} %place.2.refs_1_), custom_call_target="tpu_custom_call", output_to_operand_aliasing={{}: (1, {})} | custom-call | tf_op jit(solution)/shard_map/place/pallas_call | solution.py:294
  (36 shorter events, 2.9 us)
Async XLA Ops:
  0.0 6.8 %collective-permute-start.1 = (bf16[2048,128]{1,0:T(8,128)(2,1)}, bf16[2048,128]{1,0:T(8,128)(2,1)S(1)}, u32[]{:S(2)}, u32[]{:S(2)}) collective-permute-start(bf16[2048,128]{1,0:T(8,128)(2,1)} %refs_0_.1), channel_id=1, source_target_pairs={{0,1},{1,0},{2,3},{3,2},{4,5},{5,4},{6,7},{7,6},{8,9},{9,8},{10,11... | collective-permute-start | bytes 1572872 | tf_op jit(solution)/shard_map/ppermute | solution.py:33
  0.5 6.3 %collective-permute-start = (s32[1,4]{1,0:T(1,128)}, s32[1,4]{1,0:T(1,128)S(1)}, u32[]{:S(2)}, u32[]{:S(2)}) collective-permute-start(s32[1,4]{1,0:T(1,128)} %refs_1_.1), channel_id=1, source_target_pairs={{0,6},{1,7},{2,4},{3,5},{4,2},{5,3},{6,0},{7,1},{8,14},{9,15},{10,... | collective-permute-start | bytes 56 | tf_op jit(solution)/shard_map/ppermute | solution.py:33
  6.1 4.7 %collective-permute-start.4 = (s32[1,4]{1,0:T(1,128)S(1)}, s32[1,4]{1,0:T(1,128)S(1)}, u32[]{:S(2)}, u32[]{:S(2)}) collective-permute-start(s32[1,4]{1,0:T(1,128)S(1)} %get-tuple-element.16.refs_2_), channel_id=1, source_target_pairs={{0,2},{1,3},{2,0},{3,1},{4,6},{5,7},{6,4},{7,5},{8,10},{9,11},{10,... | collective-permute-start | bytes 56 | tf_op jit(solution)/shard_map/ppermute | solution.py:33
  6.2 4.6 %collective-permute-start.3 = (s32[1,4]{1,0:T(1,128)S(1)}, s32[1,4]{1,0:T(1,128)S(1)}, u32[]{:S(2)}, u32[]{:S(2)}) collective-permute-start(s32[1,4]{1,0:T(1,128)S(1)} %get-tuple-element.16.refs_2_), channel_id=1, source_target_pairs={{0,4},{1,5},{2,6},{3,7},{4,0},{5,1},{6,2},{7,3},{8,12},{9,13},{10,... | collective-permute-start | bytes 56 | tf_op jit(solution)/shard_map/ppermute | solution.py:33
  6.9 6.7 %collective-permute-start.2 = (bf16[128,128]{1,0:T(8,128)(2,1)S(1)}, bf16[128,128]{1,0:T(8,128)(2,1)S(1)}, u32[]{:S(2)}, u32[]{:S(2)}) collective-permute-start(bf16[128,128]{1,0:T(8,128)(2,1)S(1)} %serve.2), channel_id=1, source_target_pairs={{0,6},{1,7},{2,4},{3,5},{4,2},{5,3},{6,0},{7,1},{8,14},{9,15},{10,... | collective-permute-start | bytes 98312 | tf_op jit(solution)/shard_map/ppermute | solution.py:33
  11.0 5.0 %collective-permute-start.5 = (bf16[128,128]{1,0:T(8,128)(2,1)S(1)}, bf16[128,128]{1,0:T(8,128)(2,1)S(1)}, u32[]{:S(2)}, u32[]{:S(2)}) collective-permute-start(bf16[128,128]{1,0:T(8,128)(2,1)S(1)} %get-tuple-element.19), channel_id=1, source_target_pairs={{0,4},{1,5},{2,6},{3,7},{4,0},{5,1},{6,2},{7,3},{8,12},{9,13},{10,... | collective-permute-start | bytes 98312 | tf_op jit(solution)/shard_map/ppermute | solution.py:33
  11.4 4.6 %collective-permute-start.6 = (bf16[128,128]{1,0:T(8,128)(2,1)S(1)}, bf16[128,128]{1,0:T(8,128)(2,1)S(1)}, u32[]{:S(2)}, u32[]{:S(2)}) collective-permute-start(bf16[128,128]{1,0:T(8,128)(2,1)S(1)} %get-tuple-element.20), channel_id=1, source_target_pairs={{0,2},{1,3},{2,0},{3,1},{4,6},{5,7},{6,4},{7,5},{8,10},{9,11},{10,... | collective-permute-start | bytes 98312 | tf_op jit(solution)/shard_map/ppermute | solution.py:33
  13.6 6.7 %copy-start.4 = (bf16[128,128]{1,0:T(8,128)(2,1)S(1)}, bf16[128,128]{1,0:T(8,128)(2,1)}, u32[]{:S(2)}) copy-start(bf16[128,128]{1,0:T(8,128)(2,1)} %param.19) | copy-start | bytes 98308
  13.6 6.8 %copy-start.5 = (bf16[128,128]{1,0:T(8,128)(2,1)S(1)}, bf16[128,128]{1,0:T(8,128)(2,1)}, u32[]{:S(2)}) copy-start(bf16[128,128]{1,0:T(8,128)(2,1)} %param.20) | copy-start | bytes 98308
  13.7 6.9 %copy-start.6 = (bf16[128,128]{1,0:T(8,128)(2,1)S(1)}, bf16[128,128]{1,0:T(8,128)(2,1)}, u32[]{:S(2)}) copy-start(bf16[128,128]{1,0:T(8,128)(2,1)} %param.21) | copy-start | bytes 98308
  16.3 6.9 %collective-permute-start.9 = (bf16[512,128]{1,0:T(8,128)(2,1)S(1)}, bf16[512,128]{1,0:T(8,128)(2,1)S(1)}, u32[]{:S(2)}, u32[]{:S(2)}) collective-permute-start(bf16[512,128]{1,0:T(8,128)(2,1)S(1)} %spread.3), channel_id=1, source_target_pairs={{0,24},{1,25},{2,26},{3,27},{4,28},{5,29},{6,30},{7,31},{8,16},{9,... | collective-permute-start | bytes 393224 | tf_op jit(solution)/shard_map/ppermute | solution.py:46
  19.4 5.7 %copy-start = (bf16[128,512]{1,0:T(8,128)(2,1)S(1)}, bf16[128,512]{1,0:T(8,128)(2,1)}, u32[]{:S(2)}) copy-start(bf16[128,512]{1,0:T(8,128)(2,1)} %refs_7_.7) | copy-start | bytes 393220
  19.5 5.7 %copy-start.1 = (bf16[512,128]{1,0:T(8,128)(2,1)S(1)}, bf16[512,128]{1,0:T(8,128)(2,1)}, u32[]{:S(2)}) copy-start(bf16[512,128]{1,0:T(8,128)(2,1)} %refs_8_.7) | copy-start | bytes 393220
  19.5 5.7 %copy-start.2 = (bf16[128,128]{1,0:T(8,128)(2,1)S(1)}, bf16[128,128]{1,0:T(8,128)(2,1)}, u32[]{:S(2)}) copy-start(bf16[128,128]{1,0:T(8,128)(2,1)} %refs_5_.7) | copy-start | bytes 98308
  19.5 5.7 %copy-start.3 = (f32[128]{0:T(128)S(1)}, f32[128]{0:T(128)}, u32[]{:S(2)}) copy-start(f32[128]{0:T(128)} %param.23) | copy-start | bytes 1540
  19.5 5.0 %collective-permute-start.8 = (bf16[512,128]{1,0:T(8,128)(2,1)S(1)}, bf16[512,128]{1,0:T(8,128)(2,1)S(1)}, u32[]{:S(2)}, u32[]{:S(2)}) collective-permute-start(bf16[512,128]{1,0:T(8,128)(2,1)S(1)} %get-tuple-element.24), channel_id=1, source_target_pairs={{0,8},{1,17},{2,10},{3,19},{4,12},{5,21},{6,14},{7,23},{8,0},{9,25... | collective-permute-start | bytes 393224 | tf_op jit(solution)/shard_map/ppermute | solution.py:46
  19.9 5.0 %collective-permute-start.7 = (bf16[512,128]{1,0:T(8,128)(2,1)S(1)}, bf16[512,128]{1,0:T(8,128)(2,1)S(1)}, u32[]{:S(2)}, u32[]{:S(2)}) collective-permute-start(bf16[512,128]{1,0:T(8,128)(2,1)S(1)} %get-tuple-element.22), channel_id=1, source_target_pairs={{0,16},{1,9},{2,18},{3,11},{4,20},{5,13},{6,22},{7,15},{8,24},{9,1... | collective-permute-start | bytes 393224 | tf_op jit(solution)/shard_map/ppermute | solution.py:46
  26.1 7.0 %collective-permute-start.11 = (bf16[512,128]{1,0:T(8,128)(2,1)S(1)}, bf16[512,128]{1,0:T(8,128)(2,1)S(1)}, u32[]{:S(2)}, u32[]{:S(2)}) collective-permute-start(bf16[512,128]{1,0:T(8,128)(2,1)S(1)} %merge.5), channel_id=1, source_target_pairs={{0,24},{1,25},{2,26},{3,27},{4,28},{5,29},{6,30},{7,31},{8,16},{9,... | collective-permute-start | bytes 393224 | tf_op jit(solution)/shard_map/ppermute | solution.py:46
  28.6 5.8 %collective-permute-start.12 = (bf16[512,128]{1,0:T(8,128)(2,1)S(1)}, bf16[512,128]{1,0:T(8,128)(2,1)S(1)}, u32[]{:S(2)}, u32[]{:S(2)}) collective-permute-start(bf16[512,128]{1,0:T(8,128)(2,1)S(1)} %merge.6), channel_id=1, source_target_pairs={{0,8},{1,17},{2,10},{3,19},{4,12},{5,21},{6,14},{7,23},{8,0},{9,25... | collective-permute-start | bytes 393224 | tf_op jit(solution)/shard_map/ppermute | solution.py:46
  30.5 5.0 %collective-permute-start.10 = (bf16[512,128]{1,0:T(8,128)(2,1)S(1)}, bf16[512,128]{1,0:T(8,128)(2,1)S(1)}, u32[]{:S(2)}, u32[]{:S(2)}) collective-permute-start(bf16[512,128]{1,0:T(8,128)(2,1)S(1)} %merge.4), channel_id=1, source_target_pairs={{0,16},{1,9},{2,18},{3,11},{4,20},{5,13},{6,22},{7,15},{8,24},{9,1... | collective-permute-start | bytes 393224 | tf_op jit(solution)/shard_map/ppermute | solution.py:46
